TPU v7x, 32 devices: a whole 2x2x4 slice. The times are simulated.
32 devices in a mesh: tok: 4 (over y, core), head: 8 (over z, x).
Axes of the slice: x: 2, y: 2, z: 4, core: 2. Of those that a mesh axis runs over, the one named last changes fastest.
Arguments:
- hidden_states: bfloat16 [2560, 6144], P('tok', 'head'), may hold values from -6 to 6
- norm_gain: float32 [6144], replicated, may hold values from 0.5 to 1.5
- norm_bias: float32 [6144], replicated, may hold values from -2 to 2
- qkv_weight: bfloat16 [6144, 18432], P('tok', 'head'), may hold values from -0.125 to 0.125
- qkv_bias: bfloat16 [18432], P('head'), may hold values from -2 to 2
- dense_weight: bfloat16 [6144, 6144], P('head'), may hold values from -0.21875 to 0.21875
- dense_bias: bfloat16 [6144], P('head'), may hold values from -2 to 2
- prefix_keys: bfloat16 [8, 2048, 6144], P('tok', None, 'head'), may hold values from -70 to 70
- prefix_values: bfloat16 [8, 2048, 6144], P('tok', None, 'head'), may hold values from -10 to 10
- suffix_len: int32 [4, 8], P('tok'), may hold values from 1 to 240, as said below
- request_order: int32 [4, 8], P('tok'), may hold values from 0 to 7, each once within a row
- group_slot: int32 [8], replicated, may hold values from 0 to 7, each once
Outputs:
- layer_out: bfloat16 [2560, 6144], P('tok', 'head')
Inputs may be any that keep to these rules, and one draw needn't show every extreme that they name: `suffix_len`: each row sums to 640; one group, the same in every row, has exactly 240 in every row. `request_order`: each row names every group once. `group_slot`: each slot holds one group.
All inputs are finite; a program needn't handle non-finite values.
Results may differ from a plain program's by a relative error of at most 0.007.
The roundings to bfloat16 on the way count: a program that leaves them out, or rounds other values in their place, can miss the bound.
Values may be sent and summed in bfloat16 or wider, within the bound.
No kernel may reach another device: no remote copies, remote signals or barrier semaphores. Data moves between devices by JAX's collectives and lax.ppermute only.
A program may use at most 192 MiB of HBM per device.

v0:
```python
import functools
import math

import jax
import jax.numpy as jnp
from jax import lax
from jax.experimental import pallas as pl
from jax.experimental.pallas import tpu as pltpu
from jax.sharding import PartitionSpec as P

HS = 96
GROUP_HEADS = 4
GW = GROUP_HEADS * HS
PACK = 128
F32 = jnp.float32
BF16 = jnp.bfloat16
VMEM_LIMIT = 56 * 1024 * 1024
SCALE = 1.0 / math.sqrt(HS)
LOG2E = math.log2(math.e)
LIGHT = pl.CostEstimate(flops=1000, bytes_accessed=1000, transcendentals=0)


def windows():
    found = []
    for k in range(GROUP_HEADS):
        first = k * HS // 128 * 128
        last = -(-(k * HS + HS) // 128) * 128
        found.append((first, last - first))
    return found


def head_mask(k, first, shape):
    lane = lax.broadcasted_iota(jnp.int32, shape, 1) + first
    return (lane >= k * HS) & (lane < (k + 1) * HS)


def params():
    return pltpu.CompilerParams(vmem_limit_bytes=VMEM_LIMIT)


def norm_kernel(count, chunks, places, *refs):
    blocks = refs[:count]
    gain, shift, out, held, ready, sems, out_sems = refs[count:]
    share = blocks[0].shape[1]
    height = held.shape[0] // chunks
    tile = 32

    def copy(j, chunk):
        lanes = pl.ds(pl.multiple_of(places[j] * share, 128), share)
        rows = pl.ds(chunk * height, height)
        return pltpu.make_async_copy(
            blocks[j].at[rows, :], held.at[rows, lanes], sems.at[j, chunk]
        )

    def out_copy(chunk):
        rows = pl.ds(chunk * height, height)
        return pltpu.make_async_copy(ready.at[rows, :], out.at[rows, :], out_sems.at[chunk])

    for chunk in range(chunks):
        for j in range(count):

            @pl.when(places[j] >= 0)
            def _(j=j, chunk=chunk):
                copy(j, chunk).start()

    for chunk in range(chunks):
        for j in range(count):

            @pl.when(places[j] >= 0)
            def _(j=j, chunk=chunk):
                copy(j, chunk).wait()

        def body(i, carry, chunk=chunk):
            rows = pl.ds(pl.multiple_of(chunk * height + i * tile, tile), tile)
            widened = held[rows, :].astype(F32)
            center = jnp.mean(widened, axis=-1, keepdims=True)
            moved = widened - center
            spread = jnp.mean(jnp.square(moved), axis=-1, keepdims=True)
            scaled = moved * lax.rsqrt(spread + 1e-05) * gain[...] + shift[...]
            ready[rows, :] = scaled.astype(BF16)
            return carry

        lax.fori_loop(0, height // tile, body, 0)
        out_copy(chunk).start()
    for chunk in range(chunks):
        out_copy(chunk).wait()


def layer_norm(blocks, places, gain, shift):
    rows = blocks[0].shape[0]
    features = gain.shape[0]
    count = len(blocks)
    chunks = 4
    vmem = pl.BlockSpec(memory_space=pltpu.VMEM)
    return pl.pallas_call(
        functools.partial(norm_kernel, count, chunks),
        out_shape=jax.ShapeDtypeStruct((rows, features), BF16),
        in_specs=[pl.BlockSpec(memory_space=pltpu.SMEM)]
        + [pl.BlockSpec(memory_space=pl.ANY)] * count
        + [vmem] * 2,
        out_specs=pl.BlockSpec(memory_space=pl.ANY),
        scratch_shapes=[
            pltpu.VMEM((rows, features), BF16),
            pltpu.VMEM((rows, features), BF16),
            pltpu.SemaphoreType.DMA((count, chunks)),
            pltpu.SemaphoreType.DMA((chunks,)),
        ],
        compiler_params=params(),
        cost_estimate=LIGHT,
        name="norm",
    )(places, *blocks, gain[None, :], shift[None, :])


def shard_layout(lengths, ordering, row_count):
    group_count = lengths.shape[0]
    labels = jnp.arange(group_count, dtype=jnp.int32)
    chosen = (ordering[:, None] == labels[None, :]).astype(jnp.int32)
    ranking = jnp.sum(labels[:, None] * chosen, axis=0)
    earlier = (ranking[None, :] < ranking[:, None]).astype(jnp.int32)
    starts = jnp.sum(earlier * lengths[None, :], axis=1)
    places = jnp.arange(row_count, dtype=jnp.int32)
    member = (
        (places[:, None] >= starts[None, :]) & (places[:, None] < (starts + lengths)[None, :])
    ).astype(jnp.int32)
    row_start = jnp.sum(member * starts[None, :], axis=1)
    return starts, row_start, places - row_start


def rotary_tables(positions):
    rot = HS // 4
    half = rot // 2
    inverse = 10000.0 ** (-(jnp.arange(half, dtype=F32) * 2.0) / rot)
    angles = positions.astype(F32)[:, None] * inverse[None, :]
    cosine, sine = jnp.cos(angles), jnp.sin(angles)
    rows = positions.shape[0]
    rest = jnp.zeros((rows, HS - rot), F32)
    none = jnp.zeros((rows, half), F32)
    straight = jnp.concatenate([cosine, cosine, rest + 1.0], axis=1)
    upper = jnp.concatenate([-sine, none, rest], axis=1)
    lower = jnp.concatenate([none, sine, rest], axis=1)
    return [jnp.tile(table, (1, GROUP_HEADS)) for table in (straight, upper, lower)]


def part_kernel(bundles, wide, *outs):
    columns = wide[...]
    for c in range(3):
        merged = [None] * (GW // 128)
        for k, (first, width) in enumerate(windows()):
            source = 2 * HS * k + HS * c + first
            cut = columns[:, source : source + width]
            mask = head_mask(k, first, cut.shape)
            for w in range(width // 128):
                at = first // 128 + w
                lanes = slice(w * 128, w * 128 + 128)
                if merged[at] is None:
                    merged[at] = cut[:, lanes]
                else:
                    merged[at] = jnp.where(mask[:, lanes], cut[:, lanes], merged[at])
        for out, (begin, end) in zip(outs, bundles):
            for at, piece in enumerate(merged):
                first = c * GW + at * 128
                if begin <= first < end:
                    out[:, first - begin : first - begin + 128] = piece


def part_by_part(weight, group, bundles):
    rows = weight.shape[0]
    tile = 128
    return pl.pallas_call(
        functools.partial(part_kernel, bundles),
        out_shape=[jax.ShapeDtypeStruct((rows, end - begin), BF16) for begin, end in bundles],
        grid=(rows // tile,),
        in_specs=[pl.BlockSpec((tile, 3 * GW), lambda i: (i, group))],
        out_specs=[pl.BlockSpec((tile, end - begin), lambda i: (i, 0)) for begin, end in bundles],
        compiler_params=params(),
        cost_estimate=LIGHT,
        name="parts",
    )(weight)


def qkv_kernel(pieces, bundle, order, normed, *refs):
    count = 1 + max(part[0] for piece in pieces for part in piece)
    weights = refs[:count]
    bias, straight, upper, lower = refs[count : count + 4]
    outs = refs[count + 4 : count + 4 + len(bundle)]
    total, held_rows, held_weights, row_sems, weight_sems = refs[count + 4 + len(bundle) :]
    depth = weights[0].shape[0]

    def row_copy(j):
        lanes = pl.ds(pl.multiple_of(order[j] * depth, 128), depth)
        return pltpu.make_async_copy(
            normed.at[:, lanes], held_rows.at[:, pl.ds(j * depth, depth)], row_sems.at[j]
        )

    def weight_copies(j):
        found, at = [], 0
        for n, (source, first, width) in enumerate(pieces[j]):
            found.append(
                pltpu.make_async_copy(
                    weights[source].at[:, pl.ds(first, width)],
                    held_weights.at[pl.ds(j * depth, depth), pl.ds(at, width)],
                    weight_sems.at[j, n],
                )
            )
            at += width
        return found

    for j in range(len(pieces)):
        row_copy(j).start()
        for one in weight_copies(j):
            one.start()
    halves = 2
    each = len(pieces) // halves
    height = total.shape[0] // 2
    for n in range(halves):
        for j in range(n * each, (n + 1) * each):
            row_copy(j).wait()
            for one in weight_copies(j):
                one.wait()
        inner = slice(n * each * depth, (n + 1) * each * depth)
        for m in range(2):
            rows = slice(m * height, (m + 1) * height)
            part = jnp.dot(
                held_rows[rows, inner], held_weights[inner, :], preferred_element_type=F32
            )
            if n == 0:
                total[rows, :] = part
            else:
                total[rows, :] += part

    tile = 64

    def body(i, carry):
        rows = pl.ds(pl.multiple_of(i * tile, tile), tile)
        for spot, c in enumerate(bundle):
            lanes = slice(spot * GW, (spot + 1) * GW)
            x = total[rows, lanes] + bias[:, lanes]
            if c < 2:
                x = (
                    x * straight[rows, :]
                    + pltpu.roll(x, GW - HS // 8, 1) * upper[rows, :]
                    + pltpu.roll(x, HS // 8, 1) * lower[rows, :]
                )
            outs[spot][rows, :] = x.astype(BF16)
        return carry

    lax.fori_loop(0, total.shape[0] // tile, body, 0)


def project(normed, pieces, order, bias, tables, bundle):
    rows, features = normed.shape
    arrays, plan = [], []
    for piece in pieces:
        parts = []
        for array, first, width in piece:
            arrays.append(array)
            parts.append((len(arrays) - 1, first, width))
        plan.append(parts)
    depth = arrays[0].shape[0]
    columns = len(bundle) * GW
    out = jax.ShapeDtypeStruct((rows, GW), BF16)
    vmem = pl.BlockSpec(memory_space=pltpu.VMEM)
    anywhere = pl.BlockSpec(memory_space=pl.ANY)
    return pl.pallas_call(
        functools.partial(qkv_kernel, plan, bundle),
        out_shape=[out] * len(bundle),
        in_specs=[pl.BlockSpec(memory_space=pltpu.SMEM)]
        + [anywhere] * (len(arrays) + 1)
        + [vmem] * 4,
        out_specs=[vmem] * len(bundle),
        scratch_shapes=[
            pltpu.VMEM((rows, columns), F32),
            pltpu.VMEM((rows, features), BF16),
            pltpu.VMEM((features, columns), BF16),
            pltpu.SemaphoreType.DMA((len(plan),)),
            pltpu.SemaphoreType.DMA((len(plan), max(len(parts) for parts in plan))),
        ],
        compiler_params=params(),
        cost_estimate=LIGHT,
        name="project",
    )(order, normed, *arrays, bias, *tables)


def prefix_kernel(blocks, starts, lengths, *refs):
    queries = refs[:blocks]
    keys, values = refs[blocks : blocks + 2]
    outs = refs[blocks + 2 : 2 * blocks + 2]
    totals = refs[2 * blocks + 2]
    slot = pl.program_id(0)
    slots = pl.num_programs(0)
    rows = queries[0].shape[0]

    @pl.when(slot == 0)
    def _():
        totals[...] = jnp.zeros_like(totals)

    begin, size, offset = [], [], []
    count = 0
    for b in range(blocks):
        begin.append(starts[slot * blocks + b])
        size.append(lengths[slot * blocks + b])
        offset.append(count)
        count = count + size[b]

    def tile(base, height):
        down = lax.broadcasted_iota(jnp.int32, (height, 1), 0) + base
        across = lax.broadcasted_iota(jnp.int32, (1, height), 1) + base

        def sources(place, b):
            within = place - offset[b]
            return jnp.where((within >= 0) & (within < size[b]), within + begin[b], -1)

        picked = None
        for b in range(blocks):
            spread = lax.broadcasted_iota(jnp.int32, (height, rows), 1)
            one_hot = jnp.where(spread == sources(down, b), 1.0, 0.0).astype(BF16)
            part = jnp.dot(one_hot, queries[b][...], preferred_element_type=F32)
            picked = part if picked is None else picked + part
        picked = picked.astype(BF16)
        merged = [jnp.zeros((height, 128), F32) for _ in range(GW // 128)]
        extra = jnp.zeros((height, PACK), F32)
        place = lax.broadcasted_iota(jnp.int32, (height, PACK), 1)
        for k, (first, width) in enumerate(windows()):
            lanes = slice(first, first + width)
            mask = head_mask(k, first, (height, width))
            query = jnp.where(mask, picked[:, lanes], jnp.zeros((), BF16))
            scores = lax.dot_general(
                query,
                keys[0, :, lanes],
                (((1,), (1,)), ((), ())),
                preferred_element_type=F32,
            )
            peak = jnp.max(scores, axis=1, keepdims=True)
            weights = jnp.exp2((scores - peak) * (SCALE * LOG2E))
            mass = jnp.sum(weights, axis=1, keepdims=True)
            blended = jnp.dot(
                weights.astype(BF16), values[0, :, lanes], preferred_element_type=F32
            )
            blended = blended * (1.0 / mass)
            for w in range(width // 128):
                at = first // 128 + w
                cut = slice(w * 128, w * 128 + 128)
                merged[at] = jnp.where(mask[:, cut], blended[:, cut], merged[at])
            level = peak * SCALE + jnp.log(mass)
            high = level.astype(BF16).astype(F32)
            middle = (level - high).astype(BF16).astype(F32)
            low = level - high - middle
            for n, term in enumerate((high, middle, low)):
                extra = jnp.where(place == 32 * n + k, term, extra)
        packed = jnp.concatenate(merged + [extra], axis=1).astype(BF16)
        for b in range(blocks):
            spread = lax.broadcasted_iota(jnp.int32, (rows, height), 0)
            one_hot = jnp.where(spread == sources(across, b), 1.0, 0.0).astype(BF16)
            totals[b] += jnp.dot(one_hot, packed, preferred_element_type=F32)

    large = 256
    small = 128
    full = lax.div(count, large)
    rest = count - full * large

    def body(j, carry):
        tile(j * large, large)
        return carry

    lax.fori_loop(0, full + jnp.where(rest > small, 1, 0), body, 0)

    @pl.when((rest > 0) & (rest <= small))
    def _():
        tile(full * large, small)

    @pl.when(slot == slots - 1)
    def _():
        for b in range(blocks):
            outs[b][...] = totals[b].astype(BF16)


def prefix_attention(group, queries, cache, starts, lengths):
    blocks = len(queries)
    rows = queries[0].shape[0]
    slots, length, _ = cache[0].shape
    width = GW + PACK
    whole = lambda s, starts, lengths: (0, 0)
    block = pl.BlockSpec((1, length, GW), lambda s, starts, lengths: (s, 0, group))
    return pl.pallas_call(
        functools.partial(prefix_kernel, blocks),
        out_shape=[jax.ShapeDtypeStruct((rows, width), BF16)] * blocks,
        grid_spec=pltpu.PrefetchScalarGridSpec(
            num_scalar_prefetch=2,
            grid=(slots,),
            in_specs=[pl.BlockSpec((rows, GW), whole)] * blocks + [block] * 2,
            out_specs=[pl.BlockSpec((rows, width), whole)] * blocks,
            scratch_shapes=[pltpu.VMEM((blocks, rows, width), F32)],
        ),
        compiler_params=params(),
        cost_estimate=LIGHT,
        name="prefix",
    )(starts, lengths, *queries, *cache)


def suffix_kernel(row_start, queries, keys, values, out, levels):
    rows = queries.shape[0]
    tile = 128
    for i in range(rows // tile):
        at = slice(i * tile, (i + 1) * tile)
        wide = (i + 1) * tile
        row = lax.broadcasted_iota(jnp.int32, (tile, wide), 0) + i * tile
        column = lax.broadcasted_iota(jnp.int32, (tile, wide), 1)
        allowed = (column <= row) & (column >= row_start[at, :])
        merged = [jnp.zeros((tile, 128), F32) for _ in range(GW // 128)]
        level_row = jnp.zeros((tile, PACK), F32)
        place = lax.broadcasted_iota(jnp.int32, (tile, PACK), 1)
        for k, (first, width) in enumerate(windows()):
            lanes = slice(first, first + width)
            mask = head_mask(k, first, (tile, width))
            query = jnp.where(mask, queries[at, lanes], jnp.zeros((), BF16))
            scores = lax.dot_general(
                query,
                keys[:wide, lanes],
                (((1,), (1,)), ((), ())),
                preferred_element_type=F32,
            )
            scores = jnp.where(allowed, scores, -jnp.inf)
            peak = jnp.max(scores, axis=1, keepdims=True)
            weights = jnp.exp2((scores - peak) * (SCALE * LOG2E))
            mass = jnp.sum(weights, axis=1, keepdims=True)
            blended = jnp.dot(
                weights.astype(BF16), values[:wide, lanes], preferred_element_type=F32
            )
            blended = blended * (1.0 / mass)
            for w in range(width // 128):
                spot = first // 128 + w
                cut = slice(w * 128, w * 128 + 128)
                merged[spot] = jnp.where(mask[:, cut], blended[:, cut], merged[spot])
            level_row = jnp.where(place == k, peak * SCALE + jnp.log(mass), level_row)
        out[at, :] = jnp.concatenate(merged, axis=1)
        levels[at, :] = level_row


def suffix_attention(row_start, queries, keys, values):
    rows = queries.shape[0]
    return pl.pallas_call(
        suffix_kernel,
        out_shape=(
            jax.ShapeDtypeStruct((rows, GW), F32),
            jax.ShapeDtypeStruct((rows, PACK), F32),
        ),
        compiler_params=params(),
        cost_estimate=LIGHT,
        name="suffix",
    )(row_start, queries, keys, values)


def merge_kernel(blocks, *refs):
    parts = refs[:blocks]
    suffix, levels, out = refs[blocks:]
    rows = suffix.shape[0]
    tile = 128
    for i in range(rows // tile):
        at = slice(i * tile, (i + 1) * tile)
        prefix = parts[0][at, :].astype(F32)
        for b in range(1, blocks):
            prefix = prefix + parts[b][at, :].astype(F32)
        terms = prefix[:, GW:]
        pre = terms + pltpu.roll(terms, PACK - 32, 1) + pltpu.roll(terms, PACK - 64, 1)
        suf = levels[at, :]
        top = jnp.maximum(pre, suf)
        pre = jnp.exp(pre - top)
        suf = jnp.exp(suf - top)
        shares = pre / (pre + suf)
        spread = jnp.zeros((tile, GW), F32)
        for k in range(GROUP_HEADS):
            spread = jnp.where(head_mask(k, 0, (tile, GW)), shares[:, k : k + 1], spread)
        out[at, :] = (spread * prefix[:, :GW] + (1.0 - spread) * suffix[at, :]).astype(BF16)


def merge(parts, suffix, levels):
    rows = suffix.shape[0]
    return pl.pallas_call(
        functools.partial(merge_kernel, len(parts)),
        out_shape=jax.ShapeDtypeStruct((rows, GW), BF16),
        compiler_params=params(),
        cost_estimate=LIGHT,
        name="merge",
    )(*parts, suffix, levels)


def output_kernel(groups, lines, place, *refs):
    attention = refs[: 2 * groups]
    own, landed, crossed, out, held, joined, sems = refs[2 * groups :]
    at = pl.program_id(0)
    rows, share = out.shape[1:]
    depth = own.shape[0]
    half = lines // 2
    side, core = place[0], place[1]

    def own_copy(a):
        lanes = pl.ds(pl.multiple_of((2 * a + side) * share, 128), share)
        return pltpu.make_async_copy(
            own.at[:, lanes], held.at[a, pl.ds(0, depth)], sems.at[2 * a]
        )

    def other_copy(a):
        source = landed if a < half else crossed
        spot = lax.rem(a + core * half, lines)
        lanes = pl.ds((a % half) * share, share)
        return pltpu.make_async_copy(
            source.at[:, lanes], held.at[spot, pl.ds(depth, depth)], sems.at[2 * a + 1]
        )

    @pl.when(at == 0)
    def _():
        for a in range(lines):
            own_copy(a).start()
            other_copy(a).start()
        for n in range(2 * groups):
            joined[:, n * GW : (n + 1) * GW] = attention[n][...]

    own_copy(at).wait()
    sent = lax.rem(at + core * half, lines)
    pltpu.make_async_copy(
        landed.at[:, pl.ds(0, share)],
        held.at[at, pl.ds(depth, depth)],
        sems.at[2 * sent + 1],
    ).wait()
    out[0] = jnp.dot(joined[...], held[at], preferred_element_type=F32)


def output_projection(place, attention, own, landed, crossed, lines):
    rows = attention[0].shape[0]
    depth, features = own.shape
    share = features // (2 * lines)
    vmem = pl.BlockSpec((rows, GW), lambda a, place: (0, 0))
    anywhere = pl.BlockSpec(memory_space=pl.ANY)
    return pl.pallas_call(
        functools.partial(output_kernel, len(attention) // 2, lines),
        out_shape=jax.ShapeDtypeStruct((lines, rows, share), F32),
        grid_spec=pltpu.PrefetchScalarGridSpec(
            num_scalar_prefetch=1,
            grid=(lines,),
            in_specs=[vmem] * len(attention) + [anywhere] * 3,
            out_specs=pl.BlockSpec((1, rows, share), lambda a, place: (a, 0, 0)),
            scratch_shapes=[
                pltpu.VMEM((lines, 2 * depth, share), BF16),
                pltpu.VMEM((rows, 2 * depth), BF16),
                pltpu.SemaphoreType.DMA((2 * lines,)),
            ],
        ),
        compiler_params=params(),
        cost_estimate=LIGHT,
        name="output",
    )(place, *attention, own, landed, crossed)


def on_device(
    hidden_states,
    norm_gain,
    norm_bias,
    qkv_weight,
    qkv_bias,
    dense_weight,
    dense_bias,
    prefix_keys,
    prefix_values,
    suffix_len,
    request_order,
    group_slot,
):
    rows, share = hidden_states.shape
    held, prefix_length, local_width = prefix_keys.shape
    groups_local = local_width // GW
    tok_size = lax.axis_size("tok")
    head_size = lax.axis_size("head")
    chips = tok_size // 2
    lines = head_size // 2
    group_count = held * tok_size
    tok = lax.axis_index("tok")
    head = lax.axis_index("head")
    core, chip = tok % 2, tok // 2
    side, line = head % 2, head // 2

    def to_core(x):
        return lax.ppermute(x, "tok", [(t, t ^ 1) for t in range(tok_size)])

    def to_chip(x, shift):
        return lax.ppermute(
            x,
            "tok",
            [(t, (t // 2 + shift) % chips * 2 + t % 2) for t in range(tok_size)],
        )

    def to_side(x):
        return lax.ppermute(x, "head", [(h, h ^ 1) for h in range(head_size)])

    def after(x, *others):
        return lax.optimization_barrier((x, others))[0]

    layout = jnp.stack([suffix_len[0], request_order[0]])
    layouts = [layout] + [to_chip(layout, shift) for shift in range(1, chips)]
    (first,) = part_by_part(qkv_weight, 0, ((0, 3 * GW),))
    first, layouts = lax.optimization_barrier((first, layouts))

    pairs = [[2 * n, 2 * n + 1] for n in range(chips)]
    cache = [
        lax.all_gather(one, "tok", axis=0, tiled=True, axis_index_groups=pairs)
        for one in (prefix_keys, prefix_values)
    ]

    last = lines - 1

    def to_side_from(x, lowest, highest):
        return lax.ppermute(
            x, "head", [(h, h ^ 1) for h in range(head_size) if lowest <= h // 2 <= highest]
        )

    across = to_side(hidden_states)
    blocks = [hidden_states, across]
    places = [head, head ^ 1]
    arriving = [to_chip(first, shift) for shift in range(1, chips)]
    up = down = hidden_states
    settled = across
    for step in range(last):
        if step > 0:
            up, down, settled, first = lax.optimization_barrier((up, down, settled, first))
            blocks[4 * step - 5 if step > 1 else 1] = settled
        up = lax.ppermute(
            up, "head", [(h, h + 2) for h in range(head_size) if step <= h // 2 < last]
        )
        down = lax.ppermute(
            down, "head", [(h, h - 2) for h in range(head_size) if 0 < h // 2 <= last - step]
        )
        settled = across if step == 0 else blocks[4 * step - 1]
        blocks += [up, to_side_from(up, step + 1, last)]
        blocks += [down, to_side_from(down, 0, last - 1 - step)]
        for there, valid in (
            (line - 1 - step, line >= step + 1),
            (line + 1 + step, line + 1 + step <= last),
        ):
            places += [
                jnp.where(valid, 2 * there + side, -1),
                jnp.where(valid, 2 * there + 1 - side, -1),
            ]
    places = jnp.stack(places).astype(jnp.int32)

    columns = 3 * GW
    order = [tok, tok ^ 1]
    for shift in range(1, chips):
        source = (chip + chips - shift) % chips * 2 + core
        order += [source, source ^ 1]
    order = jnp.stack(order).astype(jnp.int32)
    source, _ = lax.optimization_barrier((qkv_weight, layouts))
    cuts = ((0, columns), (0, GW), (GW, 2 * GW), (2 * GW, columns))
    later = [part_by_part(source, g, cuts) for g in range(1, groups_local)]
    lengths = suffix_len[0]
    starts, row_start, within = shard_layout(lengths, request_order[0], rows)
    labels = jnp.arange(group_count, dtype=jnp.int32)
    slot_match = (group_slot[:, None] == labels[None, :]).astype(jnp.int32)

    def served_spans(one):
        firsts = shard_layout(one[0], one[1], rows)[0]
        spans = jnp.stack(
            [
                jnp.sum(firsts[:, None] * slot_match, axis=0),
                jnp.sum(one[0][:, None] * slot_match, axis=0),
            ]
        )
        return lax.dynamic_slice(spans, (0, chip * 2 * held), (2, 2 * held))

    served = jnp.stack([served_spans(one) for one in layouts], axis=2)
    tables = rotary_tables(prefix_length + within)
    bias = qkv_bias.astype(F32).reshape(groups_local, GROUP_HEADS, 3, HS)
    bias = jnp.transpose(bias, (0, 2, 1, 3)).reshape(groups_local, 1, columns)
    bias = [
        [bias[g]] if g == 0 else [bias[g][:, :GW], bias[g][:, GW:]]
        for g in range(groups_local)
    ]

    half = lines // 2
    outgoing = jnp.concatenate(
        [
            lax.dynamic_slice(
                dense_weight,
                (0, (2 * (core * half + a) + 1 - side) * share),
                (dense_weight.shape[0], share),
            )
            for a in range(half)
        ],
        axis=1,
    )
    ready = (
        served[0].reshape(-1),
        served[1].reshape(-1),
        tables,
        bias,
        order,
        row_start[:, None],
        jnp.stack([side, core]).astype(jnp.int32),
        outgoing,
        later,
        places,
        blocks,
    )
    arriving, ready = lax.optimization_barrier((arriving, ready))
    span_start, span_length, tables, bias, order, row_start, place, outgoing, later = ready[:9]
    places, blocks = ready[9:]

    def send(mine):
        return [to_chip(mine, shift) for shift in range(1, chips)]

    def exchange(queries):
        return [queries] + [to_chip(queries, shift) for shift in range(1, chips)]

    def pieces_of(own, arrived, first, width):
        pieces = [[(one, first, width)] for one in own]
        for n in range(chips - 1):
            for which in range(2):
                pieces.append([(part[n][which], 0, part[n][which].shape[1]) for part in arrived])
        return pieces

    def crossing(arrived):
        return [(one, to_core(one)) for one in arrived]

    coming = [send(after(one[1], arriving)) for one in later]
    first_pieces = pieces_of((first, to_core(first)), [crossing(arriving)], 0, columns)
    normed = layer_norm(blocks, places, norm_gain, norm_bias)
    settled = (normed, coming)
    normed = after(normed, coming)
    landed = to_side(after(outgoing, settled))
    own = [(one[0], to_core(after(one[0], arriving))) for one in later]
    keys_coming = [send(after(one[2], settled)) for one in later]
    heads = [project(normed, first_pieces, order, bias[0][0], tables, (0, 1, 2))]
    asked = [exchange(heads[0][0])]
    settled = heads[0]
    for g in range(1, groups_local):
        arrived = crossing(after(coming[g - 1], settled, keys_coming))
        (queries,) = project(
            normed, pieces_of(own[g - 1], [arrived], 0, GW), order, bias[g][0], tables, (0,)
        )
        asked.append(exchange(queries))
        settled = queries
    suffixes = [suffix_attention(after(row_start, settled), *heads[0])]
    values_coming = [send(after(one[3], asked[1][1:])) for one in later]
    asked[0] = after(asked[0], suffixes[0])
    returned = []
    for g in range(groups_local):
        if g > 0:
            asked[g] = after(asked[g], answers)
        answers = prefix_attention(g, asked[g], cache, span_start, span_length)
        returned.append([answers[0]] + [to_chip(answers[s], chips - s) for s in range(1, chips)])
    crossed = to_core(after(landed, returned[0][1:]))
    for g in range(1, groups_local):
        arrived = [
            crossing(keys_coming[g - 1]),
            crossing(after(values_coming[g - 1], answers, returned[0])),
        ]
        keys, values = project(
            normed, pieces_of(own[g - 1], arrived, GW, 2 * GW), order, bias[g][1], tables, (1, 2)
        )
        suffixes.append(suffix_attention(row_start, asked[g][0], keys, values))
    attention_own, attention_side = [], []
    for g in range(groups_local):
        attention = merge(returned[g], *suffixes[g])
        attention_own.append(attention)
        attention_side.append(to_side(attention))
    partial = output_projection(
        place, attention_own + attention_side, dense_weight, landed, crossed, lines
    )

    cuts = 2
    height = rows // cuts

    def chunk(place, cut):
        place = jnp.clip(place, 0, last)
        return lax.dynamic_slice(
            partial, (place, cut * height, 0), (1, height, share)
        ).reshape(height, share)

    passing = [None] * cuts
    for step in range(last):
        up_pairs = [(h, h + 2) for h in range(head_size) if h // 2 <= step and h // 2 < last]
        down_pairs = [(h, h - 2) for h in range(head_size) if last - h // 2 <= step and h // 2 > 0]
        for cut in range(cuts):
            up = chunk(last + line - step, cut)
            down = chunk(line - last + step, cut)
            if passing[cut] is not None:
                if cut > 0:
                    passing[cut], sent = lax.optimization_barrier((passing[cut], sent))
                up = up + passing[cut][0].astype(F32)
                down = down + passing[cut][1].astype(F32)
            up, down = lax.optimization_barrier((up.astype(BF16), down.astype(BF16)))
            sent = up
            passing[cut] = lax.optimization_barrier(
                (lax.ppermute(up, "head", up_pairs), lax.ppermute(down, "head", down_pairs))
            )
    base = hidden_states.astype(F32) + dense_bias.astype(F32)
    done = [
        base[cut * height : (cut + 1) * height]
        + (chunk(line, cut) + passing[cut][0].astype(F32) + passing[cut][1].astype(F32))
        for cut in range(cuts)
    ]
    return jnp.concatenate(done, axis=0).astype(BF16)


def solution(mesh):
    placed = (
        P("tok", "head"),
        P(),
        P(),
        P("tok", "head"),
        P("head"),
        P("head", None),
        P("head"),
        P("tok", None, "head"),
        P("tok", None, "head"),
        P("tok", None),
        P("tok", None),
        P(),
    )
    return jax.shard_map(
        on_device, mesh=mesh, in_specs=placed, out_specs=P("tok", "head"), check_vma=False
    )
```

profile of v0, /device:TPU:14, one launch (start us, length us, event | category | flops | bytes accessed | tf_op | source)
XLA Modules:
  0.0 430.7 jit_solution(8569349988497435534)
XLA Ops:
  8.5 3.5 collective-permute-start.2
  11.9 2.4 collective-permute-start.3
  15.9 9.8 %parts.2.refs_0_ = bf16[1536,1152]{1,0:T(8,128)(2,1)} custom-call(bf16[1536,2304]{1,0:T(8,128)(2,1)} %wide.2), custom_call_target="tpu_custom_call" | custom-call | flops 1000 | bytes 1000 | tf_op jit(solution)/shard_map/parts/pallas_call | solution.py:169
  27.2 6.7 %collective-permute-done.2.refs_2_ = bf16[640,768]{1,0:T(8,128)(2,1)S(1)} collective-permute-done((bf16[640,768]{1,0:T(8,128)(2,1)S(1)}, bf16[640,768]{1,0:T(8,128)(2,1)S(1)}, u32[]{:S(2)}, u32[]{:S(2)}) %collective-permute-start.2) | collective-permute-done | bytes 983072 | tf_op jit(solution)/shard_map/ppermute | solution.py:625
  33.8 3.3 collective-permute-done.3.refs_4_
  37.4 4.4 %collective-permute-start.5 = (bf16[640,768]{1,0:T(8,128)(2,1)S(1)}, bf16[640,768]{1,0:T(8,128)(2,1)}, u32[]{:S(2)}, u32[]{:S(2)}) collective-permute-start(bf16[640,768]{1,0:T(8,128)(2,1)S(1)} %collective-permute-done.2.refs_2_), channel_id=1, source_target_pairs={{2,4},{3,5},{4,6},{5,7},{10,12},{11,13},{12,14},{13,15},{18,20},{1... | collective-permute-start | bytes 2949128 | tf_op jit(solution)/shard_map/ppermute | solution.py:625
  41.7 1.9 collective-permute-start.6
  43.6 2.4 collective-permute-start.7
  50.2 2.4 constant_dynamic-slice_fusion.1
  52.8 3.2 collective-permute-start.8
  56.0 4.4 %collective-permute-done.5.refs_6_ = bf16[640,768]{1,0:T(8,128)(2,1)} collective-permute-done((bf16[640,768]{1,0:T(8,128)(2,1)S(1)}, bf16[640,768]{1,0:T(8,128)(2,1)}, u32[]{:S(2)}, u32[]{:S(2)}) %collective-permute-start.5) | collective-permute-done | bytes 983072 | tf_op jit(solution)/shard_map/ppermute | solution.py:625
  60.4 5.4 %collective-permute-done.6.refs_8_ = bf16[640,768]{1,0:T(8,128)(2,1)} collective-permute-done((bf16[640,768]{1,0:T(8,128)(2,1)}, bf16[640,768]{1,0:T(8,128)(2,1)}, u32[]{:S(2)}, u32[]{:S(2)}) %collective-permute-start.6) | collective-permute-done | bytes 983072 | tf_op jit(solution)/shard_map/ppermute | solution.py:628
  65.8 4.4 %collective-permute-done.7.refs_3_ = bf16[640,768]{1,0:T(8,128)(2,1)S(1)} collective-permute-done((bf16[640,768]{1,0:T(8,128)(2,1)S(1)}, bf16[640,768]{1,0:T(8,128)(2,1)S(1)}, u32[]{:S(2)}, u32[]{:S(2)}) %collective-permute-start.7) | collective-permute-done | bytes 983072 | tf_op jit(solution)/shard_map/ppermute | solution.py:611
  70.2 1.6 collective-permute-start.11
  71.9 2.2 collective-permute-start.13
  75.1 1.6 pad_maximum_fusion
  76.7 9.8 %parts.3 = (bf16[1536,1152]{1,0:T(8,128)(2,1)}, bf16[1536,384]{1,0:T(8,128)(2,1)}, bf16[1536,384]{1,0:T(8,128)(2,1)}, bf16[1536,384]{1,0:T(8,128)(2,1)}) custom-call(bf16[1536,2304]{1,0:T(8,128)(2,1)} %wide.2), custom_call_target="tpu_custom_call" | custom-call | flops 1000 | bytes 1000 | tf_op jit(solution)/shard_map/parts/pallas_call | solution.py:169
  86.6 1.6 collective-permute-start.9
  88.6 2.4 collective-permute-start.10
  91.0 1.6 collective-permute-start.12
  92.7 1.6 collective-permute-start.14
  96.6 15.2 %collective-permute-done.10.refs_9_ = bf16[640,768]{1,0:T(8,128)(2,1)} collective-permute-done((bf16[640,768]{1,0:T(8,128)(2,1)}, bf16[640,768]{1,0:T(8,128)(2,1)}, u32[]{:S(2)}, u32[]{:S(2)}) %collective-permute-start.10) | collective-permute-done | bytes 983072 | tf_op jit(solution)/shard_map/ppermute | solution.py:611
  111.8 2.0 tile.12
  113.7 2.0 tile.14
  117.6 14.4 %norm.1.normed = bf16[640,6144]{1,0:T(8,128)(2,1)} custom-call(s32[14]{0:T(128)} %stack.131.places, bf16[640,768]{1,0:T(8,128)(2,1)} %refs_0_, bf16[640,768]{1,0:T(8,128)(2,1)} %copy-done.8, bf16[640,768]{1,0:T(8,128)(2,1)} %copy-done.7, bf16[640,768]{1,0:T(8,128)(2,1)} %copy-done.9, bf16[640,768]{1,0:T(8,128)(2,1)} %collective-permute-done.3.refs_4_, ...), custom_call_target="tpu_custom_call" | custom-call | flops 1000 | bytes 1000 | tf_op jit(solution)/shard_map/norm/pallas_call | solution.py:95
  132.0 13.4 %collective-permute-done.15.refs_2_ = bf16[1536,384]{1,0:T(8,128)(2,1)} collective-permute-done((bf16[1536,384]{1,0:T(8,128)(2,1)S(1)}, bf16[1536,384]{1,0:T(8,128)(2,1)}, u32[]{:S(2)}, u32[]{:S(2)}) %collective-permute-start.15) | collective-permute-done | bytes 1179680 | tf_op jit(solution)/shard_map/ppermute | solution.py:585
  146.4 2.5 copy.49.refs_5_.refs_7_
  148.9 2.5 copy.50.refs_6_.refs_8_
  151.3 2.5 copy.51.refs_7_.refs_9_
  153.9 19.3 %project.3 = (bf16[640,384]{1,0:T(8,128)(2,1)}, bf16[640,384]{1,0:T(8,128)(2,1)}, bf16[640,384]{1,0:T(8,128)(2,1)}) custom-call(s32[4]{0:T(128)} %pad_add_fusion.4.order, bf16[640,6144]{1,0:T(8,128)(2,1)} %norm.1.normed, bf16[1536,1152]{1,0:T(8,128)(2,1)} %parts.2.refs_0_, bf16[1536,1152]{1,0:T(8,128)(2,1)} %collective-permute-done.16.refs_1_, ...), custom_call_target="tpu_custom_call" | custom-call | flops 1000 | bytes 1000 | tf_op jit(solution)/shard_map/project/pallas_call | solution.py:264
  173.3 1.6 collective-permute-start.18
  177.4 11.3 %project.4.refs_0_.queries = bf16[640,384]{1,0:T(8,128)(2,1)} custom-call(s32[4]{0:T(128)} %pad_add_fusion.4.order, bf16[640,6144]{1,0:T(8,128)(2,1)} %norm.1.normed, bf16[1536,1152]{1,0:T(8,128)(2,1)} %get-tuple-element.154.refs_0_, bf16[1536,1152]{1,0:T(8,128)(2,1)} %collective-permute-done.19.refs_1_, bf16[1536,384]{1,0:T(8,128)(2,1)} %collective-permute-done.15.refs_2_, ...), custom_call_target="tpu_custom_call" | custom-call | flops 1000 | bytes 1000 | tf_op jit(solution)/shard_map/project/pallas_call | solution.py:264
  188.7 1.6 collective-permute-start.23
  191.2 7.6 %suffix.2 = (f32[640,384]{1,0:T(8,128)}, f32[640,128]{1,0:T(8,128)}) custom-call(s32[640,1]{1,0:T(8,128)} %copy.55.row_start, bf16[640,384]{1,0:T(8,128)(2,1)} %get-tuple-element.164.queries.refs_0_, bf16[640,384]{1,0:T(8,128)(2,1)} %get-tuple-element.155.keys, bf16[640,384]{1,0:T(8,128)(2,1)} %get-tuple-element.156.values), custom_call_target="tpu_custom_call" | custom-call | flops 1000 | bytes 1000 | tf_op jit(solution)/shard_map/suffix/pallas_call | solution.py:441
  199.6 23.5 %prefix.2 = (bf16[640,512]{1,0:T(8,128)(2,1)}, bf16[640,512]{1,0:T(8,128)(2,1)}) custom-call(s32[8]{0:T(128)} %reshape_squeeze.6.starts, s32[8]{0:T(128)} %reshape_squeeze.7.lengths, bf16[640,384]{1,0:T(8,128)(2,1)} %get-tuple-element.164.queries.refs_0_, bf16[640,384]{1,0:T(8,128)(2,1)} %copy-done.11, ...), custom_call_target="tpu_custom_call" | custom-call | flops 1000 | bytes 1000 | tf_op jit(solution)/shard_map/prefix/pallas_call | solution.py:384
  223.1 2.0 collective-permute-start.25
  225.1 15.9 %collective-permute-done.22.refs_1_ = bf16[640,512]{1,0:T(8,128)(2,1)} collective-permute-done((bf16[640,512]{1,0:T(8,128)(2,1)}, bf16[640,512]{1,0:T(8,128)(2,1)}, u32[]{:S(2)}, u32[]{:S(2)}) %collective-permute-start.22) | collective-permute-done | bytes 655392 | tf_op jit(solution)/shard_map/ppermute | solution.py:585
  241.6 24.2 %prefix.3 = (bf16[640,512]{1,0:T(8,128)(2,1)}, bf16[640,512]{1,0:T(8,128)(2,1)}) custom-call(s32[8]{0:T(128)} %reshape_squeeze.6.starts, s32[8]{0:T(128)} %reshape_squeeze.7.lengths, bf16[640,384]{1,0:T(8,128)(2,1)} %project.4.refs_0_.queries, bf16[640,384]{1,0:T(8,128)(2,1)} %copy-done.10, bf16[4,2048,768]{2,1,0:T(8,128)(2,1)} %all-gather.3.cloned.1.call-done.refs_2_, ...), custom_call_target="tpu_custom_call" | custom-call | flops 1000 | bytes 1000 | tf_op jit(solution)/shard_map/prefix/pallas_call | solution.py:384
  267.0 3.6 merge.2.refs_0_
  272.1 14.5 %project.5 = (bf16[640,384]{1,0:T(8,128)(2,1)}, bf16[640,384]{1,0:T(8,128)(2,1)}) custom-call(s32[4]{0:T(128)} %pad_add_fusion.4.order, bf16[640,6144]{1,0:T(8,128)(2,1)} %norm.1.normed, bf16[1536,1152]{1,0:T(8,128)(2,1)} %get-tuple-element.154.refs_0_, bf16[1536,1152]{1,0:T(8,128)(2,1)} %collective-permute-done.19.refs_1_, ...), custom_call_target="tpu_custom_call" | custom-call | flops 1000 | bytes 1000 | tf_op jit(solution)/shard_map/project/pallas_call | solution.py:264
  286.6 7.6 %suffix.3 = (f32[640,384]{1,0:T(8,128)}, f32[640,128]{1,0:T(8,128)}) custom-call(s32[640,1]{1,0:T(8,128)} %copy.59.row_start, bf16[640,384]{1,0:T(8,128)(2,1)} %project.4.refs_0_.queries, bf16[640,384]{1,0:T(8,128)(2,1)} %get-tuple-element.176.keys, bf16[640,384]{1,0:T(8,128)(2,1)} %get-tuple-element.177.values), custom_call_target="tpu_custom_call" | custom-call | flops 1000 | bytes 1000 | tf_op jit(solution)/shard_map/suffix/pallas_call | solution.py:441
  294.2 3.6 merge.3.refs_1_
  298.4 12.8 %collective-permute-done.29.refs_3_ = bf16[640,384]{1,0:T(8,128)(2,1)S(1)} collective-permute-done((bf16[640,384]{1,0:T(8,128)(2,1)}, bf16[640,384]{1,0:T(8,128)(2,1)S(1)}, u32[]{:S(2)}, u32[]{:S(2)}) %collective-permute-start.29) | collective-permute-done | bytes 491552 | tf_op jit(solution)/shard_map/ppermute | solution.py:592
  313.4 12.0 %output.1 = f32[4,640,768]{2,1,0:T(8,128)} custom-call(s32[2]{0:T(128)} %pad_add_fusion.5.place, bf16[640,384]{1,0:T(8,128)(2,1)} %merge.2.refs_0_, bf16[640,384]{1,0:T(8,128)(2,1)} %merge.3.refs_1_, bf16[640,384]{1,0:T(8,128)(2,1)} %collective-permute-done.28.refs_2_, bf16[640,384]{1,0:T(8,128)(2,1)} %copy-done.12, bf16[768,6144]{1,0:T(8,128)(2,1)} %refs_4_.1, ...), custom_call_target="tpu_custom_call" | custom-call | flops 1000 | bytes 1000 | tf_op jit(solution)/shard_map/output/pallas_call | solution.py:534
  325.4 2.3 fusion.13
  329.0 1.6 collective-permute-start.33
  332.7 24.3 %collective-permute-done.32 = bf16[320,768]{1,0:T(8,128)(2,1)S(1)} collective-permute-done((bf16[320,768]{1,0:T(8,128)(2,1)S(1)}, bf16[320,768]{1,0:T(8,128)(2,1)S(1)}, u32[]{:S(2)}, u32[]{:S(2)}) %collective-permute-start.32) | collective-permute-done | bytes 491552 | tf_op jit(solution)/shard_map/ppermute | solution.py:792
  357.0 2.6 fusion.8
  359.6 3.4 collective-permute-start.34
  364.3 3.2 collective-permute-done.38
  367.5 10.5 %collective-permute-done.34 = bf16[320,768]{1,0:T(8,128)(2,1)S(1)} collective-permute-done((bf16[320,768]{1,0:T(8,128)(2,1)}, bf16[320,768]{1,0:T(8,128)(2,1)S(1)}, u32[]{:S(2)}, u32[]{:S(2)}) %collective-permute-start.34) | collective-permute-done | bytes 491552 | tf_op jit(solution)/shard_map/ppermute | solution.py:792
  378.0 2.7 fusion.7
  380.7 3.5 collective-permute-start.40
  385.5 4.6 %collective-permute-start.36 = (bf16[320,768]{1,0:T(8,128)(2,1)S(1)}, bf16[320,768]{1,0:T(8,128)(2,1)S(1)}, u32[]{:S(2)}, u32[]{:S(2)}) collective-permute-start(bf16[320,768]{1,0:T(8,128)(2,1)S(1)} %get-tuple-element.191), channel_id=1, source_target_pairs={{0,2},{1,3},{2,4},{3,5},{4,6},{5,7},{8,10},{9,11},{10,12},{11,13},... | collective-permute-start | bytes 1474568 | tf_op jit(solution)/shard_map/ppermute | solution.py:792
  390.1 1.9 collective-permute-start.37
  392.0 4.8 %collective-permute-done.40 = bf16[320,768]{1,0:T(8,128)(2,1)S(1)} collective-permute-done((bf16[320,768]{1,0:T(8,128)(2,1)S(1)}, bf16[320,768]{1,0:T(8,128)(2,1)S(1)}, u32[]{:S(2)}, u32[]{:S(2)}) %collective-permute-start.40) | collective-permute-done | bytes 491552 | tf_op jit(solution)/shard_map/ppermute | solution.py:792
  396.8 3.4 collective-permute-done.41
  400.2 1.8 fusion.2
  402.0 1.9 collective-permute-start.42
  403.9 4.7 %collective-permute-start.43 = (bf16[320,768]{1,0:T(8,128)(2,1)S(1)}, bf16[320,768]{1,0:T(8,128)(2,1)}, u32[]{:S(2)}, u32[]{:S(2)}) collective-permute-start(bf16[320,768]{1,0:T(8,128)(2,1)S(1)} %get-tuple-element.208), channel_id=1, source_target_pairs={{2,0},{3,1},{4,2},{5,3},{6,4},{7,5},{10,8},{11,9},{12,10},{13,11},... | collective-permute-start | bytes 1474568 | tf_op jit(solution)/shard_map/ppermute | solution.py:792
  408.8 2.0 collective-permute-done.37
  410.9 6.2 %collective-permute-done.42 = bf16[320,768]{1,0:T(8,128)(2,1)} collective-permute-done((bf16[320,768]{1,0:T(8,128)(2,1)S(1)}, bf16[320,768]{1,0:T(8,128)(2,1)}, u32[]{:S(2)}, u32[]{:S(2)}) %collective-permute-start.42) | collective-permute-done | bytes 491552 | tf_op jit(solution)/shard_map/ppermute | solution.py:792
  417.1 3.1 collective-permute-done.43
  420.2 2.4 fusion.1
  (140 shorter events, 33.2 us)
Async XLA Ops:
  6.5 192.3 %all-gather.3.cloned.1.call-start = ((), (), s32[]{:S(2)}) async-start(), calls=%async_computation | async-start | bytes 18874368 | tf_op jit(solution)/shard_map/all_gather | solution.py:604
  7.3 1.2 copy-start.1
  7.3 7.7 %copy-start.15 = (s32[1,8]{1,0:T(1,128)S(1)}, s32[1,8]{1,0:T(1,128)}, u32[]{:S(2)}) copy-start(s32[1,8]{1,0:T(1,128)} %param.21) | copy-start | bytes 100
  7.3 7.7 %copy-start.16 = (s32[1,8]{1,0:T(1,128)S(1)}, s32[1,8]{1,0:T(1,128)}, u32[]{:S(2)}) copy-start(s32[1,8]{1,0:T(1,128)} %param.22) | copy-start | bytes 100
  7.3 8.3 %copy-start.13 = (bf16[2304]{0:T(1024)(128)(2,1)S(1)}, bf16[2304]{0:T(1024)(128)(2,1)}, u32[]{:S(2)}) copy-start(bf16[2304]{0:T(1024)(128)(2,1)} %param.16) | copy-start | bytes 13828
  7.3 191.5 %all-gather.5.cloned.1.call-start = ((), (), s32[]{:S(2)}) async-start(), calls=%async_computation.1 | async-start | bytes 18874368 | tf_op jit(solution)/shard_map/all_gather | solution.py:604
  8.5 25.4 %collective-permute-start.2 = (bf16[640,768]{1,0:T(8,128)(2,1)S(1)}, bf16[640,768]{1,0:T(8,128)(2,1)S(1)}, u32[]{:S(2)}, u32[]{:S(2)}) collective-permute-start(bf16[640,768]{1,0:T(8,128)(2,1)S(1)} %copy-done.1), channel_id=1, source_target_pairs={{0,2},{1,3},{2,4},{3,5},{4,6},{5,7},{8,10},{9,11},{10,12},{11,13},... | collective-permute-start | bytes 2949128 | tf_op jit(solution)/shard_map/ppermute | solution.py:625
  11.9 25.2 %collective-permute-start.3 = (bf16[640,768]{1,0:T(8,128)(2,1)S(1)}, bf16[640,768]{1,0:T(8,128)(2,1)}, u32[]{:S(2)}, u32[]{:S(2)}) collective-permute-start(bf16[640,768]{1,0:T(8,128)(2,1)S(1)} %copy-done.1), channel_id=1, source_target_pairs={{2,0},{3,1},{4,2},{5,3},{6,4},{7,5},{10,8},{11,9},{12,10},{13,11},... | collective-permute-start | bytes 2949128 | tf_op jit(solution)/shard_map/ppermute | solution.py:628
  14.4 23.0 %collective-permute-start.4 = (bf16[640,768]{1,0:T(8,128)(2,1)S(1)}, bf16[640,768]{1,0:T(8,128)(2,1)S(1)}, u32[]{:S(2)}, u32[]{:S(2)}) collective-permute-start(bf16[640,768]{1,0:T(8,128)(2,1)S(1)} %copy-done.1), channel_id=1, source_target_pairs={{0,1},{1,0},{2,3},{3,2},{4,5},{5,4},{6,7},{7,6},{8,9},{9,8},{10,11... | collective-permute-start | bytes 2949128 | tf_op jit(solution)/shard_map/ppermute | solution.py:592
  15.0 10.7 %collective-permute-start = (s32[2,8]{1,0:T(2,128)S(1)}, s32[2,8]{1,0:T(2,128)S(1)}, u32[]{:S(2)}, u32[]{:S(2)}) collective-permute-start(s32[2,8]{1,0:T(2,128)S(1)} %pad_add_fusion.1), channel_id=1, source_target_pairs={{0,16},{8,24},{16,0},{24,8},{1,17},{9,25},{17,1},{25,9},{2,18},{10... | collective-permute-start | bytes 200 | tf_op jit(solution)/shard_map/ppermute | solution.py:585
  25.7 86.1 %collective-permute-start.1 = (bf16[1536,1152]{1,0:T(8,128)(2,1)}, bf16[1536,1152]{1,0:T(8,128)(2,1)}, u32[]{:S(2)}, u32[]{:S(2)}) collective-permute-start(bf16[1536,1152]{1,0:T(8,128)(2,1)} %parts.2.refs_0_), channel_id=1, source_target_pairs={{0,16},{8,24},{16,0},{24,8},{1,17},{9,25},{17,1},{25,9},{2,18},{10... | collective-permute-start | bytes 10616840 | tf_op jit(solution)/shard_map/ppermute | solution.py:585
  33.8 18.7 %copy-start.7 = (bf16[640,768]{1,0:T(8,128)(2,1)}, bf16[640,768]{1,0:T(8,128)(2,1)S(1)}, u32[]{:S(2)}) copy-start(bf16[640,768]{1,0:T(8,128)(2,1)S(1)} %collective-permute-done.2.refs_2_) | copy-start | bytes 2949124
  37.4 15.2 %copy-start.8 = (bf16[640,768]{1,0:T(8,128)(2,1)}, bf16[640,768]{1,0:T(8,128)(2,1)S(1)}, u32[]{:S(2)}) copy-start(bf16[640,768]{1,0:T(8,128)(2,1)S(1)} %collective-permute-done.4.refs_1_) | copy-start | bytes 2949124
  37.4 23.1 %collective-permute-start.5 = (bf16[640,768]{1,0:T(8,128)(2,1)S(1)}, bf16[640,768]{1,0:T(8,128)(2,1)}, u32[]{:S(2)}, u32[]{:S(2)}) collective-permute-start(bf16[640,768]{1,0:T(8,128)(2,1)S(1)} %collective-permute-done.2.refs_2_), channel_id=1, source_target_pairs={{2,4},{3,5},{4,6},{5,7},{10,12},{11,13},{12,14},{13,15},{18,20},{1... | collective-permute-start | bytes 2949128 | tf_op jit(solution)/shard_map/ppermute | solution.py:625
  41.7 24.1 %collective-permute-start.6 = (bf16[640,768]{1,0:T(8,128)(2,1)}, bf16[640,768]{1,0:T(8,128)(2,1)}, u32[]{:S(2)}, u32[]{:S(2)}) collective-permute-start(bf16[640,768]{1,0:T(8,128)(2,1)} %collective-permute-done.3.refs_4_), channel_id=1, source_target_pairs={{2,0},{3,1},{4,2},{5,3},{10,8},{11,9},{12,10},{13,11},{18,16},{19,... | collective-permute-start | bytes 2949128 | tf_op jit(solution)/shard_map/ppermute | solution.py:628
  43.6 26.6 %collective-permute-start.7 = (bf16[640,768]{1,0:T(8,128)(2,1)S(1)}, bf16[640,768]{1,0:T(8,128)(2,1)S(1)}, u32[]{:S(2)}, u32[]{:S(2)}) collective-permute-start(bf16[640,768]{1,0:T(8,128)(2,1)S(1)} %collective-permute-done.2.refs_2_), channel_id=1, source_target_pairs={{2,3},{3,2},{4,5},{5,4},{6,7},{7,6},{10,11},{11,10},{12,13},{13,12... | collective-permute-start | bytes 2949128 | tf_op jit(solution)/shard_map/ppermute | solution.py:611
  52.8 35.8 %collective-permute-start.8 = (bf16[640,768]{1,0:T(8,128)(2,1)}, bf16[640,768]{1,0:T(8,128)(2,1)}, u32[]{:S(2)}, u32[]{:S(2)}) collective-permute-start(bf16[640,768]{1,0:T(8,128)(2,1)} %collective-permute-done.3.refs_4_), channel_id=1, source_target_pairs={{0,1},{1,0},{2,3},{3,2},{4,5},{5,4},{8,9},{9,8},{10,11},{11,10},{1... | collective-permute-start | bytes 2949128 | tf_op jit(solution)/shard_map/ppermute | solution.py:611
  70.2 4.9 %copy-start.9 = (bf16[640,768]{1,0:T(8,128)(2,1)}, bf16[640,768]{1,0:T(8,128)(2,1)S(1)}, u32[]{:S(2)}) copy-start(bf16[640,768]{1,0:T(8,128)(2,1)S(1)} %collective-permute-done.7.refs_3_) | copy-start | bytes 2949124
  70.2 20.8 %collective-permute-start.11 = (bf16[640,768]{1,0:T(8,128)(2,1)}, bf16[640,768]{1,0:T(8,128)(2,1)}, u32[]{:S(2)}, u32[]{:S(2)}) collective-permute-start(bf16[640,768]{1,0:T(8,128)(2,1)} %collective-permute-done.5.refs_6_), channel_id=1, source_target_pairs={{4,6},{5,7},{12,14},{13,15},{20,22},{21,23},{28,30},{29,31}} | collective-permute-start | bytes 2949128 | tf_op jit(solution)/shard_map/ppermute | solution.py:625
  71.9 20.8 %collective-permute-start.13 = (bf16[640,768]{1,0:T(8,128)(2,1)}, bf16[640,768]{1,0:T(8,128)(2,1)}, u32[]{:S(2)}, u32[]{:S(2)}) collective-permute-start(bf16[640,768]{1,0:T(8,128)(2,1)} %collective-permute-done.6.refs_8_), channel_id=1, source_target_pairs={{2,0},{3,1},{10,8},{11,9},{18,16},{19,17},{26,24},{27,25}} | collective-permute-start | bytes 2949128 | tf_op jit(solution)/shard_map/ppermute | solution.py:628
  76.7 17.8 %copy-start.17 = (s32[8]{0:T(128)S(1)}, s32[8]{0:T(128)}, u32[]{:S(2)}) copy-start(s32[8]{0:T(128)} %param.23) | copy-start | bytes 100
  76.7 19.8 %copy-start = (bf16[1536,1152]{1,0:T(8,128)(2,1)S(1)}, bf16[1536,1152]{1,0:T(8,128)(2,1)}, u32[]{:S(2)}) copy-start(bf16[1536,1152]{1,0:T(8,128)(2,1)} %parts.2.refs_0_) | copy-start | bytes 10616836
  86.6 9.9 %collective-permute-start.9 = (bf16[640,768]{1,0:T(8,128)(2,1)}, bf16[640,768]{1,0:T(8,128)(2,1)}, u32[]{:S(2)}, u32[]{:S(2)}) collective-permute-start(bf16[640,768]{1,0:T(8,128)(2,1)} %collective-permute-done.5.refs_6_), channel_id=1, source_target_pairs={{4,5},{5,4},{6,7},{7,6},{12,13},{13,12},{14,15},{15,14},{20,21},{2... | collective-permute-start | bytes 2949128 | tf_op jit(solution)/shard_map/ppermute | solution.py:611
  88.6 23.2 %collective-permute-start.10 = (bf16[640,768]{1,0:T(8,128)(2,1)}, bf16[640,768]{1,0:T(8,128)(2,1)}, u32[]{:S(2)}, u32[]{:S(2)}) collective-permute-start(bf16[640,768]{1,0:T(8,128)(2,1)} %collective-permute-done.6.refs_8_), channel_id=1, source_target_pairs={{0,1},{1,0},{2,3},{3,2},{8,9},{9,8},{10,11},{11,10},{16,17},{17,16... | collective-permute-start | bytes 2949128 | tf_op jit(solution)/shard_map/ppermute | solution.py:611
  91.0 20.7 %collective-permute-start.12 = (bf16[640,768]{1,0:T(8,128)(2,1)}, bf16[640,768]{1,0:T(8,128)(2,1)}, u32[]{:S(2)}, u32[]{:S(2)}) collective-permute-start(bf16[640,768]{1,0:T(8,128)(2,1)} %collective-permute-done.11.refs_10_), channel_id=1, source_target_pairs={{6,7},{7,6},{14,15},{15,14},{22,23},{23,22},{30,31},{31,30}} | collective-permute-start | bytes 2949128 | tf_op jit(solution)/shard_map/ppermute | solution.py:611
  92.7 19.1 %collective-permute-start.14 = (bf16[640,768]{1,0:T(8,128)(2,1)}, bf16[640,768]{1,0:T(8,128)(2,1)}, u32[]{:S(2)}, u32[]{:S(2)}) collective-permute-start(bf16[640,768]{1,0:T(8,128)(2,1)} %collective-permute-done.13.refs_12_), channel_id=1, source_target_pairs={{0,1},{1,0},{8,9},{9,8},{16,17},{17,16},{24,25},{25,24}} | collective-permute-start | bytes 2949128 | tf_op jit(solution)/shard_map/ppermute | solution.py:611
  96.5 19.3 %copy-start.6 = (f32[640,96]{0,1:T(8,128)S(1)}, f32[640,96]{0,1:T(8,128)}, u32[]{:S(2)}) copy-start(f32[640,96]{0,1:T(8,128)} %get-tuple-element.231) | copy-start | bytes 737284
  96.5 20.4 %copy-start.18 = (bf16[1536,384]{1,0:T(8,128)(2,1)S(1)}, bf16[1536,384]{1,0:T(8,128)(2,1)}, u32[]{:S(2)}) copy-start(bf16[1536,384]{1,0:T(8,128)(2,1)} %get-tuple-element.144) | copy-start | bytes 3538948
  96.5 57.4 %collective-permute-start.16 = (bf16[1536,1152]{1,0:T(8,128)(2,1)S(1)}, bf16[1536,1152]{1,0:T(8,128)(2,1)}, u32[]{:S(2)}, u32[]{:S(2)}) collective-permute-start(bf16[1536,1152]{1,0:T(8,128)(2,1)S(1)} %copy-done), channel_id=1, source_target_pairs={{0,8},{8,0},{16,24},{24,16},{1,9},{9,1},{17,25},{25,17},{2,10},{10... | collective-permute-start | bytes 10616840 | tf_op jit(solution)/shard_map/ppermute | solution.py:582
  116.9 37.0 %collective-permute-start.17 = (bf16[1536,1152]{1,0:T(8,128)(2,1)}, bf16[1536,1152]{1,0:T(8,128)(2,1)}, u32[]{:S(2)}, u32[]{:S(2)}) collective-permute-start(bf16[1536,1152]{1,0:T(8,128)(2,1)} %collective-permute-done.1.refs_2_), channel_id=1, source_target_pairs={{0,8},{8,0},{16,24},{24,16},{1,9},{9,1},{17,25},{25,17},{2,10},{10... | collective-permute-start | bytes 10616840 | tf_op jit(solution)/shard_map/ppermute | solution.py:582
  116.9 28.5 %collective-permute-start.15 = (bf16[1536,384]{1,0:T(8,128)(2,1)S(1)}, bf16[1536,384]{1,0:T(8,128)(2,1)}, u32[]{:S(2)}, u32[]{:S(2)}) collective-permute-start(bf16[1536,384]{1,0:T(8,128)(2,1)S(1)} %copy-done.18), channel_id=1, source_target_pairs={{0,16},{8,24},{16,0},{24,8},{1,17},{9,25},{17,1},{25,9},{2,18},{10... | collective-permute-start | bytes 3538952 | tf_op jit(solution)/shard_map/ppermute | solution.py:585
  117.4 57.5 %collective-permute-start.19 = (bf16[1536,1152]{1,0:T(8,128)(2,1)}, bf16[1536,1152]{1,0:T(8,128)(2,1)}, u32[]{:S(2)}, u32[]{:S(2)}) collective-permute-start(bf16[1536,1152]{1,0:T(8,128)(2,1)} %get-tuple-element.154.refs_0_), channel_id=1, source_target_pairs={{0,8},{8,0},{16,24},{24,16},{1,9},{9,1},{17,25},{25,17},{2,10},{10... | collective-permute-start | bytes 10616840 | tf_op jit(solution)/shard_map/ppermute | solution.py:582
  145.3 27.9 %collective-permute-start.20 = (bf16[1536,384]{1,0:T(8,128)(2,1)}, bf16[1536,384]{1,0:T(8,128)(2,1)}, u32[]{:S(2)}, u32[]{:S(2)}) collective-permute-start(bf16[1536,384]{1,0:T(8,128)(2,1)} %get-tuple-element.158), channel_id=1, source_target_pairs={{0,16},{8,24},{16,0},{24,8},{1,17},{9,25},{17,1},{25,9},{2,18},{10... | collective-permute-start | bytes 3538952 | tf_op jit(solution)/shard_map/ppermute | solution.py:585
  145.9 79.3 %collective-permute-start.30 = (bf16[768,1536]{1,0:T(8,128)(2,1)}, bf16[768,1536]{1,0:T(8,128)(2,1)}, u32[]{:S(2)}, u32[]{:S(2)}) collective-permute-start(bf16[768,1536]{1,0:T(8,128)(2,1)} %pad_maximum_fusion), channel_id=1, source_target_pairs={{0,1},{1,0},{2,3},{3,2},{4,5},{5,4},{6,7},{7,6},{8,9},{9,8},{10,11... | collective-permute-start | bytes 7077896 | tf_op jit(solution)/shard_map/ppermute | solution.py:592
  173.3 3.1 collective-permute-start.21
  173.3 25.5 %collective-permute-start.18 = (bf16[640,384]{1,0:T(8,128)(2,1)}, bf16[640,384]{1,0:T(8,128)(2,1)S(1)}, u32[]{:S(2)}, u32[]{:S(2)}) collective-permute-start(bf16[640,384]{1,0:T(8,128)(2,1)} %get-tuple-element.164.queries.refs_0_), channel_id=1, source_target_pairs={{0,16},{8,24},{16,0},{24,8},{1,17},{9,25},{17,1},{25,9},{2,18},{10... | collective-permute-start | bytes 1474568 | tf_op jit(solution)/shard_map/ppermute | solution.py:585
  176.3 1.0 copy-start.5
  188.7 34.5 %collective-permute-start.23 = (bf16[640,384]{1,0:T(8,128)(2,1)}, bf16[640,384]{1,0:T(8,128)(2,1)S(1)}, u32[]{:S(2)}, u32[]{:S(2)}) collective-permute-start(bf16[640,384]{1,0:T(8,128)(2,1)} %project.4.refs_0_.queries), channel_id=1, source_target_pairs={{0,16},{8,24},{16,0},{24,8},{1,17},{9,25},{17,1},{25,9},{2,18},{10... | collective-permute-start | bytes 1474568 | tf_op jit(solution)/shard_map/ppermute | solution.py:585
  198.8 0.8 copy-start.11
  223.1 18.0 %collective-permute-start.22 = (bf16[640,512]{1,0:T(8,128)(2,1)}, bf16[640,512]{1,0:T(8,128)(2,1)}, u32[]{:S(2)}, u32[]{:S(2)}) collective-permute-start(bf16[640,512]{1,0:T(8,128)(2,1)} %get-tuple-element.167), channel_id=1, source_target_pairs={{0,16},{8,24},{16,0},{24,8},{1,17},{9,25},{17,1},{25,9},{2,18},{10... | collective-permute-start | bytes 1966088 | tf_op jit(solution)/shard_map/ppermute | solution.py:585
  223.1 2.0 copy-start.10
  223.1 42.7 %collective-permute-start.25 = (bf16[1536,384]{1,0:T(8,128)(2,1)}, bf16[1536,384]{1,0:T(8,128)(2,1)S(1)}, u32[]{:S(2)}, u32[]{:S(2)}) collective-permute-start(bf16[1536,384]{1,0:T(8,128)(2,1)} %get-tuple-element.173), channel_id=1, source_target_pairs={{0,16},{8,24},{16,0},{24,8},{1,17},{9,25},{17,1},{25,9},{2,18},{10... | collective-permute-start | bytes 3538952 | tf_op jit(solution)/shard_map/ppermute | solution.py:585
  241.1 70.1 %collective-permute-start.31 = (bf16[768,1536]{1,0:T(8,128)(2,1)}, bf16[768,1536]{1,0:T(8,128)(2,1)S(1)}, u32[]{:S(2)}, u32[]{:S(2)}) collective-permute-start(bf16[768,1536]{1,0:T(8,128)(2,1)} %collective-permute-done.30.refs_5_), channel_id=1, source_target_pairs={{0,8},{8,0},{16,24},{24,16},{1,9},{9,1},{17,25},{25,17},{2,10},{10... | collective-permute-start | bytes 7077896 | tf_op jit(solution)/shard_map/ppermute | solution.py:582
  241.1 30.9 %collective-permute-start.26 = (bf16[1536,384]{1,0:T(8,128)(2,1)}, bf16[1536,384]{1,0:T(8,128)(2,1)}, u32[]{:S(2)}, u32[]{:S(2)}) collective-permute-start(bf16[1536,384]{1,0:T(8,128)(2,1)} %collective-permute-done.20.refs_2_), channel_id=1, source_target_pairs={{0,8},{8,0},{16,24},{24,16},{1,9},{9,1},{17,25},{25,17},{2,10},{10... | collective-permute-start | bytes 3538952 | tf_op jit(solution)/shard_map/ppermute | solution.py:582
  265.8 6.3 %copy-start.4 = (bf16[1536,384]{1,0:T(8,128)(2,1)}, bf16[1536,384]{1,0:T(8,128)(2,1)S(1)}, u32[]{:S(2)}) copy-start(bf16[1536,384]{1,0:T(8,128)(2,1)S(1)} %collective-permute-done.25.refs_3_) | copy-start | bytes 3538948
  265.8 6.2 %collective-permute-start.27 = (bf16[1536,384]{1,0:T(8,128)(2,1)S(1)}, bf16[1536,384]{1,0:T(8,128)(2,1)}, u32[]{:S(2)}, u32[]{:S(2)}) collective-permute-start(bf16[1536,384]{1,0:T(8,128)(2,1)S(1)} %collective-permute-done.25.refs_3_), channel_id=1, source_target_pairs={{0,8},{8,0},{16,24},{24,16},{1,9},{9,1},{17,25},{25,17},{2,10},{10... | collective-permute-start | bytes 3538952 | tf_op jit(solution)/shard_map/ppermute | solution.py:582
  265.9 28.3 %collective-permute-start.24 = (bf16[640,512]{1,0:T(8,128)(2,1)}, bf16[640,512]{1,0:T(8,128)(2,1)}, u32[]{:S(2)}, u32[]{:S(2)}) collective-permute-start(bf16[640,512]{1,0:T(8,128)(2,1)} %get-tuple-element.171), channel_id=1, source_target_pairs={{0,16},{8,24},{16,0},{24,8},{1,17},{9,25},{17,1},{25,9},{2,18},{10... | collective-permute-start | bytes 1966088 | tf_op jit(solution)/shard_map/ppermute | solution.py:585
  270.6 27.8 %collective-permute-start.28 = (bf16[640,384]{1,0:T(8,128)(2,1)}, bf16[640,384]{1,0:T(8,128)(2,1)}, u32[]{:S(2)}, u32[]{:S(2)}) collective-permute-start(bf16[640,384]{1,0:T(8,128)(2,1)} %merge.2.refs_0_), channel_id=1, source_target_pairs={{0,1},{1,0},{2,3},{3,2},{4,5},{5,4},{6,7},{7,6},{8,9},{9,8},{10,11... | collective-permute-start | bytes 1474568 | tf_op jit(solution)/shard_map/ppermute | solution.py:592
  297.8 13.4 %collective-permute-start.29 = (bf16[640,384]{1,0:T(8,128)(2,1)}, bf16[640,384]{1,0:T(8,128)(2,1)S(1)}, u32[]{:S(2)}, u32[]{:S(2)}) collective-permute-start(bf16[640,384]{1,0:T(8,128)(2,1)} %merge.3.refs_1_), channel_id=1, source_target_pairs={{0,1},{1,0},{2,3},{3,2},{4,5},{5,4},{6,7},{7,6},{8,9},{9,8},{10,11... | collective-permute-start | bytes 1474568 | tf_op jit(solution)/shard_map/ppermute | solution.py:592
  312.0 1.4 copy-start.3
  327.7 29.2 %collective-permute-start.32 = (bf16[320,768]{1,0:T(8,128)(2,1)S(1)}, bf16[320,768]{1,0:T(8,128)(2,1)S(1)}, u32[]{:S(2)}, u32[]{:S(2)}) collective-permute-start(bf16[320,768]{1,0:T(8,128)(2,1)S(1)} %get-tuple-element.183), channel_id=1, source_target_pairs={{0,2},{1,3},{8,10},{9,11},{16,18},{17,19},{24,26},{25,27}} | collective-permute-start | bytes 1474568 | tf_op jit(solution)/shard_map/ppermute | solution.py:792
  329.0 27.9 %collective-permute-start.33 = (bf16[320,768]{1,0:T(8,128)(2,1)S(1)}, bf16[320,768]{1,0:T(8,128)(2,1)}, u32[]{:S(2)}, u32[]{:S(2)}) collective-permute-start(bf16[320,768]{1,0:T(8,128)(2,1)S(1)} %get-tuple-element.184), channel_id=1, source_target_pairs={{6,4},{7,5},{14,12},{15,13},{22,20},{23,21},{30,28},{31,29}} | collective-permute-start | bytes 1474568 | tf_op jit(solution)/shard_map/ppermute | solution.py:792
  330.7 36.8 %collective-permute-start.38 = (bf16[320,768]{1,0:T(8,128)(2,1)S(1)}, bf16[320,768]{1,0:T(8,128)(2,1)S(1)}, u32[]{:S(2)}, u32[]{:S(2)}) collective-permute-start(bf16[320,768]{1,0:T(8,128)(2,1)S(1)} %get-tuple-element.195), channel_id=1, source_target_pairs={{0,2},{1,3},{8,10},{9,11},{16,18},{17,19},{24,26},{25,27}} | collective-permute-start | bytes 1474568 | tf_op jit(solution)/shard_map/ppermute | solution.py:792
  332.0 35.5 %collective-permute-start.39 = (bf16[320,768]{1,0:T(8,128)(2,1)S(1)}, bf16[320,768]{1,0:T(8,128)(2,1)S(1)}, u32[]{:S(2)}, u32[]{:S(2)}) collective-permute-start(bf16[320,768]{1,0:T(8,128)(2,1)S(1)} %get-tuple-element.196), channel_id=1, source_target_pairs={{6,4},{7,5},{14,12},{15,13},{22,20},{23,21},{30,28},{31,29}} | collective-permute-start | bytes 1474568 | tf_op jit(solution)/shard_map/ppermute | solution.py:792
  359.6 18.4 %collective-permute-start.34 = (bf16[320,768]{1,0:T(8,128)(2,1)}, bf16[320,768]{1,0:T(8,128)(2,1)S(1)}, u32[]{:S(2)}, u32[]{:S(2)}) collective-permute-start(bf16[320,768]{1,0:T(8,128)(2,1)} %get-tuple-element.187), channel_id=1, source_target_pairs={{0,2},{1,3},{2,4},{3,5},{8,10},{9,11},{10,12},{11,13},{16,18},{17,... | collective-permute-start | bytes 1474568 | tf_op jit(solution)/shard_map/ppermute | solution.py:792
  363.0 15.0 %collective-permute-start.35 = (bf16[320,768]{1,0:T(8,128)(2,1)S(1)}, bf16[320,768]{1,0:T(8,128)(2,1)}, u32[]{:S(2)}, u32[]{:S(2)}) collective-permute-start(bf16[320,768]{1,0:T(8,128)(2,1)S(1)} %get-tuple-element.188), channel_id=1, source_target_pairs={{4,2},{5,3},{6,4},{7,5},{12,10},{13,11},{14,12},{15,13},{20,18},{2... | collective-permute-start | bytes 1474568 | tf_op jit(solution)/shard_map/ppermute | solution.py:792
  380.7 28.0 %copy-start.14 = (bf16[768]{0:T(1024)(128)(2,1)S(1)}, bf16[768]{0:T(1024)(128)(2,1)}, u32[]{:S(2)}) copy-start(bf16[768]{0:T(1024)(128)(2,1)} %param.18) | copy-start | bytes 4612
  380.7 28.0 %copy-start.2 = (bf16[640,768]{1,0:T(8,128)(2,1)S(1)}, bf16[640,768]{1,0:T(8,128)(2,1)}, u32[]{:S(2)}) copy-start(bf16[640,768]{1,0:T(8,128)(2,1)} %refs_0_) | copy-start | bytes 2949124
  380.7 16.1 %collective-permute-start.40 = (bf16[320,768]{1,0:T(8,128)(2,1)S(1)}, bf16[320,768]{1,0:T(8,128)(2,1)S(1)}, u32[]{:S(2)}, u32[]{:S(2)}) collective-permute-start(bf16[320,768]{1,0:T(8,128)(2,1)S(1)} %get-tuple-element.201), channel_id=1, source_target_pairs={{0,2},{1,3},{2,4},{3,5},{8,10},{9,11},{10,12},{11,13},{16,18},{17,... | collective-permute-start | bytes 1474568 | tf_op jit(solution)/shard_map/ppermute | solution.py:792
  384.2 16.0 %collective-permute-start.41 = (bf16[320,768]{1,0:T(8,128)(2,1)S(1)}, bf16[320,768]{1,0:T(8,128)(2,1)S(1)}, u32[]{:S(2)}, u32[]{:S(2)}) collective-permute-start(bf16[320,768]{1,0:T(8,128)(2,1)S(1)} %get-tuple-element.202), channel_id=1, source_target_pairs={{4,2},{5,3},{6,4},{7,5},{12,10},{13,11},{14,12},{15,13},{20,18},{2... | collective-permute-start | bytes 1474568 | tf_op jit(solution)/shard_map/ppermute | solution.py:792
  385.5 23.3 %collective-permute-start.36 = (bf16[320,768]{1,0:T(8,128)(2,1)S(1)}, bf16[320,768]{1,0:T(8,128)(2,1)S(1)}, u32[]{:S(2)}, u32[]{:S(2)}) collective-permute-start(bf16[320,768]{1,0:T(8,128)(2,1)S(1)} %get-tuple-element.191), channel_id=1, source_target_pairs={{0,2},{1,3},{2,4},{3,5},{4,6},{5,7},{8,10},{9,11},{10,12},{11,13},... | collective-permute-start | bytes 1474568 | tf_op jit(solution)/shard_map/ppermute | solution.py:792
  390.1 20.8 %collective-permute-start.37 = (bf16[320,768]{1,0:T(8,128)(2,1)S(1)}, bf16[320,768]{1,0:T(8,128)(2,1)}, u32[]{:S(2)}, u32[]{:S(2)}) collective-permute-start(bf16[320,768]{1,0:T(8,128)(2,1)S(1)} %get-tuple-element.192), channel_id=1, source_target_pairs={{2,0},{3,1},{4,2},{5,3},{6,4},{7,5},{10,8},{11,9},{12,10},{13,11},... | collective-permute-start | bytes 1474568 | tf_op jit(solution)/shard_map/ppermute | solution.py:792
  402.0 15.1 %collective-permute-start.42 = (bf16[320,768]{1,0:T(8,128)(2,1)S(1)}, bf16[320,768]{1,0:T(8,128)(2,1)}, u32[]{:S(2)}, u32[]{:S(2)}) collective-permute-start(bf16[320,768]{1,0:T(8,128)(2,1)S(1)} %get-tuple-element.207), channel_id=1, source_target_pairs={{0,2},{1,3},{2,4},{3,5},{4,6},{5,7},{8,10},{9,11},{10,12},{11,13},... | collective-permute-start | bytes 1474568 | tf_op jit(solution)/shard_map/ppermute | solution.py:792
  403.9 16.3 %collective-permute-start.43 = (bf16[320,768]{1,0:T(8,128)(2,1)S(1)}, bf16[320,768]{1,0:T(8,128)(2,1)}, u32[]{:S(2)}, u32[]{:S(2)}) collective-permute-start(bf16[320,768]{1,0:T(8,128)(2,1)S(1)} %get-tuple-element.208), channel_id=1, source_target_pairs={{2,0},{3,1},{4,2},{5,3},{6,4},{7,5},{10,8},{11,9},{12,10},{13,11},... | collective-permute-start | bytes 1474568 | tf_op jit(solution)/shard_map/ppermute | solution.py:792
  (1 other events, 0.8 us)
Sparse Core Ops, SparseCore 0:
  8.9 26.2 all-gather.2
  36.8 26.1 all-gather.4
where the time goes:
time: 436 us; the launch traced here: 431 us
  Pallas kernels  161 us (37%)
  waiting for transfers between devices  143 us (33%)
  starting transfers between devices  68.9 us (16%)
  local copies, waits for them, and re-layouts  28.1 us (6%)
  other arithmetic  15.5 us (4%)
  between operations  14.2 us (3%)
    ppermute x6, waiting for transfers between devices, on_device(): lax.ppermute(up, 'head', up_pairs)  49 us
    pallas_call x2, Pallas kernels, prefix_attention(): pl.pallas_call(functools.partial(prefix_kernel, blocks), out_shape=[jax.S...  47.7 us
    pallas_call x3, Pallas kernels, project(): pl.pallas_call(functools.partial(qkv_kernel, plan, bundle), out_shape=[ou...  45.1 us
    ppermute x9, waiting for transfers between devices, to_chip(): lax.ppermute(x, 'tok', [(t, (t // 2 + shift) % chips * 2 + t % 2) for t i...  29.4 us
    ppermute x6, waiting for transfers between devices, to_side_from(): lax.ppermute(x, 'head', [(h, h ^ 1) for h in range(head_size) if lowest <...  20 us
    pallas_call x2, Pallas kernels, part_by_part(): pl.pallas_call(functools.partial(part_kernel, bundles), out_shape=[jax.Sh...  19.6 us
    ppermute x6, starting transfers between devices, on_device(): lax.ppermute(up, 'head', up_pairs)  15.9 us
    pallas_call x2, Pallas kernels, suffix_attention(): pl.pallas_call(suffix_kernel, out_shape=(jax.ShapeDtypeStruct((rows, GW),...  15.3 us
  transfers between devices with their start and end apart: 46, of which 21 were waited for; matrix products, arithmetic and copies ran while one was open for 7% of the time, Pallas kernels for 35%

commit v1 on v0

--- a/solution.py
+++ b/solution.py
@@ -130,15 +130,10 @@
     rot = HS // 4
     half = rot // 2
     inverse = 10000.0 ** (-(jnp.arange(half, dtype=F32) * 2.0) / rot)
-    angles = positions.astype(F32)[:, None] * inverse[None, :]
-    cosine, sine = jnp.cos(angles), jnp.sin(angles)
-    rows = positions.shape[0]
-    rest = jnp.zeros((rows, HS - rot), F32)
-    none = jnp.zeros((rows, half), F32)
-    straight = jnp.concatenate([cosine, cosine, rest + 1.0], axis=1)
-    upper = jnp.concatenate([-sine, none, rest], axis=1)
-    lower = jnp.concatenate([none, sine, rest], axis=1)
-    return [jnp.tile(table, (1, GROUP_HEADS)) for table in (straight, upper, lower)]
+    lanes = jnp.concatenate([inverse, inverse, jnp.zeros((HS - rot,), F32)])
+    lanes = jnp.tile(lanes, GROUP_HEADS)
+    angles = positions.astype(F32)[:, None] * lanes[None, :]
+    return [jnp.cos(angles), jnp.sin(angles)]
 
 
 def part_kernel(bundles, wide, *outs):
@@ -181,9 +176,9 @@
 def qkv_kernel(pieces, bundle, order, normed, *refs):
     count = 1 + max(part[0] for piece in pieces for part in piece)
     weights = refs[:count]
-    bias, straight, upper, lower = refs[count : count + 4]
-    outs = refs[count + 4 : count + 4 + len(bundle)]
-    total, held_rows, held_weights, row_sems, weight_sems = refs[count + 4 + len(bundle) :]
+    bias, cosine, sine = refs[count : count + 3]
+    outs = refs[count + 3 : count + 3 + len(bundle)]
+    total, held_rows, held_weights, row_sems, weight_sems = refs[count + 3 + len(bundle) :]
     depth = weights[0].shape[0]
 
     def row_copy(j):
@@ -236,11 +231,13 @@
             lanes = slice(spot * GW, (spot + 1) * GW)
             x = total[rows, lanes] + bias[:, lanes]
             if c < 2:
-                x = (
-                    x * straight[rows, :]
-                    + pltpu.roll(x, GW - HS // 8, 1) * upper[rows, :]
-                    + pltpu.roll(x, HS // 8, 1) * lower[rows, :]
+                lane = lax.broadcasted_iota(jnp.int32, x.shape, 1) % HS
+                turned = jnp.where(
+                    lane < HS // 8,
+                    -pltpu.roll(x, GW - HS // 8, 1),
+                    pltpu.roll(x, HS // 8, 1),
                 )
+                x = x * cosine[rows, :] + turned * sine[rows, :]
             outs[spot][rows, :] = x.astype(BF16)
         return carry
 
@@ -266,7 +263,7 @@
         out_shape=[out] * len(bundle),
         in_specs=[pl.BlockSpec(memory_space=pltpu.SMEM)]
         + [anywhere] * (len(arrays) + 1)
-        + [vmem] * 4,
+        + [vmem] * 3,
         out_specs=[vmem] * len(bundle),
         scratch_shapes=[
             pltpu.VMEM((rows, columns), F32),
@@ -283,9 +280,9 @@
 
 def prefix_kernel(blocks, starts, lengths, *refs):
     queries = refs[:blocks]
-    keys, values = refs[blocks : blocks + 2]
-    outs = refs[blocks + 2 : 2 * blocks + 2]
-    totals = refs[2 * blocks + 2]
+    k_own, k_other, v_own, v_other = refs[blocks : blocks + 4]
+    outs = refs[blocks + 4 : 2 * blocks + 4]
+    totals = refs[2 * blocks + 4]
     slot = pl.program_id(0)
     slots = pl.num_programs(0)
     rows = queries[0].shape[0]
@@ -302,71 +299,82 @@
         offset.append(count)
         count = count + size[b]
 
-    def tile(base, height):
-        down = lax.broadcasted_iota(jnp.int32, (height, 1), 0) + base
-        across = lax.broadcasted_iota(jnp.int32, (1, height), 1) + base
-
-        def sources(place, b):
-            within = place - offset[b]
-            return jnp.where((within >= 0) & (within < size[b]), within + begin[b], -1)
-
-        picked = None
-        for b in range(blocks):
-            spread = lax.broadcasted_iota(jnp.int32, (height, rows), 1)
-            one_hot = jnp.where(spread == sources(down, b), 1.0, 0.0).astype(BF16)
-            part = jnp.dot(one_hot, queries[b][...], preferred_element_type=F32)
-            picked = part if picked is None else picked + part
-        picked = picked.astype(BF16)
-        merged = [jnp.zeros((height, 128), F32) for _ in range(GW // 128)]
-        extra = jnp.zeros((height, PACK), F32)
-        place = lax.broadcasted_iota(jnp.int32, (height, PACK), 1)
-        for k, (first, width) in enumerate(windows()):
-            lanes = slice(first, first + width)
-            mask = head_mask(k, first, (height, width))
-            query = jnp.where(mask, picked[:, lanes], jnp.zeros((), BF16))
-            scores = lax.dot_general(
-                query,
-                keys[0, :, lanes],
-                (((1,), (1,)), ((), ())),
-                preferred_element_type=F32,
-            )
-            peak = jnp.max(scores, axis=1, keepdims=True)
-            weights = jnp.exp2((scores - peak) * (SCALE * LOG2E))
-            mass = jnp.sum(weights, axis=1, keepdims=True)
-            blended = jnp.dot(
-                weights.astype(BF16), values[0, :, lanes], preferred_element_type=F32
-            )
-            blended = blended * (1.0 / mass)
-            for w in range(width // 128):
-                at = first // 128 + w
-                cut = slice(w * 128, w * 128 + 128)
-                merged[at] = jnp.where(mask[:, cut], blended[:, cut], merged[at])
-            level = peak * SCALE + jnp.log(mass)
-            high = level.astype(BF16).astype(F32)
-            middle = (level - high).astype(BF16).astype(F32)
-            low = level - high - middle
-            for n, term in enumerate((high, middle, low)):
-                extra = jnp.where(place == 32 * n + k, term, extra)
-        packed = jnp.concatenate(merged + [extra], axis=1).astype(BF16)
-        for b in range(blocks):
-            spread = lax.broadcasted_iota(jnp.int32, (rows, height), 0)
-            one_hot = jnp.where(spread == sources(across, b), 1.0, 0.0).astype(BF16)
-            totals[b] += jnp.dot(one_hot, packed, preferred_element_type=F32)
-
-    large = 256
-    small = 128
-    full = lax.div(count, large)
-    rest = count - full * large
-
-    def body(j, carry):
-        tile(j * large, large)
-        return carry
-
-    lax.fori_loop(0, full + jnp.where(rest > small, 1, 0), body, 0)
-
-    @pl.when((rest > 0) & (rest <= small))
+    def serve(keys, values):
+        def tile(base, height):
+            down = lax.broadcasted_iota(jnp.int32, (height, 1), 0) + base
+            across = lax.broadcasted_iota(jnp.int32, (1, height), 1) + base
+
+            def sources(place, b):
+                within = place - offset[b]
+                return jnp.where((within >= 0) & (within < size[b]), within + begin[b], -1)
+
+            picked = None
+            for b in range(blocks):
+                spread = lax.broadcasted_iota(jnp.int32, (height, rows), 1)
+                one_hot = jnp.where(spread == sources(down, b), 1.0, 0.0).astype(BF16)
+                part = jnp.dot(one_hot, queries[b][...], preferred_element_type=F32)
+                picked = part if picked is None else picked + part
+            picked = picked.astype(BF16)
+            merged = [jnp.zeros((height, 128), F32) for _ in range(GW // 128)]
+            extra = jnp.zeros((height, PACK), F32)
+            place = lax.broadcasted_iota(jnp.int32, (height, PACK), 1)
+            for k, (first, width) in enumerate(windows()):
+                lanes = slice(first, first + width)
+                mask = head_mask(k, first, (height, width))
+                query = jnp.where(mask, picked[:, lanes], jnp.zeros((), BF16))
+                scores = lax.dot_general(
+                    query,
+                    keys[0, :, lanes],
+                    (((1,), (1,)), ((), ())),
+                    preferred_element_type=F32,
+                )
+                peak = jnp.max(scores, axis=1, keepdims=True)
+                weights = jnp.exp2((scores - peak) * (SCALE * LOG2E))
+                mass = jnp.sum(weights, axis=1, keepdims=True)
+                blended = jnp.dot(
+                    weights.astype(BF16), values[0, :, lanes], preferred_element_type=F32
+                )
+                blended = blended * (1.0 / mass)
+                for w in range(width // 128):
+                    at = first // 128 + w
+                    cut = slice(w * 128, w * 128 + 128)
+                    merged[at] = jnp.where(mask[:, cut], blended[:, cut], merged[at])
+                level = peak * SCALE + jnp.log(mass)
+                high = level.astype(BF16).astype(F32)
+                middle = (level - high).astype(BF16).astype(F32)
+                low = level - high - middle
+                for n, term in enumerate((high, middle, low)):
+                    extra = jnp.where(place == 32 * n + k, term, extra)
+            packed = jnp.concatenate(merged + [extra], axis=1).astype(BF16)
+            for b in range(blocks):
+                spread = lax.broadcasted_iota(jnp.int32, (rows, height), 0)
+                one_hot = jnp.where(spread == sources(across, b), 1.0, 0.0).astype(BF16)
+                totals[b] += jnp.dot(one_hot, packed, preferred_element_type=F32)
+
+        large = 256
+        small = 128
+        full = lax.div(count, large)
+        rest = count - full * large
+
+        def body(j, carry):
+            tile(j * large, large)
+            return carry
+
+        lax.fori_loop(0, full + jnp.where(rest > small, 1, 0), body, 0)
+
+        @pl.when((rest > 0) & (rest <= small))
+        def _():
+            tile(full * large, small)
+
+    half = slots // 2
+
+    @pl.when(slot < half)
     def _():
-        tile(full * large, small)
+        serve(k_own, v_own)
+
+    @pl.when(slot >= half)
+    def _():
+        serve(k_other, v_other)
 
     @pl.when(slot == slots - 1)
     def _():
@@ -377,17 +385,20 @@
 def prefix_attention(group, queries, cache, starts, lengths):
     blocks = len(queries)
     rows = queries[0].shape[0]
-    slots, length, _ = cache[0].shape
+    held, length, _ = cache[0].shape
     width = GW + PACK
     whole = lambda s, starts, lengths: (0, 0)
-    block = pl.BlockSpec((1, length, GW), lambda s, starts, lengths: (s, 0, group))
+    own = lambda s, starts, lengths: (jnp.minimum(s, held - 1), 0, group)
+    other = lambda s, starts, lengths: (jnp.maximum(s - held, 0), 0, group)
+    block = (1, length, GW)
     return pl.pallas_call(
         functools.partial(prefix_kernel, blocks),
         out_shape=[jax.ShapeDtypeStruct((rows, width), BF16)] * blocks,
         grid_spec=pltpu.PrefetchScalarGridSpec(
             num_scalar_prefetch=2,
-            grid=(slots,),
-            in_specs=[pl.BlockSpec((rows, GW), whole)] * blocks + [block] * 2,
+            grid=(2 * held,),
+            in_specs=[pl.BlockSpec((rows, GW), whole)] * blocks
+            + [pl.BlockSpec(block, own), pl.BlockSpec(block, other)] * 2,
             out_specs=[pl.BlockSpec((rows, width), whole)] * blocks,
             scratch_shapes=[pltpu.VMEM((blocks, rows, width), F32)],
         ),
@@ -599,12 +610,6 @@
     (first,) = part_by_part(qkv_weight, 0, ((0, 3 * GW),))
     first, layouts = lax.optimization_barrier((first, layouts))
 
-    pairs = [[2 * n, 2 * n + 1] for n in range(chips)]
-    cache = [
-        lax.all_gather(one, "tok", axis=0, tiled=True, axis_index_groups=pairs)
-        for one in (prefix_keys, prefix_values)
-    ]
-
     last = lines - 1
 
     def to_side_from(x, lowest, highest):
@@ -648,7 +653,7 @@
         order += [source, source ^ 1]
     order = jnp.stack(order).astype(jnp.int32)
     source, _ = lax.optimization_barrier((qkv_weight, layouts))
-    cuts = ((0, columns), (0, GW), (GW, 2 * GW), (2 * GW, columns))
+    cuts = ((0, columns), (0, 2 * GW), (2 * GW, columns))
     later = [part_by_part(source, g, cuts) for g in range(1, groups_local)]
     lengths = suffix_len[0]
     starts, row_start, within = shard_layout(lengths, request_order[0], rows)
@@ -663,14 +668,20 @@
                 jnp.sum(one[0][:, None] * slot_match, axis=0),
             ]
         )
-        return lax.dynamic_slice(spans, (0, chip * 2 * held), (2, 2 * held))
+        return jnp.concatenate(
+            [
+                lax.dynamic_slice(spans, (0, tok * held), (2, held)),
+                lax.dynamic_slice(spans, (0, (tok ^ 1) * held), (2, held)),
+            ],
+            axis=1,
+        )
 
     served = jnp.stack([served_spans(one) for one in layouts], axis=2)
     tables = rotary_tables(prefix_length + within)
     bias = qkv_bias.astype(F32).reshape(groups_local, GROUP_HEADS, 3, HS)
     bias = jnp.transpose(bias, (0, 2, 1, 3)).reshape(groups_local, 1, columns)
     bias = [
-        [bias[g]] if g == 0 else [bias[g][:, :GW], bias[g][:, GW:]]
+        [bias[g]] if g == 0 else [bias[g][:, : 2 * GW], bias[g][:, 2 * GW :]]
         for g in range(groups_local)
     ]
 
@@ -722,43 +733,40 @@
     coming = [send(after(one[1], arriving)) for one in later]
     first_pieces = pieces_of((first, to_core(first)), [crossing(arriving)], 0, columns)
     normed = layer_norm(blocks, places, norm_gain, norm_bias)
-    settled = (normed, coming)
-    normed = after(normed, coming)
-    landed = to_side(after(outgoing, settled))
-    own = [(one[0], to_core(after(one[0], arriving))) for one in later]
-    keys_coming = [send(after(one[2], settled)) for one in later]
+    landed = to_side(after(outgoing, normed))
+    cache = [prefix_keys, to_core(after(prefix_keys, arriving))]
+    cache += [prefix_values, to_core(after(prefix_values, arriving))]
+    own = [(one[0], to_core(after(one[0], normed))) for one in later]
     heads = [project(normed, first_pieces, order, bias[0][0], tables, (0, 1, 2))]
     asked = [exchange(heads[0][0])]
-    settled = heads[0]
+    suffixes = [suffix_attention(row_start, *heads[0])]
+    settled = suffixes[0]
     for g in range(1, groups_local):
-        arrived = crossing(after(coming[g - 1], settled, keys_coming))
-        (queries,) = project(
-            normed, pieces_of(own[g - 1], [arrived], 0, GW), order, bias[g][0], tables, (0,)
-        )
-        asked.append(exchange(queries))
-        settled = queries
-    suffixes = [suffix_attention(after(row_start, settled), *heads[0])]
-    values_coming = [send(after(one[3], asked[1][1:])) for one in later]
-    asked[0] = after(asked[0], suffixes[0])
+        arrived = crossing(after(coming[g - 1], settled))
+        pair = project(
+            normed, pieces_of(own[g - 1], [arrived], 0, 2 * GW), order, bias[g][0], tables, (0, 1)
+        )
+        heads.append(pair)
+        asked.append(exchange(pair[0]))
+        settled = pair
+    values_coming = [send(after(one[2], coming)) for one in later]
+    asked[0] = after(asked[0], settled)
     returned = []
     for g in range(groups_local):
         if g > 0:
             asked[g] = after(asked[g], answers)
         answers = prefix_attention(g, asked[g], cache, span_start, span_length)
         returned.append([answers[0]] + [to_chip(answers[s], chips - s) for s in range(1, chips)])
-    crossed = to_core(after(landed, returned[0][1:]))
+    crossed = to_core(after(landed, answers))
     for g in range(1, groups_local):
-        arrived = [
-            crossing(keys_coming[g - 1]),
-            crossing(after(values_coming[g - 1], answers, returned[0])),
-        ]
-        keys, values = project(
-            normed, pieces_of(own[g - 1], arrived, GW, 2 * GW), order, bias[g][1], tables, (1, 2)
-        )
-        suffixes.append(suffix_attention(row_start, asked[g][0], keys, values))
+        arrived = crossing(after(values_coming[g - 1], answers))
+        (values,) = project(
+            normed, pieces_of(own[g - 1], [arrived], 2 * GW, GW), order, bias[g][1], tables, (2,)
+        )
+        suffixes.append(suffix_attention(row_start, heads[g][0], heads[g][1], values))
     attention_own, attention_side = [], []
     for g in range(groups_local):
-        attention = merge(returned[g], *suffixes[g])
+        attention = merge(after(returned[g], suffixes[-1]), *suffixes[g])
         attention_own.append(attention)
         attention_side.append(to_side(attention))
     partial = output_projection(

time: 436 us -> 410 us (0.940)
  the two profiles are of different devices: /device:TPU:14 before, /device:TPU:8 now
where the time goes in v1:
time: 410 us; the launch traced here: 407 us
  Pallas kernels  164 us (40%)
  waiting for transfers between devices  119 us (29%)
  starting transfers between devices  86.6 us (21%)
  other arithmetic  20.6 us (5%)
  local copies, waits for them, and re-layouts  15.9 us (4%)
    pallas_call x2, Pallas kernels, prefix_attention(): pl.pallas_call(functools.partial(prefix_kernel, blocks), out_shape=[jax.S...  51.9 us
    pallas_call x3, Pallas kernels, project(): pl.pallas_call(functools.partial(qkv_kernel, plan, bundle), out_shape=[ou...  43.4 us
    ppermute x6, waiting for transfers between devices, on_device(): lax.ppermute(up, 'head', up_pairs)  32.8 us
    ppermute x6, starting transfers between devices, on_device(): lax.ppermute(up, 'head', up_pairs)  31.7 us
    ppermute x6, waiting for transfers between devices, to_side_from(): lax.ppermute(x, 'head', [(h, h ^ 1) for h in range(head_size) if lowest <...  22.7 us
    pallas_call x2, Pallas kernels, part_by_part(): pl.pallas_call(functools.partial(part_kernel, bundles), out_shape=[jax.Sh...  19.4 us
    ppermute x4, waiting for transfers between devices, to_side(): return lax.ppermute(x, 'head', [(h, h ^ 1) for h in range(head_size)])  16.6 us
    pallas_call x2, Pallas kernels, suffix_attention(): pl.pallas_call(suffix_kernel, out_shape=(jax.ShapeDtypeStruct((rows, GW),...  15.3 us
  transfers between devices with their start and end apart: 44, of which 23 were waited for; matrix products, arithmetic and copies ran while one was open for 5% of the time, Pallas kernels for 37%

profile of v1, /device:TPU:8, one launch (start us, length us, event | category | flops | bytes accessed | tf_op | source)
XLA Modules:
  0.0 406.6 jit_solution(12515069224614121795)
XLA Ops:
  0.0 3.5 collective-permute-start.2
  3.5 2.4 collective-permute-start.3
  5.9 1.6 collective-permute-start.4
  8.1 1.5 collective-permute-start
  11.9 9.4 %parts.2.refs_0_ = bf16[1536,1152]{1,0:T(8,128)(2,1)} custom-call(bf16[1536,2304]{1,0:T(8,128)(2,1)} %wide.2), custom_call_target="tpu_custom_call" | custom-call | flops 1000 | bytes 1000 | tf_op jit(solution)/shard_map/parts/pallas_call | solution.py:164
  22.1 3.5 collective-permute-done.2.refs_2_
  25.6 3.3 collective-permute-done.3.refs_4_
  29.1 4.4 %collective-permute-start.5 = (bf16[640,768]{1,0:T(8,128)(2,1)S(1)}, bf16[640,768]{1,0:T(8,128)(2,1)}, u32[]{:S(2)}, u32[]{:S(2)}) collective-permute-start(bf16[640,768]{1,0:T(8,128)(2,1)S(1)} %collective-permute-done.2.refs_2_), channel_id=1, source_target_pairs={{2,4},{3,5},{4,6},{5,7},{10,12},{11,13},{12,14},{13,15},{18,20},{1... | collective-permute-start | bytes 2949128 | tf_op jit(solution)/shard_map/ppermute | solution.py:630
  33.6 1.9 collective-permute-start.6
  35.5 3.4 collective-permute-start.7
  38.9 2.4 collective-permute-start.8
  43.3 1.8 constant_dynamic-slice_fusion.1
  45.1 4.6 %multiply_sine_fusion = (f32[640,384]{1,0:T(8,128)}, f32[640,384]{1,0:T(8,128)}) fusion(f32[384]{0:T(512)S(1)} %mul.191, f32[640]{0:T(1024)S(1)} %add_convert_fusion), kind=kLoop, calls=%fused_computation.2 | loop fusion | flops 245760 | bytes 1970176 | tf_op jit(solution)/shard_map/sin | solution.py:136
  49.7 2.5 collective-permute-done.5.refs_6_
  52.2 5.4 %collective-permute-done.6.refs_8_ = bf16[640,768]{1,0:T(8,128)(2,1)} collective-permute-done((bf16[640,768]{1,0:T(8,128)(2,1)}, bf16[640,768]{1,0:T(8,128)(2,1)}, u32[]{:S(2)}, u32[]{:S(2)}) %collective-permute-start.6) | collective-permute-done | bytes 983072 | tf_op jit(solution)/shard_map/ppermute | solution.py:633
  57.6 4.5 %collective-permute-done.7.refs_3_ = bf16[640,768]{1,0:T(8,128)(2,1)} collective-permute-done((bf16[640,768]{1,0:T(8,128)(2,1)S(1)}, bf16[640,768]{1,0:T(8,128)(2,1)}, u32[]{:S(2)}, u32[]{:S(2)}) %collective-permute-start.7) | collective-permute-done | bytes 983072 | tf_op jit(solution)/shard_map/ppermute | solution.py:616
  62.9 2.2 collective-permute-start.13
  65.1 3.4 collective-permute-start.10
  69.9 1.6 pad_maximum_fusion
  71.5 10.0 %parts.3 = (bf16[1536,1152]{1,0:T(8,128)(2,1)}, bf16[1536,768]{1,0:T(8,128)(2,1)}, bf16[1536,384]{1,0:T(8,128)(2,1)}) custom-call(bf16[1536,2304]{1,0:T(8,128)(2,1)} %wide.2), custom_call_target="tpu_custom_call" | custom-call | flops 1000 | bytes 1000 | tf_op jit(solution)/shard_map/parts/pallas_call | solution.py:164
  81.5 1.7 collective-permute-done.8.refs_5_
  85.0 16.5 %collective-permute-done.10.refs_9_ = bf16[640,768]{1,0:T(8,128)(2,1)} collective-permute-done((bf16[640,768]{1,0:T(8,128)(2,1)}, bf16[640,768]{1,0:T(8,128)(2,1)}, u32[]{:S(2)}, u32[]{:S(2)}) %collective-permute-start.10) | collective-permute-done | bytes 983072 | tf_op jit(solution)/shard_map/ppermute | solution.py:616
  101.5 1.9 collective-permute-start.14
  107.6 14.5 %norm.1.normed = bf16[640,6144]{1,0:T(8,128)(2,1)} custom-call(s32[14]{0:T(128)} %stack.131.places, bf16[640,768]{1,0:T(8,128)(2,1)} %refs_0_, bf16[640,768]{1,0:T(8,128)(2,1)} %copy-done.8, bf16[640,768]{1,0:T(8,128)(2,1)} %copy-done.7, bf16[640,768]{1,0:T(8,128)(2,1)} %collective-permute-done.7.refs_3_, bf16[640,768]{1,0:T(8,128)(2,1)} %collective-permute-done.3.refs_4_, ...), custom_call_target="tpu_custom_call" | custom-call | flops 1000 | bytes 1000 | tf_op jit(solution)/shard_map/norm/pallas_call | solution.py:95
  123.3 19.6 %project.3 = (bf16[640,384]{1,0:T(8,128)(2,1)}, bf16[640,384]{1,0:T(8,128)(2,1)}, bf16[640,384]{1,0:T(8,128)(2,1)}) custom-call(s32[4]{0:T(128)} %pad_add_fusion.4.order, bf16[640,6144]{1,0:T(8,128)(2,1)} %norm.1.normed, bf16[1536,1152]{1,0:T(8,128)(2,1)} %parts.2.refs_0_, bf16[1536,1152]{1,0:T(8,128)(2,1)} %collective-permute-done.15.refs_1_, ...), custom_call_target="tpu_custom_call" | custom-call | flops 1000 | bytes 1000 | tf_op jit(solution)/shard_map/project/pallas_call | solution.py:261
  143.0 7.6 %suffix.2 = (f32[640,384]{1,0:T(8,128)}, f32[640,128]{1,0:T(8,128)}) custom-call(s32[640,1]{1,0:T(8,128)} %copy.25.row_start, bf16[640,384]{1,0:T(8,128)(2,1)} %get-tuple-element.160.queries.refs_0_, bf16[640,384]{1,0:T(8,128)(2,1)} %get-tuple-element.152.keys, bf16[640,384]{1,0:T(8,128)(2,1)} %get-tuple-element.153.values), custom_call_target="tpu_custom_call" | custom-call | flops 1000 | bytes 1000 | tf_op jit(solution)/shard_map/suffix/pallas_call | solution.py:452
  150.6 9.4 %collective-permute-done.19.refs_2_ = bf16[1536,768]{1,0:T(8,128)(2,1)} collective-permute-done((bf16[1536,768]{1,0:T(8,128)(2,1)}, bf16[1536,768]{1,0:T(8,128)(2,1)}, u32[]{:S(2)}, u32[]{:S(2)}) %collective-permute-start.19) | collective-permute-done | bytes 2359328 | tf_op jit(solution)/shard_map/ppermute | solution.py:596
  161.5 1.5 collective-permute-start.17
  163.0 1.7 collective-permute-done.20.refs_3_
  164.8 1.5 collective-permute-start.24
  166.3 14.2 %project.4 = (bf16[640,384]{1,0:T(8,128)(2,1)}, bf16[640,384]{1,0:T(8,128)(2,1)}) custom-call(s32[4]{0:T(128)} %pad_add_fusion.4.order, bf16[640,6144]{1,0:T(8,128)(2,1)} %norm.1.normed, bf16[1536,1152]{1,0:T(8,128)(2,1)} %get-tuple-element.148.refs_0_, bf16[1536,1152]{1,0:T(8,128)(2,1)} %collective-permute-done.18.refs_1_, ...), custom_call_target="tpu_custom_call" | custom-call | flops 1000 | bytes 1000 | tf_op jit(solution)/shard_map/project/pallas_call | solution.py:261
  180.5 1.5 collective-permute-start.25
  182.0 25.7 %prefix.2 = (bf16[640,512]{1,0:T(8,128)(2,1)}, bf16[640,512]{1,0:T(8,128)(2,1)}) custom-call(s32[8]{0:T(128)} %reshape_squeeze.6.starts, s32[8]{0:T(128)} %reshape_squeeze.7.lengths, bf16[640,384]{1,0:T(8,128)(2,1)} %get-tuple-element.160.queries.refs_0_, bf16[640,384]{1,0:T(8,128)(2,1)} %copy-done.14, bf16[2,2048,768]{2,1,0:T(8,128)(2,1)} %refs_2_.3, ...), custom_call_target="tpu_custom_call" | custom-call | flops 1000 | bytes 1000 | tf_op jit(solution)/shard_map/prefix/pallas_call | solution.py:394
  207.8 3.1 collective-permute-done.25.refs_1_
  211.7 26.2 %prefix.3 = (bf16[640,512]{1,0:T(8,128)(2,1)}, bf16[640,512]{1,0:T(8,128)(2,1)}) custom-call(s32[8]{0:T(128)} %reshape_squeeze.6.starts, s32[8]{0:T(128)} %reshape_squeeze.7.lengths, bf16[640,384]{1,0:T(8,128)(2,1)} %get-tuple-element.168.refs_0_.queries, bf16[640,384]{1,0:T(8,128)(2,1)} %copy-done.15, bf16[2,2048,768]{2,1,0:T(8,128)(2,1)} %refs_2_.3, ...), custom_call_target="tpu_custom_call" | custom-call | flops 1000 | bytes 1000 | tf_op jit(solution)/shard_map/prefix/pallas_call | solution.py:394
  238.5 2.0 collective-permute-start.23
  240.5 3.3 collective-permute-done.26.refs_3_
  244.9 9.6 %project.5.values = bf16[640,384]{1,0:T(8,128)(2,1)} custom-call(s32[4]{0:T(128)} %pad_add_fusion.4.order, bf16[640,6144]{1,0:T(8,128)(2,1)} %norm.1.normed, bf16[1536,1152]{1,0:T(8,128)(2,1)} %get-tuple-element.148.refs_0_, bf16[1536,1152]{1,0:T(8,128)(2,1)} %collective-permute-done.18.refs_1_, bf16[1536,384]{1,0:T(8,128)(2,1)} %copy-done.5, ...), custom_call_target="tpu_custom_call" | custom-call | flops 1000 | bytes 1000 | tf_op jit(solution)/shard_map/project/pallas_call | solution.py:261
  254.5 7.7 %suffix.3 = (f32[640,384]{1,0:T(8,128)}, f32[640,128]{1,0:T(8,128)}) custom-call(s32[640,1]{1,0:T(8,128)} %copy.25.row_start, bf16[640,384]{1,0:T(8,128)(2,1)} %get-tuple-element.168.refs_0_.queries, bf16[640,384]{1,0:T(8,128)(2,1)} %get-tuple-element.159.keys, bf16[640,384]{1,0:T(8,128)(2,1)} %project.5.values), custom_call_target="tpu_custom_call" | custom-call | flops 1000 | bytes 1000 | tf_op jit(solution)/shard_map/suffix/pallas_call | solution.py:452
  263.0 3.6 merge.3.refs_1_
  267.2 2.3 collective-permute-done.23.refs_1_
  270.3 3.7 merge.2.refs_0_
  274.5 6.4 %collective-permute-done.29.refs_3_ = bf16[640,384]{1,0:T(8,128)(2,1)S(1)} collective-permute-done((bf16[640,384]{1,0:T(8,128)(2,1)}, bf16[640,384]{1,0:T(8,128)(2,1)S(1)}, u32[]{:S(2)}, u32[]{:S(2)}) %collective-permute-start.29) | collective-permute-done | bytes 491552 | tf_op jit(solution)/shard_map/ppermute | solution.py:603
  280.9 10.0 %collective-permute-done.28.refs_2_ = bf16[640,384]{1,0:T(8,128)(2,1)S(1)} collective-permute-done((bf16[640,384]{1,0:T(8,128)(2,1)}, bf16[640,384]{1,0:T(8,128)(2,1)S(1)}, u32[]{:S(2)}, u32[]{:S(2)}) %collective-permute-start.28) | collective-permute-done | bytes 491552 | tf_op jit(solution)/shard_map/ppermute | solution.py:603
  293.2 12.0 %output.1 = f32[4,640,768]{2,1,0:T(8,128)} custom-call(s32[2]{0:T(128)} %pad_add_fusion.5.place, bf16[640,384]{1,0:T(8,128)(2,1)} %merge.2.refs_0_, bf16[640,384]{1,0:T(8,128)(2,1)} %merge.3.refs_1_, bf16[640,384]{1,0:T(8,128)(2,1)} %copy-done.17, bf16[640,384]{1,0:T(8,128)(2,1)} %copy-done.16, bf16[768,6144]{1,0:T(8,128)(2,1)} %refs_4_.5, ...), custom_call_target="tpu_custom_call" | custom-call | flops 1000 | bytes 1000 | tf_op jit(solution)/shard_map/output/pallas_call | solution.py:545
  305.2 2.3 fusion.13
  312.3 11.2 %collective-permute-done.32 = bf16[320,768]{1,0:T(8,128)(2,1)S(1)} collective-permute-done((bf16[320,768]{1,0:T(8,128)(2,1)S(1)}, bf16[320,768]{1,0:T(8,128)(2,1)S(1)}, u32[]{:S(2)}, u32[]{:S(2)}) %collective-permute-start.32) | collective-permute-done | bytes 491552 | tf_op jit(solution)/shard_map/ppermute | solution.py:800
  323.5 2.6 fusion.8
  326.1 19.6 %collective-permute-start.34 = (bf16[320,768]{1,0:T(8,128)(2,1)}, bf16[320,768]{1,0:T(8,128)(2,1)S(1)}, u32[]{:S(2)}, u32[]{:S(2)}) collective-permute-start(bf16[320,768]{1,0:T(8,128)(2,1)} %get-tuple-element.187), channel_id=1, source_target_pairs={{0,2},{1,3},{2,4},{3,5},{8,10},{9,11},{10,12},{11,13},{16,18},{17,... | collective-permute-start | bytes 1474568 | tf_op jit(solution)/shard_map/ppermute | solution.py:800
  347.0 10.2 %collective-permute-done.34 = bf16[320,768]{1,0:T(8,128)(2,1)S(1)} collective-permute-done((bf16[320,768]{1,0:T(8,128)(2,1)}, bf16[320,768]{1,0:T(8,128)(2,1)S(1)}, u32[]{:S(2)}, u32[]{:S(2)}) %collective-permute-start.34) | collective-permute-done | bytes 491552 | tf_op jit(solution)/shard_map/ppermute | solution.py:800
  357.2 3.9 collective-permute-done.35
  361.2 2.7 fusion.7
  363.8 3.1 collective-permute-start.40
  368.3 4.6 %collective-permute-start.36 = (bf16[320,768]{1,0:T(8,128)(2,1)S(1)}, bf16[320,768]{1,0:T(8,128)(2,1)S(1)}, u32[]{:S(2)}, u32[]{:S(2)}) collective-permute-start(bf16[320,768]{1,0:T(8,128)(2,1)S(1)} %get-tuple-element.191), channel_id=1, source_target_pairs={{0,2},{1,3},{2,4},{3,5},{4,6},{5,7},{8,10},{9,11},{10,12},{11,13},... | collective-permute-start | bytes 1474568 | tf_op jit(solution)/shard_map/ppermute | solution.py:800
  372.8 1.9 collective-permute-start.37
  374.8 5.3 %collective-permute-done.40 = bf16[320,768]{1,0:T(8,128)(2,1)S(1)} collective-permute-done((bf16[320,768]{1,0:T(8,128)(2,1)S(1)}, bf16[320,768]{1,0:T(8,128)(2,1)S(1)}, u32[]{:S(2)}, u32[]{:S(2)}) %collective-permute-start.40) | collective-permute-done | bytes 491552 | tf_op jit(solution)/shard_map/ppermute | solution.py:800
  380.0 2.9 collective-permute-done.41
  383.0 1.8 fusion.2
  384.7 1.9 collective-permute-start.42
  386.7 4.7 %collective-permute-start.43 = (bf16[320,768]{1,0:T(8,128)(2,1)S(1)}, bf16[320,768]{1,0:T(8,128)(2,1)}, u32[]{:S(2)}, u32[]{:S(2)}) collective-permute-start(bf16[320,768]{1,0:T(8,128)(2,1)S(1)} %get-tuple-element.208), channel_id=1, source_target_pairs={{2,0},{3,1},{4,2},{5,3},{6,4},{7,5},{10,8},{11,9},{12,10},{13,11},... | collective-permute-start | bytes 1474568 | tf_op jit(solution)/shard_map/ppermute | solution.py:800
  391.6 2.0 collective-permute-done.37
  393.6 6.1 %collective-permute-done.42 = bf16[320,768]{1,0:T(8,128)(2,1)} collective-permute-done((bf16[320,768]{1,0:T(8,128)(2,1)S(1)}, bf16[320,768]{1,0:T(8,128)(2,1)}, u32[]{:S(2)}, u32[]{:S(2)}) %collective-permute-start.42) | collective-permute-done | bytes 491552 | tf_op jit(solution)/shard_map/ppermute | solution.py:800
  399.7 3.3 collective-permute-done.43
  403.0 2.4 fusion.1
  (131 shorter events, 32.5 us)
Async XLA Ops:
  0.0 25.6 %collective-permute-start.2 = (bf16[640,768]{1,0:T(8,128)(2,1)}, bf16[640,768]{1,0:T(8,128)(2,1)S(1)}, u32[]{:S(2)}, u32[]{:S(2)}) collective-permute-start(bf16[640,768]{1,0:T(8,128)(2,1)} %refs_0_), channel_id=1, source_target_pairs={{0,2},{1,3},{2,4},{3,5},{4,6},{5,7},{8,10},{9,11},{10,12},{11,13},... | collective-permute-start | bytes 2949128 | tf_op jit(solution)/shard_map/ppermute | solution.py:630
  3.5 25.4 %collective-permute-start.3 = (bf16[640,768]{1,0:T(8,128)(2,1)}, bf16[640,768]{1,0:T(8,128)(2,1)}, u32[]{:S(2)}, u32[]{:S(2)}) collective-permute-start(bf16[640,768]{1,0:T(8,128)(2,1)} %refs_0_), channel_id=1, source_target_pairs={{2,0},{3,1},{4,2},{5,3},{6,4},{7,5},{10,8},{11,9},{12,10},{13,11},... | collective-permute-start | bytes 2949128 | tf_op jit(solution)/shard_map/ppermute | solution.py:633
  5.9 23.2 %collective-permute-start.4 = (bf16[640,768]{1,0:T(8,128)(2,1)}, bf16[640,768]{1,0:T(8,128)(2,1)S(1)}, u32[]{:S(2)}, u32[]{:S(2)}) collective-permute-start(bf16[640,768]{1,0:T(8,128)(2,1)} %refs_0_), channel_id=1, source_target_pairs={{0,1},{1,0},{2,3},{3,2},{4,5},{5,4},{6,7},{7,6},{8,9},{9,8},{10,11... | collective-permute-start | bytes 2949128 | tf_op jit(solution)/shard_map/ppermute | solution.py:603
  8.1 13.1 %collective-permute-start = (s32[2,8]{1,0:T(2,128)S(1)}, s32[2,8]{1,0:T(2,128)S(1)}, u32[]{:S(2)}, u32[]{:S(2)}) collective-permute-start(s32[2,8]{1,0:T(2,128)S(1)} %pad_add_fusion.1), channel_id=1, source_target_pairs={{0,16},{8,24},{16,0},{24,8},{1,17},{9,25},{17,1},{25,9},{2,18},{10... | collective-permute-start | bytes 200 | tf_op jit(solution)/shard_map/ppermute | solution.py:596
  11.9 9.9 %copy-start.19 = (s32[1,8]{1,0:T(1,128)S(1)}, s32[1,8]{1,0:T(1,128)}, u32[]{:S(2)}) copy-start(s32[1,8]{1,0:T(1,128)} %param.21) | copy-start | bytes 100
  21.2 84.2 %collective-permute-start.1 = (bf16[1536,1152]{1,0:T(8,128)(2,1)}, bf16[1536,1152]{1,0:T(8,128)(2,1)}, u32[]{:S(2)}, u32[]{:S(2)}) collective-permute-start(bf16[1536,1152]{1,0:T(8,128)(2,1)} %parts.2.refs_0_), channel_id=1, source_target_pairs={{0,16},{8,24},{16,0},{24,8},{1,17},{9,25},{17,1},{25,9},{2,18},{10... | collective-permute-start | bytes 10616840 | tf_op jit(solution)/shard_map/ppermute | solution.py:596
  25.6 19.5 %copy-start.7 = (bf16[640,768]{1,0:T(8,128)(2,1)}, bf16[640,768]{1,0:T(8,128)(2,1)S(1)}, u32[]{:S(2)}) copy-start(bf16[640,768]{1,0:T(8,128)(2,1)S(1)} %collective-permute-done.2.refs_2_) | copy-start | bytes 2949124
  29.1 14.2 %copy-start.8 = (bf16[640,768]{1,0:T(8,128)(2,1)}, bf16[640,768]{1,0:T(8,128)(2,1)S(1)}, u32[]{:S(2)}) copy-start(bf16[640,768]{1,0:T(8,128)(2,1)S(1)} %collective-permute-done.4.refs_1_) | copy-start | bytes 2949124
  29.1 23.1 %collective-permute-start.5 = (bf16[640,768]{1,0:T(8,128)(2,1)S(1)}, bf16[640,768]{1,0:T(8,128)(2,1)}, u32[]{:S(2)}, u32[]{:S(2)}) collective-permute-start(bf16[640,768]{1,0:T(8,128)(2,1)S(1)} %collective-permute-done.2.refs_2_), channel_id=1, source_target_pairs={{2,4},{3,5},{4,6},{5,7},{10,12},{11,13},{12,14},{13,15},{18,20},{1... | collective-permute-start | bytes 2949128 | tf_op jit(solution)/shard_map/ppermute | solution.py:630
  33.6 24.1 %collective-permute-start.6 = (bf16[640,768]{1,0:T(8,128)(2,1)}, bf16[640,768]{1,0:T(8,128)(2,1)}, u32[]{:S(2)}, u32[]{:S(2)}) collective-permute-start(bf16[640,768]{1,0:T(8,128)(2,1)} %collective-permute-done.3.refs_4_), channel_id=1, source_target_pairs={{2,0},{3,1},{4,2},{5,3},{10,8},{11,9},{12,10},{13,11},{18,16},{19,... | collective-permute-start | bytes 2949128 | tf_op jit(solution)/shard_map/ppermute | solution.py:633
  35.5 26.7 %collective-permute-start.7 = (bf16[640,768]{1,0:T(8,128)(2,1)S(1)}, bf16[640,768]{1,0:T(8,128)(2,1)}, u32[]{:S(2)}, u32[]{:S(2)}) collective-permute-start(bf16[640,768]{1,0:T(8,128)(2,1)S(1)} %collective-permute-done.2.refs_2_), channel_id=1, source_target_pairs={{2,3},{3,2},{4,5},{5,4},{6,7},{7,6},{10,11},{11,10},{12,13},{13,12... | collective-permute-start | bytes 2949128 | tf_op jit(solution)/shard_map/ppermute | solution.py:616
  38.9 44.3 %collective-permute-start.8 = (bf16[640,768]{1,0:T(8,128)(2,1)}, bf16[640,768]{1,0:T(8,128)(2,1)}, u32[]{:S(2)}, u32[]{:S(2)}) collective-permute-start(bf16[640,768]{1,0:T(8,128)(2,1)} %collective-permute-done.3.refs_4_), channel_id=1, source_target_pairs={{0,1},{1,0},{2,3},{3,2},{4,5},{5,4},{8,9},{9,8},{10,11},{11,10},{1... | collective-permute-start | bytes 2949128 | tf_op jit(solution)/shard_map/ppermute | solution.py:616
  62.2 21.4 %collective-permute-start.11 = (bf16[640,768]{1,0:T(8,128)(2,1)}, bf16[640,768]{1,0:T(8,128)(2,1)S(1)}, u32[]{:S(2)}, u32[]{:S(2)}) collective-permute-start(bf16[640,768]{1,0:T(8,128)(2,1)} %collective-permute-done.5.refs_6_), channel_id=1, source_target_pairs={{4,6},{5,7},{12,14},{13,15},{20,22},{21,23},{28,30},{29,31}} | collective-permute-start | bytes 2949128 | tf_op jit(solution)/shard_map/ppermute | solution.py:630
  62.9 21.4 %collective-permute-start.13 = (bf16[640,768]{1,0:T(8,128)(2,1)}, bf16[640,768]{1,0:T(8,128)(2,1)}, u32[]{:S(2)}, u32[]{:S(2)}) collective-permute-start(bf16[640,768]{1,0:T(8,128)(2,1)} %collective-permute-done.6.refs_8_), channel_id=1, source_target_pairs={{2,0},{3,1},{10,8},{11,9},{18,16},{19,17},{26,24},{27,25}} | collective-permute-start | bytes 2949128 | tf_op jit(solution)/shard_map/ppermute | solution.py:633
  65.1 36.4 %collective-permute-start.10 = (bf16[640,768]{1,0:T(8,128)(2,1)}, bf16[640,768]{1,0:T(8,128)(2,1)}, u32[]{:S(2)}, u32[]{:S(2)}) collective-permute-start(bf16[640,768]{1,0:T(8,128)(2,1)} %collective-permute-done.6.refs_8_), channel_id=1, source_target_pairs={{0,1},{1,0},{2,3},{3,2},{8,9},{9,8},{10,11},{11,10},{16,17},{17,16... | collective-permute-start | bytes 2949128 | tf_op jit(solution)/shard_map/ppermute | solution.py:616
  71.5 31.9 %copy-start.20 = (s32[8]{0:T(128)S(1)}, s32[8]{0:T(128)}, u32[]{:S(2)}) copy-start(s32[8]{0:T(128)} %param.23) | copy-start | bytes 100
  83.2 38.9 %collective-permute-start.15 = (bf16[1536,1152]{1,0:T(8,128)(2,1)}, bf16[1536,1152]{1,0:T(8,128)(2,1)}, u32[]{:S(2)}, u32[]{:S(2)}) collective-permute-start(bf16[1536,1152]{1,0:T(8,128)(2,1)} %parts.2.refs_0_), channel_id=1, source_target_pairs={{0,8},{8,0},{16,24},{24,16},{1,9},{9,1},{17,25},{25,17},{2,10},{10... | collective-permute-start | bytes 10616840 | tf_op jit(solution)/shard_map/ppermute | solution.py:593
  83.5 24.1 %copy-start.9 = (bf16[640,768]{1,0:T(8,128)(2,1)}, bf16[640,768]{1,0:T(8,128)(2,1)S(1)}, u32[]{:S(2)}) copy-start(bf16[640,768]{1,0:T(8,128)(2,1)S(1)} %collective-permute-done.11.refs_10_) | copy-start | bytes 2949124
  83.5 21.9 %collective-permute-start.9 = (bf16[640,768]{1,0:T(8,128)(2,1)}, bf16[640,768]{1,0:T(8,128)(2,1)S(1)}, u32[]{:S(2)}, u32[]{:S(2)}) collective-permute-start(bf16[640,768]{1,0:T(8,128)(2,1)} %collective-permute-done.5.refs_6_), channel_id=1, source_target_pairs={{4,5},{5,4},{6,7},{7,6},{12,13},{13,12},{14,15},{15,14},{20,21},{2... | collective-permute-start | bytes 2949128 | tf_op jit(solution)/shard_map/ppermute | solution.py:616
  84.3 21.2 %collective-permute-start.12 = (bf16[640,768]{1,0:T(8,128)(2,1)S(1)}, bf16[640,768]{1,0:T(8,128)(2,1)S(1)}, u32[]{:S(2)}, u32[]{:S(2)}) collective-permute-start(bf16[640,768]{1,0:T(8,128)(2,1)S(1)} %collective-permute-done.11.refs_10_), channel_id=1, source_target_pairs={{6,7},{7,6},{14,15},{15,14},{22,23},{23,22},{30,31},{31,30}} | collective-permute-start | bytes 2949128 | tf_op jit(solution)/shard_map/ppermute | solution.py:616
  101.5 4.0 collective-permute-start.14
  105.4 2.2 copy-start.10
  105.4 2.2 copy-start.11
  105.5 17.9 %collective-permute-start.16 = (bf16[1536,1152]{1,0:T(8,128)(2,1)}, bf16[1536,1152]{1,0:T(8,128)(2,1)}, u32[]{:S(2)}, u32[]{:S(2)}) collective-permute-start(bf16[1536,1152]{1,0:T(8,128)(2,1)} %collective-permute-done.1.refs_2_), channel_id=1, source_target_pairs={{0,8},{8,0},{16,24},{24,16},{1,9},{9,1},{17,25},{25,17},{2,10},{10... | collective-permute-start | bytes 10616840 | tf_op jit(solution)/shard_map/ppermute | solution.py:593
  105.5 76.5 %collective-permute-start.21 = (bf16[2,2048,768]{2,1,0:T(8,128)(2,1)}, bf16[2,2048,768]{2,1,0:T(8,128)(2,1)}, u32[]{:S(2)}, u32[]{:S(2)}) collective-permute-start(bf16[2,2048,768]{2,1,0:T(8,128)(2,1)} %refs_2_.3), channel_id=1, source_target_pairs={{0,8},{8,0},{16,24},{24,16},{1,9},{9,1},{17,25},{25,17},{2,10},{10... | collective-permute-start | bytes 18874376 | tf_op jit(solution)/shard_map/ppermute | solution.py:593
  106.0 76.0 %collective-permute-start.22 = (bf16[2,2048,768]{2,1,0:T(8,128)(2,1)}, bf16[2,2048,768]{2,1,0:T(8,128)(2,1)}, u32[]{:S(2)}, u32[]{:S(2)}) collective-permute-start(bf16[2,2048,768]{2,1,0:T(8,128)(2,1)} %refs_4_.4), channel_id=1, source_target_pairs={{0,8},{8,0},{16,24},{24,16},{1,9},{9,1},{17,25},{25,17},{2,10},{10... | collective-permute-start | bytes 18874376 | tf_op jit(solution)/shard_map/ppermute | solution.py:593
  106.1 53.9 %collective-permute-start.19 = (bf16[1536,768]{1,0:T(8,128)(2,1)}, bf16[1536,768]{1,0:T(8,128)(2,1)}, u32[]{:S(2)}, u32[]{:S(2)}) collective-permute-start(bf16[1536,768]{1,0:T(8,128)(2,1)} %get-tuple-element.150), channel_id=1, source_target_pairs={{0,16},{8,24},{16,0},{24,8},{1,17},{9,25},{17,1},{25,9},{2,18},{10... | collective-permute-start | bytes 7077896 | tf_op jit(solution)/shard_map/ppermute | solution.py:596
  107.6 14.5 %copy-start = (bf16[1536,1152]{1,0:T(8,128)(2,1)S(1)}, bf16[1536,1152]{1,0:T(8,128)(2,1)}, u32[]{:S(2)}) copy-start(bf16[1536,1152]{1,0:T(8,128)(2,1)} %get-tuple-element.148.refs_0_) | copy-start | bytes 10616836
  122.2 39.4 %collective-permute-start.18 = (bf16[1536,1152]{1,0:T(8,128)(2,1)S(1)}, bf16[1536,1152]{1,0:T(8,128)(2,1)}, u32[]{:S(2)}, u32[]{:S(2)}) collective-permute-start(bf16[1536,1152]{1,0:T(8,128)(2,1)S(1)} %copy-done), channel_id=1, source_target_pairs={{0,8},{8,0},{16,24},{24,16},{1,9},{9,1},{17,25},{25,17},{2,10},{10... | collective-permute-start | bytes 10616840 | tf_op jit(solution)/shard_map/ppermute | solution.py:593
  123.3 36.7 %copy-start.3 = (bf16[768,1536]{1,0:T(8,128)(2,1)S(1)}, bf16[768,1536]{1,0:T(8,128)(2,1)}, u32[]{:S(2)}) copy-start(bf16[768,1536]{1,0:T(8,128)(2,1)} %pad_maximum_fusion) | copy-start | bytes 7077892
  160.0 4.7 %collective-permute-start.20 = (bf16[1536,768]{1,0:T(8,128)(2,1)}, bf16[1536,768]{1,0:T(8,128)(2,1)S(1)}, u32[]{:S(2)}, u32[]{:S(2)}) collective-permute-start(bf16[1536,768]{1,0:T(8,128)(2,1)} %collective-permute-done.19.refs_2_), channel_id=1, source_target_pairs={{0,8},{8,0},{16,24},{24,16},{1,9},{9,1},{17,25},{25,17},{2,10},{10... | collective-permute-start | bytes 7077896 | tf_op jit(solution)/shard_map/ppermute | solution.py:593
  160.0 77.8 %collective-permute-start.30 = (bf16[768,1536]{1,0:T(8,128)(2,1)S(1)}, bf16[768,1536]{1,0:T(8,128)(2,1)}, u32[]{:S(2)}, u32[]{:S(2)}) collective-permute-start(bf16[768,1536]{1,0:T(8,128)(2,1)S(1)} %copy-done.3), channel_id=1, source_target_pairs={{0,1},{1,0},{2,3},{3,2},{4,5},{5,4},{6,7},{7,6},{8,9},{9,8},{10,11... | collective-permute-start | bytes 7077896 | tf_op jit(solution)/shard_map/ppermute | solution.py:603
  161.5 19.0 %collective-permute-start.17 = (bf16[640,384]{1,0:T(8,128)(2,1)}, bf16[640,384]{1,0:T(8,128)(2,1)S(1)}, u32[]{:S(2)}, u32[]{:S(2)}) collective-permute-start(bf16[640,384]{1,0:T(8,128)(2,1)} %get-tuple-element.160.queries.refs_0_), channel_id=1, source_target_pairs={{0,16},{8,24},{16,0},{24,8},{1,17},{9,25},{17,1},{25,9},{2,18},{10... | collective-permute-start | bytes 1474568 | tf_op jit(solution)/shard_map/ppermute | solution.py:596
  164.8 1.5 copy-start.2
  164.8 73.2 %collective-permute-start.24 = (bf16[1536,384]{1,0:T(8,128)(2,1)}, bf16[1536,384]{1,0:T(8,128)(2,1)S(1)}, u32[]{:S(2)}, u32[]{:S(2)}) collective-permute-start(bf16[1536,384]{1,0:T(8,128)(2,1)} %get-tuple-element.167), channel_id=1, source_target_pairs={{0,16},{8,24},{16,0},{24,8},{1,17},{9,25},{17,1},{25,9},{2,18},{10... | collective-permute-start | bytes 3538952 | tf_op jit(solution)/shard_map/ppermute | solution.py:596
  180.5 1.5 copy-start.14
  180.5 30.4 %collective-permute-start.25 = (bf16[640,384]{1,0:T(8,128)(2,1)}, bf16[640,384]{1,0:T(8,128)(2,1)S(1)}, u32[]{:S(2)}, u32[]{:S(2)}) collective-permute-start(bf16[640,384]{1,0:T(8,128)(2,1)} %get-tuple-element.168.refs_0_.queries), channel_id=1, source_target_pairs={{0,16},{8,24},{16,0},{24,8},{1,17},{9,25},{17,1},{25,9},{2,18},{10... | collective-permute-start | bytes 1474568 | tf_op jit(solution)/shard_map/ppermute | solution.py:596
  210.9 0.8 copy-start.15
  237.9 53.0 %collective-permute-start.31 = (bf16[768,1536]{1,0:T(8,128)(2,1)}, bf16[768,1536]{1,0:T(8,128)(2,1)S(1)}, u32[]{:S(2)}, u32[]{:S(2)}) collective-permute-start(bf16[768,1536]{1,0:T(8,128)(2,1)} %collective-permute-done.30.refs_5_), channel_id=1, source_target_pairs={{0,8},{8,0},{16,24},{24,16},{1,9},{9,1},{17,25},{25,17},{2,10},{10... | collective-permute-start | bytes 7077896 | tf_op jit(solution)/shard_map/ppermute | solution.py:593
  238.0 5.8 %copy-start.5 = (bf16[1536,384]{1,0:T(8,128)(2,1)}, bf16[1536,384]{1,0:T(8,128)(2,1)S(1)}, u32[]{:S(2)}) copy-start(bf16[1536,384]{1,0:T(8,128)(2,1)S(1)} %collective-permute-done.24.refs_2_) | copy-start | bytes 3538948
  238.0 5.8 %collective-permute-start.26 = (bf16[1536,384]{1,0:T(8,128)(2,1)S(1)}, bf16[1536,384]{1,0:T(8,128)(2,1)S(1)}, u32[]{:S(2)}, u32[]{:S(2)}) collective-permute-start(bf16[1536,384]{1,0:T(8,128)(2,1)S(1)} %collective-permute-done.24.refs_2_), channel_id=1, source_target_pairs={{0,8},{8,0},{16,24},{24,16},{1,9},{9,1},{17,25},{25,17},{2,10},{10... | collective-permute-start | bytes 3538952 | tf_op jit(solution)/shard_map/ppermute | solution.py:593
  238.5 23.7 %collective-permute-start.27 = (bf16[640,512]{1,0:T(8,128)(2,1)}, bf16[640,512]{1,0:T(8,128)(2,1)S(1)}, u32[]{:S(2)}, u32[]{:S(2)}) collective-permute-start(bf16[640,512]{1,0:T(8,128)(2,1)} %get-tuple-element.171), channel_id=1, source_target_pairs={{0,16},{8,24},{16,0},{24,8},{1,17},{9,25},{17,1},{25,9},{2,18},{10... | collective-permute-start | bytes 1966088 | tf_op jit(solution)/shard_map/ppermute | solution.py:596
  238.5 31.0 %collective-permute-start.23 = (bf16[640,512]{1,0:T(8,128)(2,1)}, bf16[640,512]{1,0:T(8,128)(2,1)S(1)}, u32[]{:S(2)}, u32[]{:S(2)}) collective-permute-start(bf16[640,512]{1,0:T(8,128)(2,1)} %get-tuple-element.165), channel_id=1, source_target_pairs={{0,16},{8,24},{16,0},{24,8},{1,17},{9,25},{17,1},{25,9},{2,18},{10... | collective-permute-start | bytes 1966088 | tf_op jit(solution)/shard_map/ppermute | solution.py:596
  243.8 1.1 copy-start.6
  262.2 0.8 copy-start.13
  266.6 14.3 %collective-permute-start.29 = (bf16[640,384]{1,0:T(8,128)(2,1)}, bf16[640,384]{1,0:T(8,128)(2,1)S(1)}, u32[]{:S(2)}, u32[]{:S(2)}) collective-permute-start(bf16[640,384]{1,0:T(8,128)(2,1)} %merge.3.refs_1_), channel_id=1, source_target_pairs={{0,1},{1,0},{2,3},{3,2},{4,5},{5,4},{6,7},{7,6},{8,9},{9,8},{10,11... | collective-permute-start | bytes 1474568 | tf_op jit(solution)/shard_map/ppermute | solution.py:603
  269.5 0.8 copy-start.12
  274.0 16.9 %collective-permute-start.28 = (bf16[640,384]{1,0:T(8,128)(2,1)}, bf16[640,384]{1,0:T(8,128)(2,1)S(1)}, u32[]{:S(2)}, u32[]{:S(2)}) collective-permute-start(bf16[640,384]{1,0:T(8,128)(2,1)} %merge.2.refs_0_), channel_id=1, source_target_pairs={{0,1},{1,0},{2,3},{3,2},{4,5},{5,4},{6,7},{7,6},{8,9},{9,8},{10,11... | collective-permute-start | bytes 1474568 | tf_op jit(solution)/shard_map/ppermute | solution.py:603
  280.9 10.0 %copy-start.16 = (bf16[640,384]{1,0:T(8,128)(2,1)}, bf16[640,384]{1,0:T(8,128)(2,1)S(1)}, u32[]{:S(2)}) copy-start(bf16[640,384]{1,0:T(8,128)(2,1)S(1)} %collective-permute-done.29.refs_3_) | copy-start | bytes 1474564
  291.7 1.5 copy-start.4
  307.5 16.0 %collective-permute-start.32 = (bf16[320,768]{1,0:T(8,128)(2,1)S(1)}, bf16[320,768]{1,0:T(8,128)(2,1)S(1)}, u32[]{:S(2)}, u32[]{:S(2)}) collective-permute-start(bf16[320,768]{1,0:T(8,128)(2,1)S(1)} %get-tuple-element.183), channel_id=1, source_target_pairs={{0,2},{1,3},{8,10},{9,11},{16,18},{17,19},{24,26},{25,27}} | collective-permute-start | bytes 1474568 | tf_op jit(solution)/shard_map/ppermute | solution.py:800
  308.8 14.7 %collective-permute-start.33 = (bf16[320,768]{1,0:T(8,128)(2,1)S(1)}, bf16[320,768]{1,0:T(8,128)(2,1)}, u32[]{:S(2)}, u32[]{:S(2)}) collective-permute-start(bf16[320,768]{1,0:T(8,128)(2,1)S(1)} %get-tuple-element.184), channel_id=1, source_target_pairs={{6,4},{7,5},{14,12},{15,13},{22,20},{23,21},{30,28},{31,29}} | collective-permute-start | bytes 1474568 | tf_op jit(solution)/shard_map/ppermute | solution.py:800
  310.3 36.7 %collective-permute-start.38 = (bf16[320,768]{1,0:T(8,128)(2,1)S(1)}, bf16[320,768]{1,0:T(8,128)(2,1)S(1)}, u32[]{:S(2)}, u32[]{:S(2)}) collective-permute-start(bf16[320,768]{1,0:T(8,128)(2,1)S(1)} %get-tuple-element.195), channel_id=1, source_target_pairs={{0,2},{1,3},{8,10},{9,11},{16,18},{17,19},{24,26},{25,27}} | collective-permute-start | bytes 1474568 | tf_op jit(solution)/shard_map/ppermute | solution.py:800
  311.6 35.4 %collective-permute-start.39 = (bf16[320,768]{1,0:T(8,128)(2,1)S(1)}, bf16[320,768]{1,0:T(8,128)(2,1)S(1)}, u32[]{:S(2)}, u32[]{:S(2)}) collective-permute-start(bf16[320,768]{1,0:T(8,128)(2,1)S(1)} %get-tuple-element.196), channel_id=1, source_target_pairs={{6,4},{7,5},{14,12},{15,13},{22,20},{23,21},{30,28},{31,29}} | collective-permute-start | bytes 1474568 | tf_op jit(solution)/shard_map/ppermute | solution.py:800
  326.1 31.2 %collective-permute-start.34 = (bf16[320,768]{1,0:T(8,128)(2,1)}, bf16[320,768]{1,0:T(8,128)(2,1)S(1)}, u32[]{:S(2)}, u32[]{:S(2)}) collective-permute-start(bf16[320,768]{1,0:T(8,128)(2,1)} %get-tuple-element.187), channel_id=1, source_target_pairs={{0,2},{1,3},{2,4},{3,5},{8,10},{9,11},{10,12},{11,13},{16,18},{17,... | collective-permute-start | bytes 1474568 | tf_op jit(solution)/shard_map/ppermute | solution.py:800
  345.7 15.5 %collective-permute-start.35 = (bf16[320,768]{1,0:T(8,128)(2,1)S(1)}, bf16[320,768]{1,0:T(8,128)(2,1)}, u32[]{:S(2)}, u32[]{:S(2)}) collective-permute-start(bf16[320,768]{1,0:T(8,128)(2,1)S(1)} %get-tuple-element.188), channel_id=1, source_target_pairs={{4,2},{5,3},{6,4},{7,5},{12,10},{13,11},{14,12},{15,13},{20,18},{2... | collective-permute-start | bytes 1474568 | tf_op jit(solution)/shard_map/ppermute | solution.py:800
  363.8 27.6 %copy-start.18 = (bf16[768]{0:T(1024)(128)(2,1)S(1)}, bf16[768]{0:T(1024)(128)(2,1)}, u32[]{:S(2)}) copy-start(bf16[768]{0:T(1024)(128)(2,1)} %param.18) | copy-start | bytes 4612
  363.8 27.6 %copy-start.1 = (bf16[640,768]{1,0:T(8,128)(2,1)S(1)}, bf16[640,768]{1,0:T(8,128)(2,1)}, u32[]{:S(2)}) copy-start(bf16[640,768]{1,0:T(8,128)(2,1)} %refs_0_) | copy-start | bytes 2949124
  363.8 16.2 %collective-permute-start.40 = (bf16[320,768]{1,0:T(8,128)(2,1)S(1)}, bf16[320,768]{1,0:T(8,128)(2,1)S(1)}, u32[]{:S(2)}, u32[]{:S(2)}) collective-permute-start(bf16[320,768]{1,0:T(8,128)(2,1)S(1)} %get-tuple-element.201), channel_id=1, source_target_pairs={{0,2},{1,3},{2,4},{3,5},{8,10},{9,11},{10,12},{11,13},{16,18},{17,... | collective-permute-start | bytes 1474568 | tf_op jit(solution)/shard_map/ppermute | solution.py:800
  367.0 16.0 %collective-permute-start.41 = (bf16[320,768]{1,0:T(8,128)(2,1)S(1)}, bf16[320,768]{1,0:T(8,128)(2,1)S(1)}, u32[]{:S(2)}, u32[]{:S(2)}) collective-permute-start(bf16[320,768]{1,0:T(8,128)(2,1)S(1)} %get-tuple-element.202), channel_id=1, source_target_pairs={{4,2},{5,3},{6,4},{7,5},{12,10},{13,11},{14,12},{15,13},{20,18},{2... | collective-permute-start | bytes 1474568 | tf_op jit(solution)/shard_map/ppermute | solution.py:800
  368.3 23.3 %collective-permute-start.36 = (bf16[320,768]{1,0:T(8,128)(2,1)S(1)}, bf16[320,768]{1,0:T(8,128)(2,1)S(1)}, u32[]{:S(2)}, u32[]{:S(2)}) collective-permute-start(bf16[320,768]{1,0:T(8,128)(2,1)S(1)} %get-tuple-element.191), channel_id=1, source_target_pairs={{0,2},{1,3},{2,4},{3,5},{4,6},{5,7},{8,10},{9,11},{10,12},{11,13},... | collective-permute-start | bytes 1474568 | tf_op jit(solution)/shard_map/ppermute | solution.py:800
  372.8 20.8 %collective-permute-start.37 = (bf16[320,768]{1,0:T(8,128)(2,1)S(1)}, bf16[320,768]{1,0:T(8,128)(2,1)}, u32[]{:S(2)}, u32[]{:S(2)}) collective-permute-start(bf16[320,768]{1,0:T(8,128)(2,1)S(1)} %get-tuple-element.192), channel_id=1, source_target_pairs={{2,0},{3,1},{4,2},{5,3},{6,4},{7,5},{10,8},{11,9},{12,10},{13,11},... | collective-permute-start | bytes 1474568 | tf_op jit(solution)/shard_map/ppermute | solution.py:800
  384.7 15.0 %collective-permute-start.42 = (bf16[320,768]{1,0:T(8,128)(2,1)S(1)}, bf16[320,768]{1,0:T(8,128)(2,1)}, u32[]{:S(2)}, u32[]{:S(2)}) collective-permute-start(bf16[320,768]{1,0:T(8,128)(2,1)S(1)} %get-tuple-element.207), channel_id=1, source_target_pairs={{0,2},{1,3},{2,4},{3,5},{4,6},{5,7},{8,10},{9,11},{10,12},{11,13},... | collective-permute-start | bytes 1474568 | tf_op jit(solution)/shard_map/ppermute | solution.py:800
  386.7 16.3 %collective-permute-start.43 = (bf16[320,768]{1,0:T(8,128)(2,1)S(1)}, bf16[320,768]{1,0:T(8,128)(2,1)}, u32[]{:S(2)}, u32[]{:S(2)}) collective-permute-start(bf16[320,768]{1,0:T(8,128)(2,1)S(1)} %get-tuple-element.208), channel_id=1, source_target_pairs={{2,0},{3,1},{4,2},{5,3},{6,4},{7,5},{10,8},{11,9},{12,10},{13,11},... | collective-permute-start | bytes 1474568 | tf_op jit(solution)/shard_map/ppermute | solution.py:800
  (1 other events, 0.8 us)

commit v2 on v1

--- a/solution.py
+++ b/solution.py
@@ -291,10 +291,13 @@
     def _():
         totals[...] = jnp.zeros_like(totals)
 
-    begin, size, offset = [], [], []
+    reach = min(256, rows)
+    begin, size, offset, window = [], [], [], []
     count = 0
     for b in range(blocks):
         begin.append(starts[slot * blocks + b])
+        first_row = jnp.minimum(lax.div(begin[b], 16) * 16, rows - reach)
+        window.append(pl.multiple_of(first_row, 16))
         size.append(lengths[slot * blocks + b])
         offset.append(count)
         count = count + size[b]
@@ -306,13 +309,17 @@
 
             def sources(place, b):
                 within = place - offset[b]
-                return jnp.where((within >= 0) & (within < size[b]), within + begin[b], -1)
+                return jnp.where(
+                    (within >= 0) & (within < size[b]), within + begin[b] - window[b], -1
+                )
 
             picked = None
             for b in range(blocks):
-                spread = lax.broadcasted_iota(jnp.int32, (height, rows), 1)
+                spread = lax.broadcasted_iota(jnp.int32, (height, reach), 1)
                 one_hot = jnp.where(spread == sources(down, b), 1.0, 0.0).astype(BF16)
-                part = jnp.dot(one_hot, queries[b][...], preferred_element_type=F32)
+                part = jnp.dot(
+                    one_hot, queries[b][pl.ds(window[b], reach), :], preferred_element_type=F32
+                )
                 picked = part if picked is None else picked + part
             picked = picked.astype(BF16)
             merged = [jnp.zeros((height, 128), F32) for _ in range(GW // 128)]
@@ -347,9 +354,11 @@
                     extra = jnp.where(place == 32 * n + k, term, extra)
             packed = jnp.concatenate(merged + [extra], axis=1).astype(BF16)
             for b in range(blocks):
-                spread = lax.broadcasted_iota(jnp.int32, (rows, height), 0)
+                spread = lax.broadcasted_iota(jnp.int32, (reach, height), 0)
                 one_hot = jnp.where(spread == sources(across, b), 1.0, 0.0).astype(BF16)
-                totals[b] += jnp.dot(one_hot, packed, preferred_element_type=F32)
+                totals[b, pl.ds(window[b], reach), :] += jnp.dot(
+                    one_hot, packed, preferred_element_type=F32
+                )
 
         large = 256
         small = 128
@@ -617,6 +626,10 @@
             x, "head", [(h, h ^ 1) for h in range(head_size) if lowest <= h // 2 <= highest]
         )
 
+    columns = 3 * GW
+    source, _ = lax.optimization_barrier((qkv_weight, layouts))
+    cuts = ((0, columns), (0, 2 * GW), (2 * GW, columns))
+    later = [part_by_part(source, g, cuts) for g in range(1, groups_local)]
     across = to_side(hidden_states)
     blocks = [hidden_states, across]
     places = [head, head ^ 1]
@@ -625,36 +638,46 @@
     settled = across
     for step in range(last):
         if step > 0:
-            up, down, settled, first = lax.optimization_barrier((up, down, settled, first))
-            blocks[4 * step - 5 if step > 1 else 1] = settled
+            up, down, settled, first, later = lax.optimization_barrier(
+                (up, down, settled, first, later)
+            )
+            blocks[1 if step == 1 else tied] = settled
         up = lax.ppermute(
             up, "head", [(h, h + 2) for h in range(head_size) if step <= h // 2 < last]
         )
         down = lax.ppermute(
             down, "head", [(h, h - 2) for h in range(head_size) if 0 < h // 2 <= last - step]
         )
-        settled = across if step == 0 else blocks[4 * step - 1]
-        blocks += [up, to_side_from(up, step + 1, last)]
-        blocks += [down, to_side_from(down, 0, last - 1 - step)]
-        for there, valid in (
-            (line - 1 - step, line >= step + 1),
-            (line + 1 + step, line + 1 + step <= last),
-        ):
+        from_below, from_above = line >= step + 1, line + 1 + step <= last
+        below, above = line - 1 - step, line + 1 + step
+        blocks += [up, down]
+        places += [
+            jnp.where(from_below, 2 * below + side, -1),
+            jnp.where(from_above, 2 * above + side, -1),
+        ]
+        marked = len(blocks)
+        if 2 * step + 1 < last:
+            blocks += [to_side_from(up, step + 1, last), to_side_from(down, 0, last - 1 - step)]
             places += [
-                jnp.where(valid, 2 * there + side, -1),
-                jnp.where(valid, 2 * there + 1 - side, -1),
+                jnp.where(from_below, 2 * below + 1 - side, -1),
+                jnp.where(from_above, 2 * above + 1 - side, -1),
             ]
+        else:
+            here = after(jnp.where(from_below, up, down), blocks[-3])
+            lines_with = [h for h in range(head_size) if h // 2 >= step + 1 or h // 2 <= last - 1 - step]
+            blocks.append(lax.ppermute(here, "head", [(h, h ^ 1) for h in lines_with]))
+            there = jnp.where(from_below, below, above)
+            places.append(jnp.where(from_below | from_above, 2 * there + 1 - side, -1))
+        if step > 0:
+            tied, settled = previous, blocks[previous]
+        previous = marked
     places = jnp.stack(places).astype(jnp.int32)
 
-    columns = 3 * GW
     order = [tok, tok ^ 1]
     for shift in range(1, chips):
         source = (chip + chips - shift) % chips * 2 + core
         order += [source, source ^ 1]
     order = jnp.stack(order).astype(jnp.int32)
-    source, _ = lax.optimization_barrier((qkv_weight, layouts))
-    cuts = ((0, columns), (0, 2 * GW), (2 * GW, columns))
-    later = [part_by_part(source, g, cuts) for g in range(1, groups_local)]
     lengths = suffix_len[0]
     starts, row_start, within = shard_layout(lengths, request_order[0], rows)
     labels = jnp.arange(group_count, dtype=jnp.int32)

time: 410 us -> 397 us (0.968)
  the two profiles are of different devices: /device:TPU:8 before, /device:TPU:14 now
where the time goes in v2:
time: 397 us; the launch traced here: 393 us
  Pallas kernels  159 us (40%)
  waiting for transfers between devices  129 us (32%)
  starting transfers between devices  61.8 us (16%)
  other arithmetic  25.4 us (6%)
  local copies, waits for them, and re-layouts  17.1 us (4%)
    pallas_call x2, Pallas kernels, prefix_attention(): pl.pallas_call(functools.partial(prefix_kernel, blocks), out_shape=[jax.S...  47.1 us
    pallas_call x3, Pallas kernels, project(): pl.pallas_call(functools.partial(qkv_kernel, plan, bundle), out_shape=[ou...  43.3 us
    ppermute x6, waiting for transfers between devices, on_device(): lax.ppermute(up, 'head', up_pairs)  33 us
    pallas_call x2, Pallas kernels, part_by_part(): pl.pallas_call(functools.partial(part_kernel, bundles), out_shape=[jax.Sh...  19.3 us
    ppermute x8, waiting for transfers between devices, to_chip(): lax.ppermute(x, 'tok', [(t, (t // 2 + shift) % chips * 2 + t % 2) for t i...  19.1 us
    ppermute x2, waiting for transfers between devices, to_side_from(): lax.ppermute(x, 'head', [(h, h ^ 1) for h in range(head_size) if lowest <...  18.5 us
    ppermute x6, starting transfers between devices, on_device(): lax.ppermute(up, 'head', up_pairs)  17.9 us
    ppermute x4, waiting for transfers between devices, to_side(): return lax.ppermute(x, 'head', [(h, h ^ 1) for h in range(head_size)])  16.4 us
  transfers between devices with their start and end apart: 42, of which 21 were waited for; matrix products, arithmetic and copies ran while one was open for 7% of the time, Pallas kernels for 37%

profile of v2, /device:TPU:14, one launch (start us, length us, event | category | flops | bytes accessed | tf_op | source)
XLA Modules:
  0.0 392.5 jit_solution(4154512320809296077)
XLA Ops:
  0.0 3.5 collective-permute-start.2
  3.5 2.4 collective-permute-start.3
  10.0 1.8 constant_dynamic-slice_fusion.1
  11.8 9.3 %parts.2.refs_0_ = bf16[1536,1152]{1,0:T(8,128)(2,1)} custom-call(bf16[1536,2304]{1,0:T(8,128)(2,1)} %wide.2), custom_call_target="tpu_custom_call" | custom-call | flops 1000 | bytes 1000 | tf_op jit(solution)/shard_map/parts/pallas_call | solution.py:164
  21.2 1.5 collective-permute-start.1
  22.7 10.0 %parts.3 = (bf16[1536,1152]{1,0:T(8,128)(2,1)}, bf16[1536,768]{1,0:T(8,128)(2,1)}, bf16[1536,384]{1,0:T(8,128)(2,1)}) custom-call(bf16[1536,2304]{1,0:T(8,128)(2,1)} %wide.2), custom_call_target="tpu_custom_call" | custom-call | flops 1000 | bytes 1000 | tf_op jit(solution)/shard_map/parts/pallas_call | solution.py:164
  33.6 3.5 collective-permute-start.5
  37.1 1.9 collective-permute-start.6
  39.1 3.4 collective-permute-start.7
  42.7 2.4 collective-permute-start.8
  45.9 4.6 %multiply_sine_fusion = (f32[640,384]{1,0:T(8,128)}, f32[640,384]{1,0:T(8,128)}) fusion(f32[384]{0:T(512)S(1)} %mul.193, f32[640]{0:T(1024)S(1)} %add_convert_fusion), kind=kLoop, calls=%fused_computation.2 | loop fusion | flops 245760 | bytes 1970176 | tf_op jit(solution)/shard_map/sin | solution.py:136
  50.5 1.7 pad_maximum_fusion
  52.1 4.8 %collective-permute-done.5.refs_6_ = bf16[640,768]{1,0:T(8,128)(2,1)S(1)} collective-permute-done((bf16[640,768]{1,0:T(8,128)(2,1)}, bf16[640,768]{1,0:T(8,128)(2,1)S(1)}, u32[]{:S(2)}, u32[]{:S(2)}) %collective-permute-start.5) | collective-permute-done | bytes 983072 | tf_op jit(solution)/shard_map/ppermute | solution.py:645
  57.0 4.2 %collective-permute-done.6.refs_7_ = bf16[640,768]{1,0:T(8,128)(2,1)} collective-permute-done((bf16[640,768]{1,0:T(8,128)(2,1)}, bf16[640,768]{1,0:T(8,128)(2,1)}, u32[]{:S(2)}, u32[]{:S(2)}) %collective-permute-start.6) | collective-permute-done | bytes 983072 | tf_op jit(solution)/shard_map/ppermute | solution.py:648
  61.2 4.7 %collective-permute-done.7.refs_4_ = bf16[640,768]{1,0:T(8,128)(2,1)} collective-permute-done((bf16[640,768]{1,0:T(8,128)(2,1)}, bf16[640,768]{1,0:T(8,128)(2,1)}, u32[]{:S(2)}, u32[]{:S(2)}) %collective-permute-start.7) | collective-permute-done | bytes 983072 | tf_op jit(solution)/shard_map/ppermute | solution.py:625
  66.7 1.4 collective-permute-start.11
  68.0 2.3 broadcast_select_fusion.1
  70.3 13.8 %collective-permute-done.8.refs_5_ = bf16[640,768]{1,0:T(8,128)(2,1)} collective-permute-done((bf16[640,768]{1,0:T(8,128)(2,1)}, bf16[640,768]{1,0:T(8,128)(2,1)}, u32[]{:S(2)}, u32[]{:S(2)}) %collective-permute-start.8) | collective-permute-done | bytes 983072 | tf_op jit(solution)/shard_map/ppermute | solution.py:625
  84.2 1.5 collective-permute-start.9
  90.3 15.0 %collective-permute-done.9.refs_8_ = bf16[640,768]{1,0:T(8,128)(2,1)} collective-permute-done((bf16[640,768]{1,0:T(8,128)(2,1)}, bf16[640,768]{1,0:T(8,128)(2,1)}, u32[]{:S(2)}, u32[]{:S(2)}) %collective-permute-start.9) | collective-permute-done | bytes 983072 | tf_op jit(solution)/shard_map/ppermute | solution.py:668
  109.5 14.4 %norm.1.normed = bf16[640,6144]{1,0:T(8,128)(2,1)} custom-call(s32[12]{0:T(128)} %stack.123.places, bf16[640,768]{1,0:T(8,128)(2,1)} %refs_0_, bf16[640,768]{1,0:T(8,128)(2,1)} %collective-permute-done.4.refs_1_, bf16[640,768]{1,0:T(8,128)(2,1)} %copy-done.10, bf16[640,768]{1,0:T(8,128)(2,1)} %collective-permute-done.3.refs_3_, ...), custom_call_target="tpu_custom_call" | custom-call | flops 1000 | bytes 1000 | tf_op jit(solution)/shard_map/norm/pallas_call | solution.py:95
  125.1 19.5 %project.3 = (bf16[640,384]{1,0:T(8,128)(2,1)}, bf16[640,384]{1,0:T(8,128)(2,1)}, bf16[640,384]{1,0:T(8,128)(2,1)}) custom-call(s32[4]{0:T(128)} %pad_add_fusion.4.order, bf16[640,6144]{1,0:T(8,128)(2,1)} %norm.1.normed, bf16[1536,1152]{1,0:T(8,128)(2,1)} %parts.2.refs_0_, bf16[1536,1152]{1,0:T(8,128)(2,1)} %collective-permute-done.13.refs_1_, ...), custom_call_target="tpu_custom_call" | custom-call | flops 1000 | bytes 1000 | tf_op jit(solution)/shard_map/project/pallas_call | solution.py:261
  144.6 7.7 %suffix.2 = (f32[640,384]{1,0:T(8,128)}, f32[640,128]{1,0:T(8,128)}) custom-call(s32[640,1]{1,0:T(8,128)} %copy.25.row_start, bf16[640,384]{1,0:T(8,128)(2,1)} %get-tuple-element.172.queries.refs_0_, bf16[640,384]{1,0:T(8,128)(2,1)} %get-tuple-element.164.keys, bf16[640,384]{1,0:T(8,128)(2,1)} %get-tuple-element.165.values), custom_call_target="tpu_custom_call" | custom-call | flops 1000 | bytes 1000 | tf_op jit(solution)/shard_map/suffix/pallas_call | solution.py:461
  152.2 10.7 %collective-permute-done.17.refs_2_ = bf16[1536,768]{1,0:T(8,128)(2,1)} collective-permute-done((bf16[1536,768]{1,0:T(8,128)(2,1)}, bf16[1536,768]{1,0:T(8,128)(2,1)}, u32[]{:S(2)}, u32[]{:S(2)}) %collective-permute-start.17) | collective-permute-done | bytes 2359328 | tf_op jit(solution)/shard_map/ppermute | solution.py:605
  162.9 1.5 collective-permute-start.28
  164.9 2.7 collective-permute-done.18.refs_3_
  169.1 14.2 %project.4 = (bf16[640,384]{1,0:T(8,128)(2,1)}, bf16[640,384]{1,0:T(8,128)(2,1)}) custom-call(s32[4]{0:T(128)} %pad_add_fusion.4.order, bf16[640,6144]{1,0:T(8,128)(2,1)} %norm.1.normed, bf16[1536,1152]{1,0:T(8,128)(2,1)} %get-tuple-element.160.refs_0_, bf16[1536,1152]{1,0:T(8,128)(2,1)} %collective-permute-done.16.refs_1_, ...), custom_call_target="tpu_custom_call" | custom-call | flops 1000 | bytes 1000 | tf_op jit(solution)/shard_map/project/pallas_call | solution.py:261
  184.0 23.6 %prefix.2 = (bf16[640,512]{1,0:T(8,128)(2,1)}, bf16[640,512]{1,0:T(8,128)(2,1)}) custom-call(s32[8]{0:T(128)} %reshape_squeeze.6.starts, s32[8]{0:T(128)} %reshape_squeeze.7.lengths, bf16[640,384]{1,0:T(8,128)(2,1)} %get-tuple-element.172.queries.refs_0_, bf16[640,384]{1,0:T(8,128)(2,1)} %copy-done.14, bf16[2,2048,768]{2,1,0:T(8,128)(2,1)} %refs_2_.3, ...), custom_call_target="tpu_custom_call" | custom-call | flops 1000 | bytes 1000 | tf_op jit(solution)/shard_map/prefix/pallas_call | solution.py:403
  207.6 6.2 %collective-permute-done.23.refs_1_ = bf16[640,384]{1,0:T(8,128)(2,1)S(1)} collective-permute-done((bf16[640,384]{1,0:T(8,128)(2,1)}, bf16[640,384]{1,0:T(8,128)(2,1)S(1)}, u32[]{:S(2)}, u32[]{:S(2)}) %collective-permute-start.23) | collective-permute-done | bytes 491552 | tf_op jit(solution)/shard_map/ppermute | solution.py:605
  214.6 23.5 %prefix.3 = (bf16[640,512]{1,0:T(8,128)(2,1)}, bf16[640,512]{1,0:T(8,128)(2,1)}) custom-call(s32[8]{0:T(128)} %reshape_squeeze.6.starts, s32[8]{0:T(128)} %reshape_squeeze.7.lengths, bf16[640,384]{1,0:T(8,128)(2,1)} %get-tuple-element.180.refs_0_.queries, bf16[640,384]{1,0:T(8,128)(2,1)} %copy-done.15, bf16[2,2048,768]{2,1,0:T(8,128)(2,1)} %refs_2_.3, ...), custom_call_target="tpu_custom_call" | custom-call | flops 1000 | bytes 1000 | tf_op jit(solution)/shard_map/prefix/pallas_call | solution.py:403
  238.7 2.0 collective-permute-start.21
  240.7 3.3 collective-permute-done.24.refs_3_
  245.1 9.6 %project.5.values = bf16[640,384]{1,0:T(8,128)(2,1)} custom-call(s32[4]{0:T(128)} %pad_add_fusion.4.order, bf16[640,6144]{1,0:T(8,128)(2,1)} %norm.1.normed, bf16[1536,1152]{1,0:T(8,128)(2,1)} %get-tuple-element.160.refs_0_, bf16[1536,1152]{1,0:T(8,128)(2,1)} %collective-permute-done.16.refs_1_, bf16[1536,384]{1,0:T(8,128)(2,1)} %copy-done.8, ...), custom_call_target="tpu_custom_call" | custom-call | flops 1000 | bytes 1000 | tf_op jit(solution)/shard_map/project/pallas_call | solution.py:261
  254.7 7.7 %suffix.3 = (f32[640,384]{1,0:T(8,128)}, f32[640,128]{1,0:T(8,128)}) custom-call(s32[640,1]{1,0:T(8,128)} %copy.25.row_start, bf16[640,384]{1,0:T(8,128)(2,1)} %get-tuple-element.180.refs_0_.queries, bf16[640,384]{1,0:T(8,128)(2,1)} %get-tuple-element.171.keys, bf16[640,384]{1,0:T(8,128)(2,1)} %project.5.values), custom_call_target="tpu_custom_call" | custom-call | flops 1000 | bytes 1000 | tf_op jit(solution)/shard_map/suffix/pallas_call | solution.py:461
  263.2 3.6 merge.3.refs_1_
  267.4 2.3 collective-permute-done.21.refs_1_
  270.5 3.6 merge.2.refs_0_
  274.7 6.4 %collective-permute-done.27.refs_3_ = bf16[640,384]{1,0:T(8,128)(2,1)S(1)} collective-permute-done((bf16[640,384]{1,0:T(8,128)(2,1)}, bf16[640,384]{1,0:T(8,128)(2,1)S(1)}, u32[]{:S(2)}, u32[]{:S(2)}) %collective-permute-start.27) | collective-permute-done | bytes 491552 | tf_op jit(solution)/shard_map/ppermute | solution.py:612
  281.1 10.0 %collective-permute-done.26.refs_2_ = bf16[640,384]{1,0:T(8,128)(2,1)S(1)} collective-permute-done((bf16[640,384]{1,0:T(8,128)(2,1)}, bf16[640,384]{1,0:T(8,128)(2,1)S(1)}, u32[]{:S(2)}, u32[]{:S(2)}) %collective-permute-start.26) | collective-permute-done | bytes 491552 | tf_op jit(solution)/shard_map/ppermute | solution.py:612
  291.9 1.5 copy-done.7
  293.4 12.0 %output.1 = f32[4,640,768]{2,1,0:T(8,128)} custom-call(s32[2]{0:T(128)} %pad_add_fusion.5.place, bf16[640,384]{1,0:T(8,128)(2,1)} %merge.2.refs_0_, bf16[640,384]{1,0:T(8,128)(2,1)} %merge.3.refs_1_, bf16[640,384]{1,0:T(8,128)(2,1)} %copy-done.17, bf16[640,384]{1,0:T(8,128)(2,1)} %copy-done.16, bf16[768,6144]{1,0:T(8,128)(2,1)} %refs_4_.5, ...), custom_call_target="tpu_custom_call" | custom-call | flops 1000 | bytes 1000 | tf_op jit(solution)/shard_map/output/pallas_call | solution.py:554
  305.4 2.3 fusion.13
  307.7 1.3 collective-permute-start.30
  309.0 1.5 collective-permute-start.31
  312.5 11.1 %collective-permute-done.30 = bf16[320,768]{1,0:T(8,128)(2,1)S(1)} collective-permute-done((bf16[320,768]{1,0:T(8,128)(2,1)S(1)}, bf16[320,768]{1,0:T(8,128)(2,1)S(1)}, u32[]{:S(2)}, u32[]{:S(2)}) %collective-permute-start.30) | collective-permute-done | bytes 491552 | tf_op jit(solution)/shard_map/ppermute | solution.py:823
  323.6 2.6 fusion.8
  326.2 5.4 %collective-permute-start.32 = (bf16[320,768]{1,0:T(8,128)(2,1)}, bf16[320,768]{1,0:T(8,128)(2,1)S(1)}, u32[]{:S(2)}, u32[]{:S(2)}) collective-permute-start(bf16[320,768]{1,0:T(8,128)(2,1)} %get-tuple-element.199), channel_id=1, source_target_pairs={{0,2},{1,3},{2,4},{3,5},{8,10},{9,11},{10,12},{11,13},{16,18},{17,... | collective-permute-start | bytes 1474568 | tf_op jit(solution)/shard_map/ppermute | solution.py:823
  331.6 1.3 collective-permute-start.33
  334.1 10.5 %collective-permute-done.32 = bf16[320,768]{1,0:T(8,128)(2,1)S(1)} collective-permute-done((bf16[320,768]{1,0:T(8,128)(2,1)}, bf16[320,768]{1,0:T(8,128)(2,1)S(1)}, u32[]{:S(2)}, u32[]{:S(2)}) %collective-permute-start.32) | collective-permute-done | bytes 491552 | tf_op jit(solution)/shard_map/ppermute | solution.py:823
  344.7 2.0 collective-permute-done.33
  346.6 2.7 fusion.7
  349.3 3.5 collective-permute-start.38
  352.9 1.3 collective-permute-start.39
  354.2 4.6 %collective-permute-start.34 = (bf16[320,768]{1,0:T(8,128)(2,1)S(1)}, bf16[320,768]{1,0:T(8,128)(2,1)S(1)}, u32[]{:S(2)}, u32[]{:S(2)}) collective-permute-start(bf16[320,768]{1,0:T(8,128)(2,1)S(1)} %get-tuple-element.203), channel_id=1, source_target_pairs={{0,2},{1,3},{2,4},{3,5},{4,6},{5,7},{8,10},{9,11},{10,12},{11,13},... | collective-permute-start | bytes 1474568 | tf_op jit(solution)/shard_map/ppermute | solution.py:823
  358.7 1.9 collective-permute-start.35
  360.6 4.9 %collective-permute-done.38 = bf16[320,768]{1,0:T(8,128)(2,1)S(1)} collective-permute-done((bf16[320,768]{1,0:T(8,128)(2,1)S(1)}, bf16[320,768]{1,0:T(8,128)(2,1)S(1)}, u32[]{:S(2)}, u32[]{:S(2)}) %collective-permute-start.38) | collective-permute-done | bytes 491552 | tf_op jit(solution)/shard_map/ppermute | solution.py:823
  365.5 3.3 collective-permute-done.39
  368.9 1.8 fusion.2
  370.6 1.9 collective-permute-start.40
  372.6 4.7 %collective-permute-start.41 = (bf16[320,768]{1,0:T(8,128)(2,1)S(1)}, bf16[320,768]{1,0:T(8,128)(2,1)}, u32[]{:S(2)}, u32[]{:S(2)}) collective-permute-start(bf16[320,768]{1,0:T(8,128)(2,1)S(1)} %get-tuple-element.220), channel_id=1, source_target_pairs={{2,0},{3,1},{4,2},{5,3},{6,4},{7,5},{10,8},{11,9},{12,10},{13,11},... | collective-permute-start | bytes 1474568 | tf_op jit(solution)/shard_map/ppermute | solution.py:823
  377.4 2.1 collective-permute-done.35
  379.5 5.2 %collective-permute-done.40 = bf16[320,768]{1,0:T(8,128)(2,1)} collective-permute-done((bf16[320,768]{1,0:T(8,128)(2,1)S(1)}, bf16[320,768]{1,0:T(8,128)(2,1)}, u32[]{:S(2)}, u32[]{:S(2)}) %collective-permute-start.40) | collective-permute-done | bytes 491552 | tf_op jit(solution)/shard_map/ppermute | solution.py:823
  384.7 4.2 %collective-permute-done.41 = bf16[320,768]{1,0:T(8,128)(2,1)} collective-permute-done((bf16[320,768]{1,0:T(8,128)(2,1)S(1)}, bf16[320,768]{1,0:T(8,128)(2,1)}, u32[]{:S(2)}, u32[]{:S(2)}) %collective-permute-start.41) | collective-permute-done | bytes 491552 | tf_op jit(solution)/shard_map/ppermute | solution.py:823
  388.9 2.4 fusion.1
  (129 shorter events, 29.7 us)
Async XLA Ops:
  0.0 32.7 %collective-permute-start.2 = (bf16[640,768]{1,0:T(8,128)(2,1)}, bf16[640,768]{1,0:T(8,128)(2,1)S(1)}, u32[]{:S(2)}, u32[]{:S(2)}) collective-permute-start(bf16[640,768]{1,0:T(8,128)(2,1)} %refs_0_), channel_id=1, source_target_pairs={{0,2},{1,3},{2,4},{3,5},{4,6},{5,7},{8,10},{9,11},{10,12},{11,13},... | collective-permute-start | bytes 2949128 | tf_op jit(solution)/shard_map/ppermute | solution.py:645
  3.5 29.2 %collective-permute-start.3 = (bf16[640,768]{1,0:T(8,128)(2,1)}, bf16[640,768]{1,0:T(8,128)(2,1)}, u32[]{:S(2)}, u32[]{:S(2)}) collective-permute-start(bf16[640,768]{1,0:T(8,128)(2,1)} %refs_0_), channel_id=1, source_target_pairs={{2,0},{3,1},{4,2},{5,3},{6,4},{7,5},{10,8},{11,9},{12,10},{13,11},... | collective-permute-start | bytes 2949128 | tf_op jit(solution)/shard_map/ppermute | solution.py:648
  5.9 26.8 %collective-permute-start.4 = (bf16[640,768]{1,0:T(8,128)(2,1)}, bf16[640,768]{1,0:T(8,128)(2,1)}, u32[]{:S(2)}, u32[]{:S(2)}) collective-permute-start(bf16[640,768]{1,0:T(8,128)(2,1)} %refs_0_), channel_id=1, source_target_pairs={{0,1},{1,0},{2,3},{3,2},{4,5},{5,4},{6,7},{7,6},{8,9},{9,8},{10,11... | collective-permute-start | bytes 2949128 | tf_op jit(solution)/shard_map/ppermute | solution.py:612
  7.2 14.0 %collective-permute-start = (s32[2,8]{1,0:T(2,128)S(1)}, s32[2,8]{1,0:T(2,128)S(1)}, u32[]{:S(2)}, u32[]{:S(2)}) collective-permute-start(s32[2,8]{1,0:T(2,128)S(1)} %pad_add_fusion.1), channel_id=1, source_target_pairs={{0,16},{8,24},{16,0},{24,8},{1,17},{9,25},{17,1},{25,9},{2,18},{10... | collective-permute-start | bytes 200 | tf_op jit(solution)/shard_map/ppermute | solution.py:605
  21.2 87.2 %collective-permute-start.1 = (bf16[1536,1152]{1,0:T(8,128)(2,1)}, bf16[1536,1152]{1,0:T(8,128)(2,1)}, u32[]{:S(2)}, u32[]{:S(2)}) collective-permute-start(bf16[1536,1152]{1,0:T(8,128)(2,1)} %parts.2.refs_0_), channel_id=1, source_target_pairs={{0,16},{8,24},{16,0},{24,8},{1,17},{9,25},{17,1},{25,9},{2,18},{10... | collective-permute-start | bytes 10616840 | tf_op jit(solution)/shard_map/ppermute | solution.py:605
  22.7 20.0 %copy-start.18 = (bf16[2304]{0:T(1024)(128)(2,1)S(1)}, bf16[2304]{0:T(1024)(128)(2,1)}, u32[]{:S(2)}) copy-start(bf16[2304]{0:T(1024)(128)(2,1)} %param.16) | copy-start | bytes 13828
  32.7 0.9 copy-start.10
  33.6 23.3 %collective-permute-start.5 = (bf16[640,768]{1,0:T(8,128)(2,1)}, bf16[640,768]{1,0:T(8,128)(2,1)S(1)}, u32[]{:S(2)}, u32[]{:S(2)}) collective-permute-start(bf16[640,768]{1,0:T(8,128)(2,1)} %copy-done.10), channel_id=1, source_target_pairs={{2,4},{3,5},{4,6},{5,7},{10,12},{11,13},{12,14},{13,15},{18,20},{1... | collective-permute-start | bytes 2949128 | tf_op jit(solution)/shard_map/ppermute | solution.py:645
  37.1 24.1 %collective-permute-start.6 = (bf16[640,768]{1,0:T(8,128)(2,1)}, bf16[640,768]{1,0:T(8,128)(2,1)}, u32[]{:S(2)}, u32[]{:S(2)}) collective-permute-start(bf16[640,768]{1,0:T(8,128)(2,1)} %collective-permute-done.3.refs_3_), channel_id=1, source_target_pairs={{2,0},{3,1},{4,2},{5,3},{10,8},{11,9},{12,10},{13,11},{18,16},{19,... | collective-permute-start | bytes 2949128 | tf_op jit(solution)/shard_map/ppermute | solution.py:648
  39.1 26.9 %collective-permute-start.7 = (bf16[640,768]{1,0:T(8,128)(2,1)}, bf16[640,768]{1,0:T(8,128)(2,1)}, u32[]{:S(2)}, u32[]{:S(2)}) collective-permute-start(bf16[640,768]{1,0:T(8,128)(2,1)} %copy-done.10), channel_id=1, source_target_pairs={{2,3},{3,2},{4,5},{5,4},{6,7},{7,6},{10,11},{11,10},{12,13},{13,12... | collective-permute-start | bytes 2949128 | tf_op jit(solution)/shard_map/ppermute | solution.py:625
  42.7 41.4 %collective-permute-start.8 = (bf16[640,768]{1,0:T(8,128)(2,1)}, bf16[640,768]{1,0:T(8,128)(2,1)}, u32[]{:S(2)}, u32[]{:S(2)}) collective-permute-start(bf16[640,768]{1,0:T(8,128)(2,1)} %collective-permute-done.3.refs_3_), channel_id=1, source_target_pairs={{0,1},{1,0},{2,3},{3,2},{4,5},{5,4},{8,9},{9,8},{10,11},{11,10},{1... | collective-permute-start | bytes 2949128 | tf_op jit(solution)/shard_map/ppermute | solution.py:625
  52.1 54.1 %copy-start.20 = (s32[8]{0:T(128)S(1)}, s32[8]{0:T(128)}, u32[]{:S(2)}) copy-start(s32[8]{0:T(128)} %param.23) | copy-start | bytes 100
  57.0 33.3 %copy-start.2 = (bf16[640,768]{1,0:T(8,128)(2,1)}, bf16[640,768]{1,0:T(8,128)(2,1)S(1)}, u32[]{:S(2)}) copy-start(bf16[640,768]{1,0:T(8,128)(2,1)S(1)} %collective-permute-done.5.refs_6_) | copy-start | bytes 2949124
  66.0 23.1 %collective-permute-start.10 = (bf16[640,768]{1,0:T(8,128)(2,1)S(1)}, bf16[640,768]{1,0:T(8,128)(2,1)S(1)}, u32[]{:S(2)}, u32[]{:S(2)}) collective-permute-start(bf16[640,768]{1,0:T(8,128)(2,1)S(1)} %collective-permute-done.5.refs_6_), channel_id=1, source_target_pairs={{4,6},{5,7},{12,14},{13,15},{20,22},{21,23},{28,30},{29,31}} | collective-permute-start | bytes 2949128 | tf_op jit(solution)/shard_map/ppermute | solution.py:645
  66.7 22.4 %collective-permute-start.11 = (bf16[640,768]{1,0:T(8,128)(2,1)}, bf16[640,768]{1,0:T(8,128)(2,1)S(1)}, u32[]{:S(2)}, u32[]{:S(2)}) collective-permute-start(bf16[640,768]{1,0:T(8,128)(2,1)} %collective-permute-done.6.refs_7_), channel_id=1, source_target_pairs={{2,0},{3,1},{10,8},{11,9},{18,16},{19,17},{26,24},{27,25}} | collective-permute-start | bytes 2949128 | tf_op jit(solution)/shard_map/ppermute | solution.py:648
  84.2 21.2 %collective-permute-start.9 = (bf16[640,768]{1,0:T(8,128)(2,1)}, bf16[640,768]{1,0:T(8,128)(2,1)}, u32[]{:S(2)}, u32[]{:S(2)}) collective-permute-start(bf16[640,768]{1,0:T(8,128)(2,1)} %broadcast_select_fusion.1), channel_id=1, source_target_pairs={{0,1},{1,0},{2,3},{3,2},{4,5},{5,4},{6,7},{7,6},{8,9},{9,8},{10,11... | collective-permute-start | bytes 2949128 | tf_op jit(solution)/shard_map/ppermute | solution.py:668
  88.8 35.1 %collective-permute-start.13 = (bf16[1536,1152]{1,0:T(8,128)(2,1)}, bf16[1536,1152]{1,0:T(8,128)(2,1)}, u32[]{:S(2)}, u32[]{:S(2)}) collective-permute-start(bf16[1536,1152]{1,0:T(8,128)(2,1)} %parts.2.refs_0_), channel_id=1, source_target_pairs={{0,8},{8,0},{16,24},{24,16},{1,9},{9,1},{17,25},{25,17},{2,10},{10... | collective-permute-start | bytes 10616840 | tf_op jit(solution)/shard_map/ppermute | solution.py:602
  89.1 20.4 %copy-start.3 = (bf16[640,768]{1,0:T(8,128)(2,1)}, bf16[640,768]{1,0:T(8,128)(2,1)S(1)}, u32[]{:S(2)}) copy-start(bf16[640,768]{1,0:T(8,128)(2,1)S(1)} %collective-permute-done.10.refs_9_) | copy-start | bytes 2949124
  89.1 20.4 %copy-start.4 = (bf16[640,768]{1,0:T(8,128)(2,1)}, bf16[640,768]{1,0:T(8,128)(2,1)S(1)}, u32[]{:S(2)}) copy-start(bf16[640,768]{1,0:T(8,128)(2,1)S(1)} %collective-permute-done.11.refs_10_) | copy-start | bytes 2949124
  105.4 3.0 collective-permute-start.12
  108.3 1.2 copy-start.11
  108.3 16.7 %collective-permute-start.14 = (bf16[1536,1152]{1,0:T(8,128)(2,1)}, bf16[1536,1152]{1,0:T(8,128)(2,1)}, u32[]{:S(2)}, u32[]{:S(2)}) collective-permute-start(bf16[1536,1152]{1,0:T(8,128)(2,1)} %collective-permute-done.1.refs_2_), channel_id=1, source_target_pairs={{0,8},{8,0},{16,24},{24,16},{1,9},{9,1},{17,25},{25,17},{2,10},{10... | collective-permute-start | bytes 10616840 | tf_op jit(solution)/shard_map/ppermute | solution.py:602
  108.4 75.5 %collective-permute-start.19 = (bf16[2,2048,768]{2,1,0:T(8,128)(2,1)}, bf16[2,2048,768]{2,1,0:T(8,128)(2,1)}, u32[]{:S(2)}, u32[]{:S(2)}) collective-permute-start(bf16[2,2048,768]{2,1,0:T(8,128)(2,1)} %refs_2_.3), channel_id=1, source_target_pairs={{0,8},{8,0},{16,24},{24,16},{1,9},{9,1},{17,25},{25,17},{2,10},{10... | collective-permute-start | bytes 18874376 | tf_op jit(solution)/shard_map/ppermute | solution.py:602
  108.9 75.0 %collective-permute-start.20 = (bf16[2,2048,768]{2,1,0:T(8,128)(2,1)}, bf16[2,2048,768]{2,1,0:T(8,128)(2,1)}, u32[]{:S(2)}, u32[]{:S(2)}) collective-permute-start(bf16[2,2048,768]{2,1,0:T(8,128)(2,1)} %refs_4_.4), channel_id=1, source_target_pairs={{0,8},{8,0},{16,24},{24,16},{1,9},{9,1},{17,25},{25,17},{2,10},{10... | collective-permute-start | bytes 18874376 | tf_op jit(solution)/shard_map/ppermute | solution.py:602
  109.0 53.9 %collective-permute-start.17 = (bf16[1536,768]{1,0:T(8,128)(2,1)}, bf16[1536,768]{1,0:T(8,128)(2,1)}, u32[]{:S(2)}, u32[]{:S(2)}) collective-permute-start(bf16[1536,768]{1,0:T(8,128)(2,1)} %get-tuple-element.162), channel_id=1, source_target_pairs={{0,16},{8,24},{16,0},{24,8},{1,17},{9,25},{17,1},{25,9},{2,18},{10... | collective-permute-start | bytes 7077896 | tf_op jit(solution)/shard_map/ppermute | solution.py:605
  109.5 14.4 %copy-start = (bf16[1536,1152]{1,0:T(8,128)(2,1)S(1)}, bf16[1536,1152]{1,0:T(8,128)(2,1)}, u32[]{:S(2)}) copy-start(bf16[1536,1152]{1,0:T(8,128)(2,1)} %get-tuple-element.160.refs_0_) | copy-start | bytes 10616836
  123.9 40.5 %collective-permute-start.16 = (bf16[1536,1152]{1,0:T(8,128)(2,1)S(1)}, bf16[1536,1152]{1,0:T(8,128)(2,1)}, u32[]{:S(2)}, u32[]{:S(2)}) collective-permute-start(bf16[1536,1152]{1,0:T(8,128)(2,1)S(1)} %copy-done), channel_id=1, source_target_pairs={{0,8},{8,0},{16,24},{24,16},{1,9},{9,1},{17,25},{25,17},{2,10},{10... | collective-permute-start | bytes 10616840 | tf_op jit(solution)/shard_map/ppermute | solution.py:602
  125.1 37.8 %copy-start.6 = (bf16[768,1536]{1,0:T(8,128)(2,1)S(1)}, bf16[768,1536]{1,0:T(8,128)(2,1)}, u32[]{:S(2)}) copy-start(bf16[768,1536]{1,0:T(8,128)(2,1)} %pad_maximum_fusion) | copy-start | bytes 7077892
  162.9 4.7 %collective-permute-start.18 = (bf16[1536,768]{1,0:T(8,128)(2,1)}, bf16[1536,768]{1,0:T(8,128)(2,1)S(1)}, u32[]{:S(2)}, u32[]{:S(2)}) collective-permute-start(bf16[1536,768]{1,0:T(8,128)(2,1)} %collective-permute-done.17.refs_2_), channel_id=1, source_target_pairs={{0,8},{8,0},{16,24},{24,16},{1,9},{9,1},{17,25},{25,17},{2,10},{10... | collective-permute-start | bytes 7077896 | tf_op jit(solution)/shard_map/ppermute | solution.py:602
  162.9 75.2 %collective-permute-start.28 = (bf16[768,1536]{1,0:T(8,128)(2,1)S(1)}, bf16[768,1536]{1,0:T(8,128)(2,1)}, u32[]{:S(2)}, u32[]{:S(2)}) collective-permute-start(bf16[768,1536]{1,0:T(8,128)(2,1)S(1)} %copy-done.6), channel_id=1, source_target_pairs={{0,1},{1,0},{2,3},{3,2},{4,5},{5,4},{6,7},{7,6},{8,9},{9,8},{10,11... | collective-permute-start | bytes 7077896 | tf_op jit(solution)/shard_map/ppermute | solution.py:612
  164.4 18.8 %collective-permute-start.15 = (bf16[640,384]{1,0:T(8,128)(2,1)}, bf16[640,384]{1,0:T(8,128)(2,1)S(1)}, u32[]{:S(2)}, u32[]{:S(2)}) collective-permute-start(bf16[640,384]{1,0:T(8,128)(2,1)} %get-tuple-element.172.queries.refs_0_), channel_id=1, source_target_pairs={{0,16},{8,24},{16,0},{24,8},{1,17},{9,25},{17,1},{25,9},{2,18},{10... | collective-permute-start | bytes 1474568 | tf_op jit(solution)/shard_map/ppermute | solution.py:605
  167.6 1.4 copy-start.5
  167.7 70.5 %collective-permute-start.22 = (bf16[1536,384]{1,0:T(8,128)(2,1)}, bf16[1536,384]{1,0:T(8,128)(2,1)S(1)}, u32[]{:S(2)}, u32[]{:S(2)}) collective-permute-start(bf16[1536,384]{1,0:T(8,128)(2,1)} %get-tuple-element.179), channel_id=1, source_target_pairs={{0,16},{8,24},{16,0},{24,8},{1,17},{9,25},{17,1},{25,9},{2,18},{10... | collective-permute-start | bytes 3538952 | tf_op jit(solution)/shard_map/ppermute | solution.py:605
  183.2 0.8 copy-start.14
  183.2 30.5 %collective-permute-start.23 = (bf16[640,384]{1,0:T(8,128)(2,1)}, bf16[640,384]{1,0:T(8,128)(2,1)S(1)}, u32[]{:S(2)}, u32[]{:S(2)}) collective-permute-start(bf16[640,384]{1,0:T(8,128)(2,1)} %get-tuple-element.180.refs_0_.queries), channel_id=1, source_target_pairs={{0,16},{8,24},{16,0},{24,8},{1,17},{9,25},{17,1},{25,9},{2,18},{10... | collective-permute-start | bytes 1474568 | tf_op jit(solution)/shard_map/ppermute | solution.py:605
  213.8 0.8 copy-start.15
  238.1 53.0 %collective-permute-start.29 = (bf16[768,1536]{1,0:T(8,128)(2,1)}, bf16[768,1536]{1,0:T(8,128)(2,1)S(1)}, u32[]{:S(2)}, u32[]{:S(2)}) collective-permute-start(bf16[768,1536]{1,0:T(8,128)(2,1)} %collective-permute-done.28.refs_5_), channel_id=1, source_target_pairs={{0,8},{8,0},{16,24},{24,16},{1,9},{9,1},{17,25},{25,17},{2,10},{10... | collective-permute-start | bytes 7077896 | tf_op jit(solution)/shard_map/ppermute | solution.py:602
  238.2 5.8 %copy-start.8 = (bf16[1536,384]{1,0:T(8,128)(2,1)}, bf16[1536,384]{1,0:T(8,128)(2,1)S(1)}, u32[]{:S(2)}) copy-start(bf16[1536,384]{1,0:T(8,128)(2,1)S(1)} %collective-permute-done.22.refs_2_) | copy-start | bytes 3538948
  238.2 5.8 %collective-permute-start.24 = (bf16[1536,384]{1,0:T(8,128)(2,1)S(1)}, bf16[1536,384]{1,0:T(8,128)(2,1)S(1)}, u32[]{:S(2)}, u32[]{:S(2)}) collective-permute-start(bf16[1536,384]{1,0:T(8,128)(2,1)S(1)} %collective-permute-done.22.refs_2_), channel_id=1, source_target_pairs={{0,8},{8,0},{16,24},{24,16},{1,9},{9,1},{17,25},{25,17},{2,10},{10... | collective-permute-start | bytes 3538952 | tf_op jit(solution)/shard_map/ppermute | solution.py:602
  238.7 23.7 %collective-permute-start.25 = (bf16[640,512]{1,0:T(8,128)(2,1)}, bf16[640,512]{1,0:T(8,128)(2,1)S(1)}, u32[]{:S(2)}, u32[]{:S(2)}) collective-permute-start(bf16[640,512]{1,0:T(8,128)(2,1)} %get-tuple-element.183), channel_id=1, source_target_pairs={{0,16},{8,24},{16,0},{24,8},{1,17},{9,25},{17,1},{25,9},{2,18},{10... | collective-permute-start | bytes 1966088 | tf_op jit(solution)/shard_map/ppermute | solution.py:605
  238.7 31.0 %collective-permute-start.21 = (bf16[640,512]{1,0:T(8,128)(2,1)}, bf16[640,512]{1,0:T(8,128)(2,1)S(1)}, u32[]{:S(2)}, u32[]{:S(2)}) collective-permute-start(bf16[640,512]{1,0:T(8,128)(2,1)} %get-tuple-element.177), channel_id=1, source_target_pairs={{0,16},{8,24},{16,0},{24,8},{1,17},{9,25},{17,1},{25,9},{2,18},{10... | collective-permute-start | bytes 1966088 | tf_op jit(solution)/shard_map/ppermute | solution.py:605
  244.0 1.0 copy-start.9
  262.4 0.9 copy-start.13
  266.9 14.3 %collective-permute-start.27 = (bf16[640,384]{1,0:T(8,128)(2,1)}, bf16[640,384]{1,0:T(8,128)(2,1)S(1)}, u32[]{:S(2)}, u32[]{:S(2)}) collective-permute-start(bf16[640,384]{1,0:T(8,128)(2,1)} %merge.3.refs_1_), channel_id=1, source_target_pairs={{0,1},{1,0},{2,3},{3,2},{4,5},{5,4},{6,7},{7,6},{8,9},{9,8},{10,11... | collective-permute-start | bytes 1474568 | tf_op jit(solution)/shard_map/ppermute | solution.py:612
  269.7 0.9 copy-start.12
  274.1 17.0 %collective-permute-start.26 = (bf16[640,384]{1,0:T(8,128)(2,1)}, bf16[640,384]{1,0:T(8,128)(2,1)S(1)}, u32[]{:S(2)}, u32[]{:S(2)}) collective-permute-start(bf16[640,384]{1,0:T(8,128)(2,1)} %merge.2.refs_0_), channel_id=1, source_target_pairs={{0,1},{1,0},{2,3},{3,2},{4,5},{5,4},{6,7},{7,6},{8,9},{9,8},{10,11... | collective-permute-start | bytes 1474568 | tf_op jit(solution)/shard_map/ppermute | solution.py:612
  281.1 10.0 %copy-start.16 = (bf16[640,384]{1,0:T(8,128)(2,1)}, bf16[640,384]{1,0:T(8,128)(2,1)S(1)}, u32[]{:S(2)}) copy-start(bf16[640,384]{1,0:T(8,128)(2,1)S(1)} %collective-permute-done.27.refs_3_) | copy-start | bytes 1474564
  291.1 0.8 copy-start.17
  291.9 1.5 copy-start.7
  307.7 15.9 %collective-permute-start.30 = (bf16[320,768]{1,0:T(8,128)(2,1)S(1)}, bf16[320,768]{1,0:T(8,128)(2,1)S(1)}, u32[]{:S(2)}, u32[]{:S(2)}) collective-permute-start(bf16[320,768]{1,0:T(8,128)(2,1)S(1)} %get-tuple-element.195), channel_id=1, source_target_pairs={{0,2},{1,3},{8,10},{9,11},{16,18},{17,19},{24,26},{25,27}} | collective-permute-start | bytes 1474568 | tf_op jit(solution)/shard_map/ppermute | solution.py:823
  309.0 14.6 %collective-permute-start.31 = (bf16[320,768]{1,0:T(8,128)(2,1)S(1)}, bf16[320,768]{1,0:T(8,128)(2,1)}, u32[]{:S(2)}, u32[]{:S(2)}) collective-permute-start(bf16[320,768]{1,0:T(8,128)(2,1)S(1)} %get-tuple-element.196), channel_id=1, source_target_pairs={{6,4},{7,5},{14,12},{15,13},{22,20},{23,21},{30,28},{31,29}} | collective-permute-start | bytes 1474568 | tf_op jit(solution)/shard_map/ppermute | solution.py:823
  310.5 23.6 %collective-permute-start.36 = (bf16[320,768]{1,0:T(8,128)(2,1)S(1)}, bf16[320,768]{1,0:T(8,128)(2,1)S(1)}, u32[]{:S(2)}, u32[]{:S(2)}) collective-permute-start(bf16[320,768]{1,0:T(8,128)(2,1)S(1)} %get-tuple-element.207), channel_id=1, source_target_pairs={{0,2},{1,3},{8,10},{9,11},{16,18},{17,19},{24,26},{25,27}} | collective-permute-start | bytes 1474568 | tf_op jit(solution)/shard_map/ppermute | solution.py:823
  311.8 22.3 %collective-permute-start.37 = (bf16[320,768]{1,0:T(8,128)(2,1)S(1)}, bf16[320,768]{1,0:T(8,128)(2,1)S(1)}, u32[]{:S(2)}, u32[]{:S(2)}) collective-permute-start(bf16[320,768]{1,0:T(8,128)(2,1)S(1)} %get-tuple-element.208), channel_id=1, source_target_pairs={{6,4},{7,5},{14,12},{15,13},{22,20},{23,21},{30,28},{31,29}} | collective-permute-start | bytes 1474568 | tf_op jit(solution)/shard_map/ppermute | solution.py:823
  326.2 18.4 %collective-permute-start.32 = (bf16[320,768]{1,0:T(8,128)(2,1)}, bf16[320,768]{1,0:T(8,128)(2,1)S(1)}, u32[]{:S(2)}, u32[]{:S(2)}) collective-permute-start(bf16[320,768]{1,0:T(8,128)(2,1)} %get-tuple-element.199), channel_id=1, source_target_pairs={{0,2},{1,3},{2,4},{3,5},{8,10},{9,11},{10,12},{11,13},{16,18},{17,... | collective-permute-start | bytes 1474568 | tf_op jit(solution)/shard_map/ppermute | solution.py:823
  331.6 15.1 %collective-permute-start.33 = (bf16[320,768]{1,0:T(8,128)(2,1)S(1)}, bf16[320,768]{1,0:T(8,128)(2,1)}, u32[]{:S(2)}, u32[]{:S(2)}) collective-permute-start(bf16[320,768]{1,0:T(8,128)(2,1)S(1)} %get-tuple-element.200), channel_id=1, source_target_pairs={{4,2},{5,3},{6,4},{7,5},{12,10},{13,11},{14,12},{15,13},{20,18},{2... | collective-permute-start | bytes 1474568 | tf_op jit(solution)/shard_map/ppermute | solution.py:823
  349.3 28.0 %copy-start.19 = (bf16[768]{0:T(1024)(128)(2,1)S(1)}, bf16[768]{0:T(1024)(128)(2,1)}, u32[]{:S(2)}) copy-start(bf16[768]{0:T(1024)(128)(2,1)} %param.18) | copy-start | bytes 4612
  349.3 28.0 %copy-start.1 = (bf16[640,768]{1,0:T(8,128)(2,1)S(1)}, bf16[640,768]{1,0:T(8,128)(2,1)}, u32[]{:S(2)}) copy-start(bf16[640,768]{1,0:T(8,128)(2,1)} %refs_0_) | copy-start | bytes 2949124
  349.3 16.2 %collective-permute-start.38 = (bf16[320,768]{1,0:T(8,128)(2,1)S(1)}, bf16[320,768]{1,0:T(8,128)(2,1)S(1)}, u32[]{:S(2)}, u32[]{:S(2)}) collective-permute-start(bf16[320,768]{1,0:T(8,128)(2,1)S(1)} %get-tuple-element.213), channel_id=1, source_target_pairs={{0,2},{1,3},{2,4},{3,5},{8,10},{9,11},{10,12},{11,13},{16,18},{17,... | collective-permute-start | bytes 1474568 | tf_op jit(solution)/shard_map/ppermute | solution.py:823
  352.9 16.0 %collective-permute-start.39 = (bf16[320,768]{1,0:T(8,128)(2,1)S(1)}, bf16[320,768]{1,0:T(8,128)(2,1)S(1)}, u32[]{:S(2)}, u32[]{:S(2)}) collective-permute-start(bf16[320,768]{1,0:T(8,128)(2,1)S(1)} %get-tuple-element.214), channel_id=1, source_target_pairs={{4,2},{5,3},{6,4},{7,5},{12,10},{13,11},{14,12},{15,13},{20,18},{2... | collective-permute-start | bytes 1474568 | tf_op jit(solution)/shard_map/ppermute | solution.py:823
  354.2 23.3 %collective-permute-start.34 = (bf16[320,768]{1,0:T(8,128)(2,1)S(1)}, bf16[320,768]{1,0:T(8,128)(2,1)S(1)}, u32[]{:S(2)}, u32[]{:S(2)}) collective-permute-start(bf16[320,768]{1,0:T(8,128)(2,1)S(1)} %get-tuple-element.203), channel_id=1, source_target_pairs={{0,2},{1,3},{2,4},{3,5},{4,6},{5,7},{8,10},{9,11},{10,12},{11,13},... | collective-permute-start | bytes 1474568 | tf_op jit(solution)/shard_map/ppermute | solution.py:823
  358.7 20.8 %collective-permute-start.35 = (bf16[320,768]{1,0:T(8,128)(2,1)S(1)}, bf16[320,768]{1,0:T(8,128)(2,1)}, u32[]{:S(2)}, u32[]{:S(2)}) collective-permute-start(bf16[320,768]{1,0:T(8,128)(2,1)S(1)} %get-tuple-element.204), channel_id=1, source_target_pairs={{2,0},{3,1},{4,2},{5,3},{6,4},{7,5},{10,8},{11,9},{12,10},{13,11},... | collective-permute-start | bytes 1474568 | tf_op jit(solution)/shard_map/ppermute | solution.py:823
  370.6 14.1 %collective-permute-start.40 = (bf16[320,768]{1,0:T(8,128)(2,1)S(1)}, bf16[320,768]{1,0:T(8,128)(2,1)}, u32[]{:S(2)}, u32[]{:S(2)}) collective-permute-start(bf16[320,768]{1,0:T(8,128)(2,1)S(1)} %get-tuple-element.219), channel_id=1, source_target_pairs={{0,2},{1,3},{2,4},{3,5},{4,6},{5,7},{8,10},{9,11},{10,12},{11,13},... | collective-permute-start | bytes 1474568 | tf_op jit(solution)/shard_map/ppermute | solution.py:823
  372.6 16.3 %collective-permute-start.41 = (bf16[320,768]{1,0:T(8,128)(2,1)S(1)}, bf16[320,768]{1,0:T(8,128)(2,1)}, u32[]{:S(2)}, u32[]{:S(2)}) collective-permute-start(bf16[320,768]{1,0:T(8,128)(2,1)S(1)} %get-tuple-element.220), channel_id=1, source_target_pairs={{2,0},{3,1},{4,2},{5,3},{6,4},{7,5},{10,8},{11,9},{12,10},{13,11},... | collective-permute-start | bytes 1474568 | tf_op jit(solution)/shard_map/ppermute | solution.py:823

commit v3 on v2

--- a/solution.py
+++ b/solution.py
@@ -762,8 +762,8 @@
     own = [(one[0], to_core(after(one[0], normed))) for one in later]
     heads = [project(normed, first_pieces, order, bias[0][0], tables, (0, 1, 2))]
     asked = [exchange(heads[0][0])]
-    suffixes = [suffix_attention(row_start, *heads[0])]
-    settled = suffixes[0]
+    settled = heads[0]
+    values_coming = []
     for g in range(1, groups_local):
         arrived = crossing(after(coming[g - 1], settled))
         pair = project(
@@ -772,8 +772,11 @@
         heads.append(pair)
         asked.append(exchange(pair[0]))
         settled = pair
-    values_coming = [send(after(one[2], coming)) for one in later]
-    asked[0] = after(asked[0], settled)
+    suffixes = [suffix_attention(after(row_start, settled), *heads[0])]
+    values_coming = [
+        send(after(one[2], asked[0][1:], asked[-1][1:], suffixes[0])) for one in later
+    ]
+    asked[0] = after(asked[0], suffixes[0])
     returned = []
     for g in range(groups_local):
         if g > 0:
@@ -781,17 +784,20 @@
         answers = prefix_attention(g, asked[g], cache, span_start, span_length)
         returned.append([answers[0]] + [to_chip(answers[s], chips - s) for s in range(1, chips)])
     crossed = to_core(after(landed, answers))
+    attention_own, attention_side = [], []
     for g in range(1, groups_local):
         arrived = crossing(after(values_coming[g - 1], answers))
         (values,) = project(
             normed, pieces_of(own[g - 1], [arrived], 2 * GW, GW), order, bias[g][1], tables, (2,)
         )
-        suffixes.append(suffix_attention(row_start, heads[g][0], heads[g][1], values))
-    attention_own, attention_side = [], []
-    for g in range(groups_local):
-        attention = merge(after(returned[g], suffixes[-1]), *suffixes[g])
-        attention_own.append(attention)
-        attention_side.append(to_side(attention))
+        parts_first = after(returned[g - 1], values)
+        attention_own.append(merge(parts_first, *suffixes[g - 1]))
+        attention_side.append(to_side(attention_own[-1]))
+        suffixes.append(
+            suffix_attention(after(row_start, attention_own[-1]), heads[g][0], heads[g][1], values)
+        )
+    attention_own.append(merge(after(returned[-1], attention_side), *suffixes[-1]))
+    attention_side.append(to_side(attention_own[-1]))
     partial = output_projection(
         place, attention_own + attention_side, dense_weight, landed, crossed, lines
     )

time: 397 us -> 393 us (0.990)
  waiting for transfers between devices: 129 us -> 124 us
    ppermute x8, waiting for transfers between devices: 19.1 us -> 25.5 us  [to_chip(): lax.ppermute(x, 'tok', [(t, (t // 2 + shift) % chips * 2 + t % 2) for t i...]
    ppermute x6, waiting for transfers between devices: 33 us -> 26.7 us  [on_device(): lax.ppermute(up, 'head', up_pairs)]
    ppermute x4, waiting for transfers between devices: 16.4 us -> 11.8 us  [to_side(): return lax.ppermute(x, 'head', [(h, h ^ 1) for h in range(head_size)])]
    unnamed x42, local copies, waits for them, and re-layouts: 7.77 us -> 3.66 us
  transfers between devices with their start and end apart: 42 -> 42, of which waited for: 21 -> 21; matrix products, arithmetic and copies ran while one was open for 7% -> 7% of each run, Pallas kernels for 37% -> 38%
where the time goes in v3:
time: 393 us; the launch traced here: 386 us
  Pallas kernels  157 us (40%)
  waiting for transfers between devices  124 us (32%)
  starting transfers between devices  65 us (17%)
  other arithmetic  25.2 us (6%)
  local copies, waits for them, and re-layouts  13.9 us (4%)
    pallas_call x2, Pallas kernels, prefix_attention(): pl.pallas_call(functools.partial(prefix_kernel, blocks), out_shape=[jax.S...  45.6 us
    pallas_call x3, Pallas kernels, project(): pl.pallas_call(functools.partial(qkv_kernel, plan, bundle), out_shape=[ou...  43 us
    ppermute x6, waiting for transfers between devices, on_device(): lax.ppermute(up, 'head', up_pairs)  26.7 us
    ppermute x8, waiting for transfers between devices, to_chip(): lax.ppermute(x, 'tok', [(t, (t // 2 + shift) % chips * 2 + t % 2) for t i...  25.5 us
    ppermute x6, starting transfers between devices, on_device(): lax.ppermute(up, 'head', up_pairs)  19.4 us
    pallas_call x2, Pallas kernels, part_by_part(): pl.pallas_call(functools.partial(part_kernel, bundles), out_shape=[jax.Sh...  19.3 us
    ppermute x2, waiting for transfers between devices, to_side_from(): lax.ppermute(x, 'head', [(h, h ^ 1) for h in range(head_size) if lowest <...  18.6 us
    pallas_call x2, Pallas kernels, suffix_attention(): pl.pallas_call(suffix_kernel, out_shape=(jax.ShapeDtypeStruct((rows, GW),...  15.3 us
  transfers between devices with their start and end apart: 42, of which 21 were waited for; matrix products, arithmetic and copies ran while one was open for 7% of the time, Pallas kernels for 38%

profile of v3, /device:TPU:14, one launch (start us, length us, event | category | flops | bytes accessed | tf_op | source)
XLA Modules:
  0.0 385.9 jit_solution(1084817812859300885)
XLA Ops:
  0.0 3.5 collective-permute-start.2
  3.5 2.4 collective-permute-start.3
  10.0 1.8 constant_dynamic-slice_fusion.1
  11.8 9.3 %parts.2.refs_0_ = bf16[1536,1152]{1,0:T(8,128)(2,1)} custom-call(bf16[1536,2304]{1,0:T(8,128)(2,1)} %wide.2), custom_call_target="tpu_custom_call" | custom-call | flops 1000 | bytes 1000 | tf_op jit(solution)/shard_map/parts/pallas_call | solution.py:164
  21.2 1.5 collective-permute-start.1
  22.7 10.0 %parts.3 = (bf16[1536,1152]{1,0:T(8,128)(2,1)}, bf16[1536,768]{1,0:T(8,128)(2,1)}, bf16[1536,384]{1,0:T(8,128)(2,1)}) custom-call(bf16[1536,2304]{1,0:T(8,128)(2,1)} %wide.2), custom_call_target="tpu_custom_call" | custom-call | flops 1000 | bytes 1000 | tf_op jit(solution)/shard_map/parts/pallas_call | solution.py:164
  33.6 3.5 collective-permute-start.5
  37.1 1.9 collective-permute-start.6
  39.0 3.4 collective-permute-start.7
  42.7 2.4 collective-permute-start.8
  45.8 4.6 %multiply_sine_fusion = (f32[640,384]{1,0:T(8,128)}, f32[640,384]{1,0:T(8,128)}) fusion(f32[384]{0:T(512)S(1)} %mul.193, f32[640]{0:T(1024)S(1)} %add_convert_fusion), kind=kLoop, calls=%fused_computation.2 | loop fusion | flops 245760 | bytes 1970176 | tf_op jit(solution)/shard_map/sin | solution.py:136
  50.4 1.6 pad_maximum_fusion
  52.0 5.0 %collective-permute-done.5.refs_6_ = bf16[640,768]{1,0:T(8,128)(2,1)S(1)} collective-permute-done((bf16[640,768]{1,0:T(8,128)(2,1)}, bf16[640,768]{1,0:T(8,128)(2,1)S(1)}, u32[]{:S(2)}, u32[]{:S(2)}) %collective-permute-start.5) | collective-permute-done | bytes 983072 | tf_op jit(solution)/shard_map/ppermute | solution.py:645
  56.9 4.2 %collective-permute-done.6.refs_7_ = bf16[640,768]{1,0:T(8,128)(2,1)} collective-permute-done((bf16[640,768]{1,0:T(8,128)(2,1)}, bf16[640,768]{1,0:T(8,128)(2,1)}, u32[]{:S(2)}, u32[]{:S(2)}) %collective-permute-start.6) | collective-permute-done | bytes 983072 | tf_op jit(solution)/shard_map/ppermute | solution.py:648
  61.2 4.8 %collective-permute-done.7.refs_4_ = bf16[640,768]{1,0:T(8,128)(2,1)} collective-permute-done((bf16[640,768]{1,0:T(8,128)(2,1)}, bf16[640,768]{1,0:T(8,128)(2,1)}, u32[]{:S(2)}, u32[]{:S(2)}) %collective-permute-start.7) | collective-permute-done | bytes 983072 | tf_op jit(solution)/shard_map/ppermute | solution.py:625
  66.6 1.4 collective-permute-start.11
  68.0 2.3 broadcast_select_fusion.1
  70.3 13.8 %collective-permute-done.8.refs_5_ = bf16[640,768]{1,0:T(8,128)(2,1)} collective-permute-done((bf16[640,768]{1,0:T(8,128)(2,1)}, bf16[640,768]{1,0:T(8,128)(2,1)}, u32[]{:S(2)}, u32[]{:S(2)}) %collective-permute-start.8) | collective-permute-done | bytes 983072 | tf_op jit(solution)/shard_map/ppermute | solution.py:625
  84.1 1.5 collective-permute-start.9
  90.3 15.0 %collective-permute-done.9.refs_8_ = bf16[640,768]{1,0:T(8,128)(2,1)} collective-permute-done((bf16[640,768]{1,0:T(8,128)(2,1)}, bf16[640,768]{1,0:T(8,128)(2,1)}, u32[]{:S(2)}, u32[]{:S(2)}) %collective-permute-start.9) | collective-permute-done | bytes 983072 | tf_op jit(solution)/shard_map/ppermute | solution.py:668
  109.5 14.4 %norm.1.normed = bf16[640,6144]{1,0:T(8,128)(2,1)} custom-call(s32[12]{0:T(128)} %stack.123.places, bf16[640,768]{1,0:T(8,128)(2,1)} %refs_0_, bf16[640,768]{1,0:T(8,128)(2,1)} %collective-permute-done.4.refs_1_, bf16[640,768]{1,0:T(8,128)(2,1)} %copy-done.9, bf16[640,768]{1,0:T(8,128)(2,1)} %collective-permute-done.3.refs_3_, ...), custom_call_target="tpu_custom_call" | custom-call | flops 1000 | bytes 1000 | tf_op jit(solution)/shard_map/norm/pallas_call | solution.py:95
  124.1 19.2 %project.3 = (bf16[640,384]{1,0:T(8,128)(2,1)}, bf16[640,384]{1,0:T(8,128)(2,1)}, bf16[640,384]{1,0:T(8,128)(2,1)}) custom-call(s32[4]{0:T(128)} %pad_add_fusion.4.order, bf16[640,6144]{1,0:T(8,128)(2,1)} %norm.1.normed, bf16[1536,1152]{1,0:T(8,128)(2,1)} %parts.2.refs_0_, bf16[1536,1152]{1,0:T(8,128)(2,1)} %collective-permute-done.13.refs_1_, ...), custom_call_target="tpu_custom_call" | custom-call | flops 1000 | bytes 1000 | tf_op jit(solution)/shard_map/project/pallas_call | solution.py:261
  143.4 19.5 %collective-permute-done.17.refs_2_ = bf16[1536,768]{1,0:T(8,128)(2,1)} collective-permute-done((bf16[1536,768]{1,0:T(8,128)(2,1)}, bf16[1536,768]{1,0:T(8,128)(2,1)}, u32[]{:S(2)}, u32[]{:S(2)}) %collective-permute-start.17) | collective-permute-done | bytes 2359328 | tf_op jit(solution)/shard_map/ppermute | solution.py:605
  162.9 1.5 collective-permute-start.28
  164.9 2.9 collective-permute-done.18.refs_3_
  167.7 14.2 %project.4 = (bf16[640,384]{1,0:T(8,128)(2,1)}, bf16[640,384]{1,0:T(8,128)(2,1)}) custom-call(s32[4]{0:T(128)} %pad_add_fusion.4.order, bf16[640,6144]{1,0:T(8,128)(2,1)} %norm.1.normed, bf16[1536,1152]{1,0:T(8,128)(2,1)} %get-tuple-element.163.refs_0_, bf16[1536,1152]{1,0:T(8,128)(2,1)} %copy-done.1, bf16[1536,768]{1,0:T(8,128)(2,1)} %collective-permute-done.17.refs_2_, ...), custom_call_target="tpu_custom_call" | custom-call | flops 1000 | bytes 1000 | tf_op jit(solution)/shard_map/project/pallas_call | solution.py:261
  183.4 7.6 %suffix.2 = (f32[640,384]{1,0:T(8,128)}, f32[640,128]{1,0:T(8,128)}) custom-call(s32[640,1]{1,0:T(8,128)} %copy.25.row_start, bf16[640,384]{1,0:T(8,128)(2,1)} %get-tuple-element.175.queries.refs_0_, bf16[640,384]{1,0:T(8,128)(2,1)} %get-tuple-element.166.keys, bf16[640,384]{1,0:T(8,128)(2,1)} %get-tuple-element.167.values), custom_call_target="tpu_custom_call" | custom-call | flops 1000 | bytes 1000 | tf_op jit(solution)/shard_map/suffix/pallas_call | solution.py:461
  191.0 4.5 %collective-permute-done.22.refs_1_ = bf16[640,384]{1,0:T(8,128)(2,1)S(1)} collective-permute-done((bf16[640,384]{1,0:T(8,128)(2,1)}, bf16[640,384]{1,0:T(8,128)(2,1)S(1)}, u32[]{:S(2)}, u32[]{:S(2)}) %collective-permute-start.22) | collective-permute-done | bytes 491552 | tf_op jit(solution)/shard_map/ppermute | solution.py:605
  195.9 22.7 %prefix.2 = (bf16[640,512]{1,0:T(8,128)(2,1)}, bf16[640,512]{1,0:T(8,128)(2,1)}) custom-call(s32[8]{0:T(128)} %reshape_squeeze.6.starts, s32[8]{0:T(128)} %reshape_squeeze.7.lengths, bf16[640,384]{1,0:T(8,128)(2,1)} %get-tuple-element.175.queries.refs_0_, bf16[640,384]{1,0:T(8,128)(2,1)} %copy-done.13, bf16[2,2048,768]{2,1,0:T(8,128)(2,1)} %refs_2_.3, ...), custom_call_target="tpu_custom_call" | custom-call | flops 1000 | bytes 1000 | tf_op jit(solution)/shard_map/prefix/pallas_call | solution.py:403
  218.7 22.9 %prefix.3 = (bf16[640,512]{1,0:T(8,128)(2,1)}, bf16[640,512]{1,0:T(8,128)(2,1)}) custom-call(s32[8]{0:T(128)} %reshape_squeeze.6.starts, s32[8]{0:T(128)} %reshape_squeeze.7.lengths, bf16[640,384]{1,0:T(8,128)(2,1)} %get-tuple-element.183.refs_0_.queries, bf16[640,384]{1,0:T(8,128)(2,1)} %copy-done.14, bf16[2,2048,768]{2,1,0:T(8,128)(2,1)} %refs_2_.3, ...), custom_call_target="tpu_custom_call" | custom-call | flops 1000 | bytes 1000 | tf_op jit(solution)/shard_map/prefix/pallas_call | solution.py:403
  242.1 2.0 collective-permute-start.25
  244.1 3.3 collective-permute-done.24.refs_3_
  248.5 9.6 %project.5.values = bf16[640,384]{1,0:T(8,128)(2,1)} custom-call(s32[4]{0:T(128)} %pad_add_fusion.4.order, bf16[640,6144]{1,0:T(8,128)(2,1)} %norm.1.normed, bf16[1536,1152]{1,0:T(8,128)(2,1)} %get-tuple-element.163.refs_0_, bf16[1536,1152]{1,0:T(8,128)(2,1)} %copy-done.1, bf16[1536,384]{1,0:T(8,128)(2,1)} %copy-done.7, bf16[1536,384]{1,0:T(8,128)(2,1)} %copy-done.8, ...), custom_call_target="tpu_custom_call" | custom-call | flops 1000 | bytes 1000 | tf_op jit(solution)/shard_map/project/pallas_call | solution.py:261
  258.1 1.6 collective-permute-done.21.refs_1_
  260.5 3.6 merge.2.refs_0_
  264.2 1.5 collective-permute-start.26
  266.6 7.6 %suffix.3 = (f32[640,384]{1,0:T(8,128)}, f32[640,128]{1,0:T(8,128)}) custom-call(s32[640,1]{1,0:T(8,128)} %copy.26.row_start, bf16[640,384]{1,0:T(8,128)(2,1)} %get-tuple-element.183.refs_0_.queries, bf16[640,384]{1,0:T(8,128)(2,1)} %get-tuple-element.171.keys, bf16[640,384]{1,0:T(8,128)(2,1)} %project.5.values), custom_call_target="tpu_custom_call" | custom-call | flops 1000 | bytes 1000 | tf_op jit(solution)/shard_map/suffix/pallas_call | solution.py:461
  274.2 2.1 collective-permute-done.26.refs_2_
  276.3 3.8 merge.3.refs_1_
  280.1 1.5 collective-permute-start.27
  281.6 9.7 %collective-permute-done.27.refs_3_ = bf16[640,384]{1,0:T(8,128)(2,1)S(1)} collective-permute-done((bf16[640,384]{1,0:T(8,128)(2,1)}, bf16[640,384]{1,0:T(8,128)(2,1)S(1)}, u32[]{:S(2)}, u32[]{:S(2)}) %collective-permute-start.27) | collective-permute-done | bytes 491552 | tf_op jit(solution)/shard_map/ppermute | solution.py:612
  292.1 12.0 %output.1 = f32[4,640,768]{2,1,0:T(8,128)} custom-call(s32[2]{0:T(128)} %pad_add_fusion.5.place, bf16[640,384]{1,0:T(8,128)(2,1)} %merge.2.refs_0_, bf16[640,384]{1,0:T(8,128)(2,1)} %merge.3.refs_1_, bf16[640,384]{1,0:T(8,128)(2,1)} %copy-done.15, bf16[640,384]{1,0:T(8,128)(2,1)} %copy-done.16, bf16[768,6144]{1,0:T(8,128)(2,1)} %refs_4_.5, ...), custom_call_target="tpu_custom_call" | custom-call | flops 1000 | bytes 1000 | tf_op jit(solution)/shard_map/output/pallas_call | solution.py:554
  304.1 2.3 fusion.13
  306.4 1.3 collective-permute-start.30
  307.7 1.5 collective-permute-start.31
  311.2 11.3 %collective-permute-done.30 = bf16[320,768]{1,0:T(8,128)(2,1)S(1)} collective-permute-done((bf16[320,768]{1,0:T(8,128)(2,1)S(1)}, bf16[320,768]{1,0:T(8,128)(2,1)S(1)}, u32[]{:S(2)}, u32[]{:S(2)}) %collective-permute-start.30) | collective-permute-done | bytes 491552 | tf_op jit(solution)/shard_map/ppermute | solution.py:829
  322.5 2.6 fusion.8
  325.1 5.3 %collective-permute-start.32 = (bf16[320,768]{1,0:T(8,128)(2,1)}, bf16[320,768]{1,0:T(8,128)(2,1)S(1)}, u32[]{:S(2)}, u32[]{:S(2)}) collective-permute-start(bf16[320,768]{1,0:T(8,128)(2,1)} %get-tuple-element.203), channel_id=1, source_target_pairs={{0,2},{1,3},{2,4},{3,5},{8,10},{9,11},{10,12},{11,13},{16,18},{17,... | collective-permute-start | bytes 1474568 | tf_op jit(solution)/shard_map/ppermute | solution.py:829
  330.4 1.3 collective-permute-start.33
  331.7 1.3 collective-permute-done.36
  333.0 7.9 %collective-permute-done.32 = bf16[320,768]{1,0:T(8,128)(2,1)S(1)} collective-permute-done((bf16[320,768]{1,0:T(8,128)(2,1)}, bf16[320,768]{1,0:T(8,128)(2,1)S(1)}, u32[]{:S(2)}, u32[]{:S(2)}) %collective-permute-start.32) | collective-permute-done | bytes 491552 | tf_op jit(solution)/shard_map/ppermute | solution.py:829
  341.2 2.7 fusion.7
  343.9 5.1 %collective-permute-start.38 = (bf16[320,768]{1,0:T(8,128)(2,1)S(1)}, bf16[320,768]{1,0:T(8,128)(2,1)S(1)}, u32[]{:S(2)}, u32[]{:S(2)}) collective-permute-start(bf16[320,768]{1,0:T(8,128)(2,1)S(1)} %get-tuple-element.217), channel_id=1, source_target_pairs={{0,2},{1,3},{2,4},{3,5},{8,10},{9,11},{10,12},{11,13},{16,18},{17,... | collective-permute-start | bytes 1474568 | tf_op jit(solution)/shard_map/ppermute | solution.py:829
  350.3 4.6 %collective-permute-start.34 = (bf16[320,768]{1,0:T(8,128)(2,1)S(1)}, bf16[320,768]{1,0:T(8,128)(2,1)S(1)}, u32[]{:S(2)}, u32[]{:S(2)}) collective-permute-start(bf16[320,768]{1,0:T(8,128)(2,1)S(1)} %get-tuple-element.207), channel_id=1, source_target_pairs={{0,2},{1,3},{2,4},{3,5},{4,6},{5,7},{8,10},{9,11},{10,12},{11,13},... | collective-permute-start | bytes 1474568 | tf_op jit(solution)/shard_map/ppermute | solution.py:829
  354.9 1.9 collective-permute-start.35
  356.8 3.9 %collective-permute-done.38 = bf16[320,768]{1,0:T(8,128)(2,1)S(1)} collective-permute-done((bf16[320,768]{1,0:T(8,128)(2,1)S(1)}, bf16[320,768]{1,0:T(8,128)(2,1)S(1)}, u32[]{:S(2)}, u32[]{:S(2)}) %collective-permute-start.38) | collective-permute-done | bytes 491552 | tf_op jit(solution)/shard_map/ppermute | solution.py:829
  360.6 4.4 %collective-permute-done.39 = bf16[320,768]{1,0:T(8,128)(2,1)S(1)} collective-permute-done((bf16[320,768]{1,0:T(8,128)(2,1)S(1)}, bf16[320,768]{1,0:T(8,128)(2,1)S(1)}, u32[]{:S(2)}, u32[]{:S(2)}) %collective-permute-start.39) | collective-permute-done | bytes 491552 | tf_op jit(solution)/shard_map/ppermute | solution.py:829
  365.0 1.8 fusion.2
  366.8 1.9 collective-permute-start.40
  368.7 4.7 %collective-permute-start.41 = (bf16[320,768]{1,0:T(8,128)(2,1)S(1)}, bf16[320,768]{1,0:T(8,128)(2,1)}, u32[]{:S(2)}, u32[]{:S(2)}) collective-permute-start(bf16[320,768]{1,0:T(8,128)(2,1)S(1)} %get-tuple-element.224), channel_id=1, source_target_pairs={{2,0},{3,1},{4,2},{5,3},{6,4},{7,5},{10,8},{11,9},{12,10},{13,11},... | collective-permute-start | bytes 1474568 | tf_op jit(solution)/shard_map/ppermute | solution.py:829
  373.6 2.1 collective-permute-done.35
  375.7 2.4 collective-permute-done.40
  378.1 4.2 %collective-permute-done.41 = bf16[320,768]{1,0:T(8,128)(2,1)} collective-permute-done((bf16[320,768]{1,0:T(8,128)(2,1)S(1)}, bf16[320,768]{1,0:T(8,128)(2,1)}, u32[]{:S(2)}, u32[]{:S(2)}) %collective-permute-start.41) | collective-permute-done | bytes 491552 | tf_op jit(solution)/shard_map/ppermute | solution.py:829
  382.3 2.4 fusion.1
  (130 shorter events, 27.1 us)
Async XLA Ops:
  0.0 32.7 %collective-permute-start.2 = (bf16[640,768]{1,0:T(8,128)(2,1)}, bf16[640,768]{1,0:T(8,128)(2,1)S(1)}, u32[]{:S(2)}, u32[]{:S(2)}) collective-permute-start(bf16[640,768]{1,0:T(8,128)(2,1)} %refs_0_), channel_id=1, source_target_pairs={{0,2},{1,3},{2,4},{3,5},{4,6},{5,7},{8,10},{9,11},{10,12},{11,13},... | collective-permute-start | bytes 2949128 | tf_op jit(solution)/shard_map/ppermute | solution.py:645
  3.5 29.2 %collective-permute-start.3 = (bf16[640,768]{1,0:T(8,128)(2,1)}, bf16[640,768]{1,0:T(8,128)(2,1)}, u32[]{:S(2)}, u32[]{:S(2)}) collective-permute-start(bf16[640,768]{1,0:T(8,128)(2,1)} %refs_0_), channel_id=1, source_target_pairs={{2,0},{3,1},{4,2},{5,3},{6,4},{7,5},{10,8},{11,9},{12,10},{13,11},... | collective-permute-start | bytes 2949128 | tf_op jit(solution)/shard_map/ppermute | solution.py:648
  5.9 26.8 %collective-permute-start.4 = (bf16[640,768]{1,0:T(8,128)(2,1)}, bf16[640,768]{1,0:T(8,128)(2,1)}, u32[]{:S(2)}, u32[]{:S(2)}) collective-permute-start(bf16[640,768]{1,0:T(8,128)(2,1)} %refs_0_), channel_id=1, source_target_pairs={{0,1},{1,0},{2,3},{3,2},{4,5},{5,4},{6,7},{7,6},{8,9},{9,8},{10,11... | collective-permute-start | bytes 2949128 | tf_op jit(solution)/shard_map/ppermute | solution.py:612
  7.2 14.0 %collective-permute-start = (s32[2,8]{1,0:T(2,128)S(1)}, s32[2,8]{1,0:T(2,128)S(1)}, u32[]{:S(2)}, u32[]{:S(2)}) collective-permute-start(s32[2,8]{1,0:T(2,128)S(1)} %pad_add_fusion.1), channel_id=1, source_target_pairs={{0,16},{8,24},{16,0},{24,8},{1,17},{9,25},{17,1},{25,9},{2,18},{10... | collective-permute-start | bytes 200 | tf_op jit(solution)/shard_map/ppermute | solution.py:605
  21.2 87.1 %collective-permute-start.1 = (bf16[1536,1152]{1,0:T(8,128)(2,1)}, bf16[1536,1152]{1,0:T(8,128)(2,1)}, u32[]{:S(2)}, u32[]{:S(2)}) collective-permute-start(bf16[1536,1152]{1,0:T(8,128)(2,1)} %parts.2.refs_0_), channel_id=1, source_target_pairs={{0,16},{8,24},{16,0},{24,8},{1,17},{9,25},{17,1},{25,9},{2,18},{10... | collective-permute-start | bytes 10616840 | tf_op jit(solution)/shard_map/ppermute | solution.py:605
  22.7 19.9 %copy-start.17 = (bf16[2304]{0:T(1024)(128)(2,1)S(1)}, bf16[2304]{0:T(1024)(128)(2,1)}, u32[]{:S(2)}) copy-start(bf16[2304]{0:T(1024)(128)(2,1)} %param.16) | copy-start | bytes 13828
  32.7 0.9 copy-start.9
  33.6 23.3 %collective-permute-start.5 = (bf16[640,768]{1,0:T(8,128)(2,1)}, bf16[640,768]{1,0:T(8,128)(2,1)S(1)}, u32[]{:S(2)}, u32[]{:S(2)}) collective-permute-start(bf16[640,768]{1,0:T(8,128)(2,1)} %copy-done.9), channel_id=1, source_target_pairs={{2,4},{3,5},{4,6},{5,7},{10,12},{11,13},{12,14},{13,15},{18,20},{1... | collective-permute-start | bytes 2949128 | tf_op jit(solution)/shard_map/ppermute | solution.py:645
  37.1 24.1 %collective-permute-start.6 = (bf16[640,768]{1,0:T(8,128)(2,1)}, bf16[640,768]{1,0:T(8,128)(2,1)}, u32[]{:S(2)}, u32[]{:S(2)}) collective-permute-start(bf16[640,768]{1,0:T(8,128)(2,1)} %collective-permute-done.3.refs_3_), channel_id=1, source_target_pairs={{2,0},{3,1},{4,2},{5,3},{10,8},{11,9},{12,10},{13,11},{18,16},{19,... | collective-permute-start | bytes 2949128 | tf_op jit(solution)/shard_map/ppermute | solution.py:648
  39.0 26.9 %collective-permute-start.7 = (bf16[640,768]{1,0:T(8,128)(2,1)}, bf16[640,768]{1,0:T(8,128)(2,1)}, u32[]{:S(2)}, u32[]{:S(2)}) collective-permute-start(bf16[640,768]{1,0:T(8,128)(2,1)} %copy-done.9), channel_id=1, source_target_pairs={{2,3},{3,2},{4,5},{5,4},{6,7},{7,6},{10,11},{11,10},{12,13},{13,12... | collective-permute-start | bytes 2949128 | tf_op jit(solution)/shard_map/ppermute | solution.py:625
  42.7 41.4 %collective-permute-start.8 = (bf16[640,768]{1,0:T(8,128)(2,1)}, bf16[640,768]{1,0:T(8,128)(2,1)}, u32[]{:S(2)}, u32[]{:S(2)}) collective-permute-start(bf16[640,768]{1,0:T(8,128)(2,1)} %collective-permute-done.3.refs_3_), channel_id=1, source_target_pairs={{0,1},{1,0},{2,3},{3,2},{4,5},{5,4},{8,9},{9,8},{10,11},{11,10},{1... | collective-permute-start | bytes 2949128 | tf_op jit(solution)/shard_map/ppermute | solution.py:625
  52.0 54.2 %copy-start.19 = (s32[8]{0:T(128)S(1)}, s32[8]{0:T(128)}, u32[]{:S(2)}) copy-start(s32[8]{0:T(128)} %param.23) | copy-start | bytes 100
  56.9 33.4 %copy-start.3 = (bf16[640,768]{1,0:T(8,128)(2,1)}, bf16[640,768]{1,0:T(8,128)(2,1)S(1)}, u32[]{:S(2)}) copy-start(bf16[640,768]{1,0:T(8,128)(2,1)S(1)} %collective-permute-done.5.refs_6_) | copy-start | bytes 2949124
  65.9 23.2 %collective-permute-start.10 = (bf16[640,768]{1,0:T(8,128)(2,1)S(1)}, bf16[640,768]{1,0:T(8,128)(2,1)S(1)}, u32[]{:S(2)}, u32[]{:S(2)}) collective-permute-start(bf16[640,768]{1,0:T(8,128)(2,1)S(1)} %collective-permute-done.5.refs_6_), channel_id=1, source_target_pairs={{4,6},{5,7},{12,14},{13,15},{20,22},{21,23},{28,30},{29,31}} | collective-permute-start | bytes 2949128 | tf_op jit(solution)/shard_map/ppermute | solution.py:645
  66.6 22.5 %collective-permute-start.11 = (bf16[640,768]{1,0:T(8,128)(2,1)}, bf16[640,768]{1,0:T(8,128)(2,1)S(1)}, u32[]{:S(2)}, u32[]{:S(2)}) collective-permute-start(bf16[640,768]{1,0:T(8,128)(2,1)} %collective-permute-done.6.refs_7_), channel_id=1, source_target_pairs={{2,0},{3,1},{10,8},{11,9},{18,16},{19,17},{26,24},{27,25}} | collective-permute-start | bytes 2949128 | tf_op jit(solution)/shard_map/ppermute | solution.py:648
  84.1 21.2 %collective-permute-start.9 = (bf16[640,768]{1,0:T(8,128)(2,1)}, bf16[640,768]{1,0:T(8,128)(2,1)}, u32[]{:S(2)}, u32[]{:S(2)}) collective-permute-start(bf16[640,768]{1,0:T(8,128)(2,1)} %broadcast_select_fusion.1), channel_id=1, source_target_pairs={{0,1},{1,0},{2,3},{3,2},{4,5},{5,4},{6,7},{7,6},{8,9},{9,8},{10,11... | collective-permute-start | bytes 2949128 | tf_op jit(solution)/shard_map/ppermute | solution.py:668
  89.1 34.8 %collective-permute-start.13 = (bf16[1536,1152]{1,0:T(8,128)(2,1)}, bf16[1536,1152]{1,0:T(8,128)(2,1)}, u32[]{:S(2)}, u32[]{:S(2)}) collective-permute-start(bf16[1536,1152]{1,0:T(8,128)(2,1)} %parts.2.refs_0_), channel_id=1, source_target_pairs={{0,8},{8,0},{16,24},{24,16},{1,9},{9,1},{17,25},{25,17},{2,10},{10... | collective-permute-start | bytes 10616840 | tf_op jit(solution)/shard_map/ppermute | solution.py:602
  89.2 20.3 %copy-start.4 = (bf16[640,768]{1,0:T(8,128)(2,1)}, bf16[640,768]{1,0:T(8,128)(2,1)S(1)}, u32[]{:S(2)}) copy-start(bf16[640,768]{1,0:T(8,128)(2,1)S(1)} %collective-permute-done.10.refs_9_) | copy-start | bytes 2949124
  89.2 20.3 %copy-start.5 = (bf16[640,768]{1,0:T(8,128)(2,1)}, bf16[640,768]{1,0:T(8,128)(2,1)S(1)}, u32[]{:S(2)}) copy-start(bf16[640,768]{1,0:T(8,128)(2,1)S(1)} %collective-permute-done.11.refs_10_) | copy-start | bytes 2949124
  105.3 3.0 collective-permute-start.12
  108.3 1.2 copy-start.10
  108.3 15.8 %collective-permute-start.14 = (bf16[1536,1152]{1,0:T(8,128)(2,1)}, bf16[1536,1152]{1,0:T(8,128)(2,1)}, u32[]{:S(2)}, u32[]{:S(2)}) collective-permute-start(bf16[1536,1152]{1,0:T(8,128)(2,1)} %collective-permute-done.1.refs_2_), channel_id=1, source_target_pairs={{0,8},{8,0},{16,24},{24,16},{1,9},{9,1},{17,25},{25,17},{2,10},{10... | collective-permute-start | bytes 10616840 | tf_op jit(solution)/shard_map/ppermute | solution.py:602
  108.4 87.6 %collective-permute-start.19 = (bf16[2,2048,768]{2,1,0:T(8,128)(2,1)}, bf16[2,2048,768]{2,1,0:T(8,128)(2,1)}, u32[]{:S(2)}, u32[]{:S(2)}) collective-permute-start(bf16[2,2048,768]{2,1,0:T(8,128)(2,1)} %refs_2_.3), channel_id=1, source_target_pairs={{0,8},{8,0},{16,24},{24,16},{1,9},{9,1},{17,25},{25,17},{2,10},{10... | collective-permute-start | bytes 18874376 | tf_op jit(solution)/shard_map/ppermute | solution.py:602
  108.9 87.1 %collective-permute-start.20 = (bf16[2,2048,768]{2,1,0:T(8,128)(2,1)}, bf16[2,2048,768]{2,1,0:T(8,128)(2,1)}, u32[]{:S(2)}, u32[]{:S(2)}) collective-permute-start(bf16[2,2048,768]{2,1,0:T(8,128)(2,1)} %refs_4_.4), channel_id=1, source_target_pairs={{0,8},{8,0},{16,24},{24,16},{1,9},{9,1},{17,25},{25,17},{2,10},{10... | collective-permute-start | bytes 18874376 | tf_op jit(solution)/shard_map/ppermute | solution.py:602
  108.9 53.9 %collective-permute-start.17 = (bf16[1536,768]{1,0:T(8,128)(2,1)}, bf16[1536,768]{1,0:T(8,128)(2,1)}, u32[]{:S(2)}, u32[]{:S(2)}) collective-permute-start(bf16[1536,768]{1,0:T(8,128)(2,1)} %get-tuple-element.165), channel_id=1, source_target_pairs={{0,16},{8,24},{16,0},{24,8},{1,17},{9,25},{17,1},{25,9},{2,18},{10... | collective-permute-start | bytes 7077896 | tf_op jit(solution)/shard_map/ppermute | solution.py:605
  109.5 14.4 %copy-start = (bf16[1536,1152]{1,0:T(8,128)(2,1)S(1)}, bf16[1536,1152]{1,0:T(8,128)(2,1)}, u32[]{:S(2)}) copy-start(bf16[1536,1152]{1,0:T(8,128)(2,1)} %get-tuple-element.163.refs_0_) | copy-start | bytes 10616836
  123.9 40.5 %collective-permute-start.16 = (bf16[1536,1152]{1,0:T(8,128)(2,1)S(1)}, bf16[1536,1152]{1,0:T(8,128)(2,1)S(1)}, u32[]{:S(2)}, u32[]{:S(2)}) collective-permute-start(bf16[1536,1152]{1,0:T(8,128)(2,1)S(1)} %copy-done), channel_id=1, source_target_pairs={{0,8},{8,0},{16,24},{24,16},{1,9},{9,1},{17,25},{25,17},{2,10},{10... | collective-permute-start | bytes 10616840 | tf_op jit(solution)/shard_map/ppermute | solution.py:602
  162.8 4.9 %collective-permute-start.18 = (bf16[1536,768]{1,0:T(8,128)(2,1)}, bf16[1536,768]{1,0:T(8,128)(2,1)}, u32[]{:S(2)}, u32[]{:S(2)}) collective-permute-start(bf16[1536,768]{1,0:T(8,128)(2,1)} %collective-permute-done.17.refs_2_), channel_id=1, source_target_pairs={{0,8},{8,0},{16,24},{24,16},{1,9},{9,1},{17,25},{25,17},{2,10},{10... | collective-permute-start | bytes 7077896 | tf_op jit(solution)/shard_map/ppermute | solution.py:602
  162.9 78.7 %collective-permute-start.28 = (bf16[768,1536]{1,0:T(8,128)(2,1)}, bf16[768,1536]{1,0:T(8,128)(2,1)}, u32[]{:S(2)}, u32[]{:S(2)}) collective-permute-start(bf16[768,1536]{1,0:T(8,128)(2,1)} %pad_maximum_fusion), channel_id=1, source_target_pairs={{0,1},{1,0},{2,3},{3,2},{4,5},{5,4},{6,7},{7,6},{8,9},{9,8},{10,11... | collective-permute-start | bytes 7077896 | tf_op jit(solution)/shard_map/ppermute | solution.py:612
  164.3 3.4 copy-start.1
  164.4 26.7 %collective-permute-start.15 = (bf16[640,384]{1,0:T(8,128)(2,1)}, bf16[640,384]{1,0:T(8,128)(2,1)S(1)}, u32[]{:S(2)}, u32[]{:S(2)}) collective-permute-start(bf16[640,384]{1,0:T(8,128)(2,1)} %get-tuple-element.175.queries.refs_0_), channel_id=1, source_target_pairs={{0,16},{8,24},{16,0},{24,8},{1,17},{9,25},{17,1},{25,9},{2,18},{10... | collective-permute-start | bytes 1474568 | tf_op jit(solution)/shard_map/ppermute | solution.py:605
  181.9 13.5 %collective-permute-start.22 = (bf16[640,384]{1,0:T(8,128)(2,1)}, bf16[640,384]{1,0:T(8,128)(2,1)S(1)}, u32[]{:S(2)}, u32[]{:S(2)}) collective-permute-start(bf16[640,384]{1,0:T(8,128)(2,1)} %get-tuple-element.183.refs_0_.queries), channel_id=1, source_target_pairs={{0,16},{8,24},{16,0},{24,8},{1,17},{9,25},{17,1},{25,9},{2,18},{10... | collective-permute-start | bytes 1474568 | tf_op jit(solution)/shard_map/ppermute | solution.py:605
  191.0 4.9 %copy-start.13 = (bf16[640,384]{1,0:T(8,128)(2,1)}, bf16[640,384]{1,0:T(8,128)(2,1)S(1)}, u32[]{:S(2)}) copy-start(bf16[640,384]{1,0:T(8,128)(2,1)S(1)} %collective-permute-done.15.refs_1_) | copy-start | bytes 1474564
  195.5 23.2 %copy-start.14 = (bf16[640,384]{1,0:T(8,128)(2,1)}, bf16[640,384]{1,0:T(8,128)(2,1)S(1)}, u32[]{:S(2)}) copy-start(bf16[640,384]{1,0:T(8,128)(2,1)S(1)} %collective-permute-done.22.refs_1_) | copy-start | bytes 1474564
  195.5 46.1 %collective-permute-start.23 = (bf16[1536,384]{1,0:T(8,128)(2,1)}, bf16[1536,384]{1,0:T(8,128)(2,1)S(1)}, u32[]{:S(2)}, u32[]{:S(2)}) collective-permute-start(bf16[1536,384]{1,0:T(8,128)(2,1)} %get-tuple-element.182), channel_id=1, source_target_pairs={{0,16},{8,24},{16,0},{24,8},{1,17},{9,25},{17,1},{25,9},{2,18},{10... | collective-permute-start | bytes 3538952 | tf_op jit(solution)/shard_map/ppermute | solution.py:605
  218.7 23.5 %copy-start.20 = (bf16[640,512]{1,0:T(8,128)(2,1)S(1)}, bf16[640,512]{1,0:T(8,128)(2,1)}, u32[]{:S(2)}) copy-start(bf16[640,512]{1,0:T(8,128)(2,1)} %get-tuple-element.180) | copy-start | bytes 1966084
  241.5 40.1 %collective-permute-start.29 = (bf16[768,1536]{1,0:T(8,128)(2,1)}, bf16[768,1536]{1,0:T(8,128)(2,1)S(1)}, u32[]{:S(2)}, u32[]{:S(2)}) collective-permute-start(bf16[768,1536]{1,0:T(8,128)(2,1)} %collective-permute-done.28.refs_5_), channel_id=1, source_target_pairs={{0,8},{8,0},{16,24},{24,16},{1,9},{9,1},{17,25},{25,17},{2,10},{10... | collective-permute-start | bytes 7077896 | tf_op jit(solution)/shard_map/ppermute | solution.py:602
  241.6 5.8 %copy-start.7 = (bf16[1536,384]{1,0:T(8,128)(2,1)}, bf16[1536,384]{1,0:T(8,128)(2,1)S(1)}, u32[]{:S(2)}) copy-start(bf16[1536,384]{1,0:T(8,128)(2,1)S(1)} %collective-permute-done.23.refs_2_) | copy-start | bytes 3538948
  241.6 5.8 %collective-permute-start.24 = (bf16[1536,384]{1,0:T(8,128)(2,1)S(1)}, bf16[1536,384]{1,0:T(8,128)(2,1)S(1)}, u32[]{:S(2)}, u32[]{:S(2)}) collective-permute-start(bf16[1536,384]{1,0:T(8,128)(2,1)S(1)} %collective-permute-done.23.refs_2_), channel_id=1, source_target_pairs={{0,8},{8,0},{16,24},{24,16},{1,9},{9,1},{17,25},{25,17},{2,10},{10... | collective-permute-start | bytes 3538952 | tf_op jit(solution)/shard_map/ppermute | solution.py:602
  242.1 17.6 %collective-permute-start.21 = (bf16[640,512]{1,0:T(8,128)(2,1)S(1)}, bf16[640,512]{1,0:T(8,128)(2,1)S(1)}, u32[]{:S(2)}, u32[]{:S(2)}) collective-permute-start(bf16[640,512]{1,0:T(8,128)(2,1)S(1)} %copy-done.20), channel_id=1, source_target_pairs={{0,16},{8,24},{16,0},{24,8},{1,17},{9,25},{17,1},{25,9},{2,18},{10... | collective-permute-start | bytes 1966088 | tf_op jit(solution)/shard_map/ppermute | solution.py:605
  242.1 32.1 %collective-permute-start.25 = (bf16[640,512]{1,0:T(8,128)(2,1)}, bf16[640,512]{1,0:T(8,128)(2,1)S(1)}, u32[]{:S(2)}, u32[]{:S(2)}) collective-permute-start(bf16[640,512]{1,0:T(8,128)(2,1)} %get-tuple-element.186), channel_id=1, source_target_pairs={{0,16},{8,24},{16,0},{24,8},{1,17},{9,25},{17,1},{25,9},{2,18},{10... | collective-permute-start | bytes 1966088 | tf_op jit(solution)/shard_map/ppermute | solution.py:605
  247.5 1.0 copy-start.8
  259.7 0.8 copy-start.12
  264.2 12.1 %collective-permute-start.26 = (bf16[640,384]{1,0:T(8,128)(2,1)}, bf16[640,384]{1,0:T(8,128)(2,1)S(1)}, u32[]{:S(2)}, u32[]{:S(2)}) collective-permute-start(bf16[640,384]{1,0:T(8,128)(2,1)} %merge.2.refs_0_), channel_id=1, source_target_pairs={{0,1},{1,0},{2,3},{3,2},{4,5},{5,4},{6,7},{7,6},{8,9},{9,8},{10,11... | collective-permute-start | bytes 1474568 | tf_op jit(solution)/shard_map/ppermute | solution.py:612
  274.2 2.1 copy-start.11
  276.3 15.0 %copy-start.15 = (bf16[640,384]{1,0:T(8,128)(2,1)}, bf16[640,384]{1,0:T(8,128)(2,1)S(1)}, u32[]{:S(2)}) copy-start(bf16[640,384]{1,0:T(8,128)(2,1)S(1)} %collective-permute-done.26.refs_2_) | copy-start | bytes 1474564
  280.1 11.2 %collective-permute-start.27 = (bf16[640,384]{1,0:T(8,128)(2,1)}, bf16[640,384]{1,0:T(8,128)(2,1)S(1)}, u32[]{:S(2)}, u32[]{:S(2)}) collective-permute-start(bf16[640,384]{1,0:T(8,128)(2,1)} %merge.3.refs_1_), channel_id=1, source_target_pairs={{0,1},{1,0},{2,3},{3,2},{4,5},{5,4},{6,7},{7,6},{8,9},{9,8},{10,11... | collective-permute-start | bytes 1474568 | tf_op jit(solution)/shard_map/ppermute | solution.py:612
  281.6 9.7 %copy-start.6 = (bf16[768,1536]{1,0:T(8,128)(2,1)}, bf16[768,1536]{1,0:T(8,128)(2,1)S(1)}, u32[]{:S(2)}) copy-start(bf16[768,1536]{1,0:T(8,128)(2,1)S(1)} %collective-permute-done.29.refs_6_) | copy-start | bytes 7077892
  291.3 0.8 copy-start.16
  306.4 16.1 %collective-permute-start.30 = (bf16[320,768]{1,0:T(8,128)(2,1)S(1)}, bf16[320,768]{1,0:T(8,128)(2,1)S(1)}, u32[]{:S(2)}, u32[]{:S(2)}) collective-permute-start(bf16[320,768]{1,0:T(8,128)(2,1)S(1)} %get-tuple-element.199), channel_id=1, source_target_pairs={{0,2},{1,3},{8,10},{9,11},{16,18},{17,19},{24,26},{25,27}} | collective-permute-start | bytes 1474568 | tf_op jit(solution)/shard_map/ppermute | solution.py:829
  307.7 14.8 %collective-permute-start.31 = (bf16[320,768]{1,0:T(8,128)(2,1)S(1)}, bf16[320,768]{1,0:T(8,128)(2,1)}, u32[]{:S(2)}, u32[]{:S(2)}) collective-permute-start(bf16[320,768]{1,0:T(8,128)(2,1)S(1)} %get-tuple-element.200), channel_id=1, source_target_pairs={{6,4},{7,5},{14,12},{15,13},{22,20},{23,21},{30,28},{31,29}} | collective-permute-start | bytes 1474568 | tf_op jit(solution)/shard_map/ppermute | solution.py:829
  309.2 23.8 %collective-permute-start.36 = (bf16[320,768]{1,0:T(8,128)(2,1)S(1)}, bf16[320,768]{1,0:T(8,128)(2,1)S(1)}, u32[]{:S(2)}, u32[]{:S(2)}) collective-permute-start(bf16[320,768]{1,0:T(8,128)(2,1)S(1)} %get-tuple-element.211), channel_id=1, source_target_pairs={{0,2},{1,3},{8,10},{9,11},{16,18},{17,19},{24,26},{25,27}} | collective-permute-start | bytes 1474568 | tf_op jit(solution)/shard_map/ppermute | solution.py:829
  310.5 22.5 %collective-permute-start.37 = (bf16[320,768]{1,0:T(8,128)(2,1)S(1)}, bf16[320,768]{1,0:T(8,128)(2,1)S(1)}, u32[]{:S(2)}, u32[]{:S(2)}) collective-permute-start(bf16[320,768]{1,0:T(8,128)(2,1)S(1)} %get-tuple-element.212), channel_id=1, source_target_pairs={{6,4},{7,5},{14,12},{15,13},{22,20},{23,21},{30,28},{31,29}} | collective-permute-start | bytes 1474568 | tf_op jit(solution)/shard_map/ppermute | solution.py:829
  325.1 15.8 %collective-permute-start.32 = (bf16[320,768]{1,0:T(8,128)(2,1)}, bf16[320,768]{1,0:T(8,128)(2,1)S(1)}, u32[]{:S(2)}, u32[]{:S(2)}) collective-permute-start(bf16[320,768]{1,0:T(8,128)(2,1)} %get-tuple-element.203), channel_id=1, source_target_pairs={{0,2},{1,3},{2,4},{3,5},{8,10},{9,11},{10,12},{11,13},{16,18},{17,... | collective-permute-start | bytes 1474568 | tf_op jit(solution)/shard_map/ppermute | solution.py:829
  330.4 10.8 %collective-permute-start.33 = (bf16[320,768]{1,0:T(8,128)(2,1)S(1)}, bf16[320,768]{1,0:T(8,128)(2,1)}, u32[]{:S(2)}, u32[]{:S(2)}) collective-permute-start(bf16[320,768]{1,0:T(8,128)(2,1)S(1)} %get-tuple-element.204), channel_id=1, source_target_pairs={{4,2},{5,3},{6,4},{7,5},{12,10},{13,11},{14,12},{15,13},{20,18},{2... | collective-permute-start | bytes 1474568 | tf_op jit(solution)/shard_map/ppermute | solution.py:829
  343.9 29.6 %copy-start.18 = (bf16[768]{0:T(1024)(128)(2,1)S(1)}, bf16[768]{0:T(1024)(128)(2,1)}, u32[]{:S(2)}) copy-start(bf16[768]{0:T(1024)(128)(2,1)} %param.18) | copy-start | bytes 4612
  343.9 29.6 %copy-start.2 = (bf16[640,768]{1,0:T(8,128)(2,1)S(1)}, bf16[640,768]{1,0:T(8,128)(2,1)}, u32[]{:S(2)}) copy-start(bf16[640,768]{1,0:T(8,128)(2,1)} %refs_0_) | copy-start | bytes 2949124
  343.9 16.7 %collective-permute-start.38 = (bf16[320,768]{1,0:T(8,128)(2,1)S(1)}, bf16[320,768]{1,0:T(8,128)(2,1)S(1)}, u32[]{:S(2)}, u32[]{:S(2)}) collective-permute-start(bf16[320,768]{1,0:T(8,128)(2,1)S(1)} %get-tuple-element.217), channel_id=1, source_target_pairs={{0,2},{1,3},{2,4},{3,5},{8,10},{9,11},{10,12},{11,13},{16,18},{17,... | collective-permute-start | bytes 1474568 | tf_op jit(solution)/shard_map/ppermute | solution.py:829
  349.0 16.1 %collective-permute-start.39 = (bf16[320,768]{1,0:T(8,128)(2,1)S(1)}, bf16[320,768]{1,0:T(8,128)(2,1)S(1)}, u32[]{:S(2)}, u32[]{:S(2)}) collective-permute-start(bf16[320,768]{1,0:T(8,128)(2,1)S(1)} %get-tuple-element.218), channel_id=1, source_target_pairs={{4,2},{5,3},{6,4},{7,5},{12,10},{13,11},{14,12},{15,13},{20,18},{2... | collective-permute-start | bytes 1474568 | tf_op jit(solution)/shard_map/ppermute | solution.py:829
  350.3 23.3 %collective-permute-start.34 = (bf16[320,768]{1,0:T(8,128)(2,1)S(1)}, bf16[320,768]{1,0:T(8,128)(2,1)S(1)}, u32[]{:S(2)}, u32[]{:S(2)}) collective-permute-start(bf16[320,768]{1,0:T(8,128)(2,1)S(1)} %get-tuple-element.207), channel_id=1, source_target_pairs={{0,2},{1,3},{2,4},{3,5},{4,6},{5,7},{8,10},{9,11},{10,12},{11,13},... | collective-permute-start | bytes 1474568 | tf_op jit(solution)/shard_map/ppermute | solution.py:829
  354.9 20.8 %collective-permute-start.35 = (bf16[320,768]{1,0:T(8,128)(2,1)S(1)}, bf16[320,768]{1,0:T(8,128)(2,1)}, u32[]{:S(2)}, u32[]{:S(2)}) collective-permute-start(bf16[320,768]{1,0:T(8,128)(2,1)S(1)} %get-tuple-element.208), channel_id=1, source_target_pairs={{2,0},{3,1},{4,2},{5,3},{6,4},{7,5},{10,8},{11,9},{12,10},{13,11},... | collective-permute-start | bytes 1474568 | tf_op jit(solution)/shard_map/ppermute | solution.py:829
  366.8 11.3 %collective-permute-start.40 = (bf16[320,768]{1,0:T(8,128)(2,1)S(1)}, bf16[320,768]{1,0:T(8,128)(2,1)}, u32[]{:S(2)}, u32[]{:S(2)}) collective-permute-start(bf16[320,768]{1,0:T(8,128)(2,1)S(1)} %get-tuple-element.223), channel_id=1, source_target_pairs={{0,2},{1,3},{2,4},{3,5},{4,6},{5,7},{8,10},{9,11},{10,12},{11,13},... | collective-permute-start | bytes 1474568 | tf_op jit(solution)/shard_map/ppermute | solution.py:829
  368.7 13.6 %collective-permute-start.41 = (bf16[320,768]{1,0:T(8,128)(2,1)S(1)}, bf16[320,768]{1,0:T(8,128)(2,1)}, u32[]{:S(2)}, u32[]{:S(2)}) collective-permute-start(bf16[320,768]{1,0:T(8,128)(2,1)S(1)} %get-tuple-element.224), channel_id=1, source_target_pairs={{2,0},{3,1},{4,2},{5,3},{6,4},{7,5},{10,8},{11,9},{12,10},{13,11},... | collective-permute-start | bytes 1474568 | tf_op jit(solution)/shard_map/ppermute | solution.py:829

commit v4 on v3

--- a/solution.py
+++ b/solution.py
@@ -786,7 +786,7 @@
     crossed = to_core(after(landed, answers))
     attention_own, attention_side = [], []
     for g in range(1, groups_local):
-        arrived = crossing(after(values_coming[g - 1], answers))
+        arrived = crossing(after(values_coming[g - 1], answers, returned[g - 1][1:]))
         (values,) = project(
             normed, pieces_of(own[g - 1], [arrived], 2 * GW, GW), order, bias[g][1], tables, (2,)
         )

time: 393 us -> 397 us (1.010)
  waiting for transfers between devices: 124 us -> 132 us
  transfers between devices with their start and end apart: 42 -> 42, of which waited for: 21 -> 20; matrix products, arithmetic and copies ran while one was open for 7% -> 7% of each run, Pallas kernels for 38% -> 37%
where the time goes in v4:
time: 397 us; the launch traced here: 392 us
  Pallas kernels  159 us (40%)
  waiting for transfers between devices  132 us (33%)
  starting transfers between devices  62.5 us (16%)
  other arithmetic  25.3 us (6%)
  local copies, waits for them, and re-layouts  13.1 us (3%)
    pallas_call x2, Pallas kernels, prefix_attention(): pl.pallas_call(functools.partial(prefix_kernel, blocks), out_shape=[jax.S...  47.2 us
    pallas_call x3, Pallas kernels, project(): pl.pallas_call(functools.partial(qkv_kernel, plan, bundle), out_shape=[ou...  43 us
    ppermute x6, waiting for transfers between devices, on_device(): lax.ppermute(up, 'head', up_pairs)  30.3 us
    ppermute x8, waiting for transfers between devices, to_chip(): lax.ppermute(x, 'tok', [(t, (t // 2 + shift) % chips * 2 + t % 2) for t i...  23.9 us
    pallas_call x2, Pallas kernels, part_by_part(): pl.pallas_call(functools.partial(part_kernel, bundles), out_shape=[jax.Sh...  19.3 us
    ppermute x6, starting transfers between devices, on_device(): lax.ppermute(up, 'head', up_pairs)  18.8 us
    ppermute x2, waiting for transfers between devices, to_side_from(): lax.ppermute(x, 'head', [(h, h ^ 1) for h in range(head_size) if lowest <...  18.6 us
    pallas_call x2, Pallas kernels, suffix_attention(): pl.pallas_call(suffix_kernel, out_shape=(jax.ShapeDtypeStruct((rows, GW),...  15.3 us
  transfers between devices with their start and end apart: 42, of which 20 were waited for; matrix products, arithmetic and copies ran while one was open for 7% of the time, Pallas kernels for 37%

profile of v4, /device:TPU:14, one launch (start us, length us, event | category | flops | bytes accessed | tf_op | source)
XLA Modules:
  0.0 391.9 jit_solution(17883660524749462401)
XLA Ops:
  0.0 3.5 collective-permute-start.2
  3.5 2.4 collective-permute-start.3
  10.0 1.8 constant_dynamic-slice_fusion.1
  11.8 9.3 %parts.2.refs_0_ = bf16[1536,1152]{1,0:T(8,128)(2,1)} custom-call(bf16[1536,2304]{1,0:T(8,128)(2,1)} %wide.2), custom_call_target="tpu_custom_call" | custom-call | flops 1000 | bytes 1000 | tf_op jit(solution)/shard_map/parts/pallas_call | solution.py:164
  21.2 1.5 collective-permute-start.1
  22.7 10.0 %parts.3 = (bf16[1536,1152]{1,0:T(8,128)(2,1)}, bf16[1536,768]{1,0:T(8,128)(2,1)}, bf16[1536,384]{1,0:T(8,128)(2,1)}) custom-call(bf16[1536,2304]{1,0:T(8,128)(2,1)} %wide.2), custom_call_target="tpu_custom_call" | custom-call | flops 1000 | bytes 1000 | tf_op jit(solution)/shard_map/parts/pallas_call | solution.py:164
  33.6 3.5 collective-permute-start.5
  37.1 1.9 collective-permute-start.6
  39.0 3.4 collective-permute-start.7
  42.7 2.4 collective-permute-start.8
  45.8 4.6 %multiply_sine_fusion = (f32[640,384]{1,0:T(8,128)}, f32[640,384]{1,0:T(8,128)}) fusion(f32[384]{0:T(512)S(1)} %mul.193, f32[640]{0:T(1024)S(1)} %add_convert_fusion), kind=kLoop, calls=%fused_computation.2 | loop fusion | flops 245760 | bytes 1970176 | tf_op jit(solution)/shard_map/sin | solution.py:136
  50.4 1.6 pad_maximum_fusion
  52.0 4.9 %collective-permute-done.5.refs_6_ = bf16[640,768]{1,0:T(8,128)(2,1)S(1)} collective-permute-done((bf16[640,768]{1,0:T(8,128)(2,1)}, bf16[640,768]{1,0:T(8,128)(2,1)S(1)}, u32[]{:S(2)}, u32[]{:S(2)}) %collective-permute-start.5) | collective-permute-done | bytes 983072 | tf_op jit(solution)/shard_map/ppermute | solution.py:645
  56.9 4.2 %collective-permute-done.6.refs_7_ = bf16[640,768]{1,0:T(8,128)(2,1)} collective-permute-done((bf16[640,768]{1,0:T(8,128)(2,1)}, bf16[640,768]{1,0:T(8,128)(2,1)}, u32[]{:S(2)}, u32[]{:S(2)}) %collective-permute-start.6) | collective-permute-done | bytes 983072 | tf_op jit(solution)/shard_map/ppermute | solution.py:648
  61.2 4.8 %collective-permute-done.7.refs_4_ = bf16[640,768]{1,0:T(8,128)(2,1)} collective-permute-done((bf16[640,768]{1,0:T(8,128)(2,1)}, bf16[640,768]{1,0:T(8,128)(2,1)}, u32[]{:S(2)}, u32[]{:S(2)}) %collective-permute-start.7) | collective-permute-done | bytes 983072 | tf_op jit(solution)/shard_map/ppermute | solution.py:625
  66.6 1.4 collective-permute-start.11
  68.0 2.3 broadcast_select_fusion.1
  70.3 13.8 %collective-permute-done.8.refs_5_ = bf16[640,768]{1,0:T(8,128)(2,1)} collective-permute-done((bf16[640,768]{1,0:T(8,128)(2,1)}, bf16[640,768]{1,0:T(8,128)(2,1)}, u32[]{:S(2)}, u32[]{:S(2)}) %collective-permute-start.8) | collective-permute-done | bytes 983072 | tf_op jit(solution)/shard_map/ppermute | solution.py:625
  84.1 1.5 collective-permute-start.9
  90.3 15.0 %collective-permute-done.9.refs_8_ = bf16[640,768]{1,0:T(8,128)(2,1)} collective-permute-done((bf16[640,768]{1,0:T(8,128)(2,1)}, bf16[640,768]{1,0:T(8,128)(2,1)}, u32[]{:S(2)}, u32[]{:S(2)}) %collective-permute-start.9) | collective-permute-done | bytes 983072 | tf_op jit(solution)/shard_map/ppermute | solution.py:668
  109.5 14.4 %norm.1.normed = bf16[640,6144]{1,0:T(8,128)(2,1)} custom-call(s32[12]{0:T(128)} %stack.123.places, bf16[640,768]{1,0:T(8,128)(2,1)} %refs_0_, bf16[640,768]{1,0:T(8,128)(2,1)} %collective-permute-done.4.refs_1_, bf16[640,768]{1,0:T(8,128)(2,1)} %copy-done.9, bf16[640,768]{1,0:T(8,128)(2,1)} %collective-permute-done.3.refs_3_, ...), custom_call_target="tpu_custom_call" | custom-call | flops 1000 | bytes 1000 | tf_op jit(solution)/shard_map/norm/pallas_call | solution.py:95
  124.1 19.2 %project.3 = (bf16[640,384]{1,0:T(8,128)(2,1)}, bf16[640,384]{1,0:T(8,128)(2,1)}, bf16[640,384]{1,0:T(8,128)(2,1)}) custom-call(s32[4]{0:T(128)} %pad_add_fusion.4.order, bf16[640,6144]{1,0:T(8,128)(2,1)} %norm.1.normed, bf16[1536,1152]{1,0:T(8,128)(2,1)} %parts.2.refs_0_, bf16[1536,1152]{1,0:T(8,128)(2,1)} %collective-permute-done.13.refs_1_, ...), custom_call_target="tpu_custom_call" | custom-call | flops 1000 | bytes 1000 | tf_op jit(solution)/shard_map/project/pallas_call | solution.py:261
  143.4 19.5 %collective-permute-done.17.refs_2_ = bf16[1536,768]{1,0:T(8,128)(2,1)} collective-permute-done((bf16[1536,768]{1,0:T(8,128)(2,1)}, bf16[1536,768]{1,0:T(8,128)(2,1)}, u32[]{:S(2)}, u32[]{:S(2)}) %collective-permute-start.17) | collective-permute-done | bytes 2359328 | tf_op jit(solution)/shard_map/ppermute | solution.py:605
  162.9 1.5 collective-permute-start.28
  164.9 2.9 collective-permute-done.18.refs_3_
  167.7 14.2 %project.4 = (bf16[640,384]{1,0:T(8,128)(2,1)}, bf16[640,384]{1,0:T(8,128)(2,1)}) custom-call(s32[4]{0:T(128)} %pad_add_fusion.4.order, bf16[640,6144]{1,0:T(8,128)(2,1)} %norm.1.normed, bf16[1536,1152]{1,0:T(8,128)(2,1)} %get-tuple-element.163.refs_0_, bf16[1536,1152]{1,0:T(8,128)(2,1)} %copy-done.1, bf16[1536,768]{1,0:T(8,128)(2,1)} %collective-permute-done.17.refs_2_, ...), custom_call_target="tpu_custom_call" | custom-call | flops 1000 | bytes 1000 | tf_op jit(solution)/shard_map/project/pallas_call | solution.py:261
  183.4 7.6 %suffix.2 = (f32[640,384]{1,0:T(8,128)}, f32[640,128]{1,0:T(8,128)}) custom-call(s32[640,1]{1,0:T(8,128)} %copy.25.row_start, bf16[640,384]{1,0:T(8,128)(2,1)} %get-tuple-element.175.queries.refs_0_, bf16[640,384]{1,0:T(8,128)(2,1)} %get-tuple-element.166.keys, bf16[640,384]{1,0:T(8,128)(2,1)} %get-tuple-element.167.values), custom_call_target="tpu_custom_call" | custom-call | flops 1000 | bytes 1000 | tf_op jit(solution)/shard_map/suffix/pallas_call | solution.py:461
  191.0 4.4 %collective-permute-done.22.refs_1_ = bf16[640,384]{1,0:T(8,128)(2,1)S(1)} collective-permute-done((bf16[640,384]{1,0:T(8,128)(2,1)}, bf16[640,384]{1,0:T(8,128)(2,1)S(1)}, u32[]{:S(2)}, u32[]{:S(2)}) %collective-permute-start.22) | collective-permute-done | bytes 491552 | tf_op jit(solution)/shard_map/ppermute | solution.py:605
  196.0 23.6 %prefix.2 = (bf16[640,512]{1,0:T(8,128)(2,1)}, bf16[640,512]{1,0:T(8,128)(2,1)}) custom-call(s32[8]{0:T(128)} %reshape_squeeze.6.starts, s32[8]{0:T(128)} %reshape_squeeze.7.lengths, bf16[640,384]{1,0:T(8,128)(2,1)} %get-tuple-element.175.queries.refs_0_, bf16[640,384]{1,0:T(8,128)(2,1)} %copy-done.13, bf16[2,2048,768]{2,1,0:T(8,128)(2,1)} %refs_2_.3, ...), custom_call_target="tpu_custom_call" | custom-call | flops 1000 | bytes 1000 | tf_op jit(solution)/shard_map/prefix/pallas_call | solution.py:403
  219.6 23.6 %prefix.3 = (bf16[640,512]{1,0:T(8,128)(2,1)}, bf16[640,512]{1,0:T(8,128)(2,1)}) custom-call(s32[8]{0:T(128)} %reshape_squeeze.6.starts, s32[8]{0:T(128)} %reshape_squeeze.7.lengths, bf16[640,384]{1,0:T(8,128)(2,1)} %get-tuple-element.183.refs_0_.queries, bf16[640,384]{1,0:T(8,128)(2,1)} %copy-done.14, bf16[2,2048,768]{2,1,0:T(8,128)(2,1)} %refs_2_.3, ...), custom_call_target="tpu_custom_call" | custom-call | flops 1000 | bytes 1000 | tf_op jit(solution)/shard_map/prefix/pallas_call | solution.py:403
  243.9 5.3 %collective-permute-done.24.refs_3_ = bf16[1536,384]{1,0:T(8,128)(2,1)S(1)} collective-permute-done((bf16[1536,384]{1,0:T(8,128)(2,1)S(1)}, bf16[1536,384]{1,0:T(8,128)(2,1)S(1)}, u32[]{:S(2)}, u32[]{:S(2)}) %collective-permute-start.24) | collective-permute-done | bytes 1179680 | tf_op jit(solution)/shard_map/ppermute | solution.py:602
  250.2 9.6 %project.5.values = bf16[640,384]{1,0:T(8,128)(2,1)} custom-call(s32[4]{0:T(128)} %pad_add_fusion.4.order, bf16[640,6144]{1,0:T(8,128)(2,1)} %norm.1.normed, bf16[1536,1152]{1,0:T(8,128)(2,1)} %get-tuple-element.163.refs_0_, bf16[1536,1152]{1,0:T(8,128)(2,1)} %copy-done.1, bf16[1536,384]{1,0:T(8,128)(2,1)} %copy-done.7, bf16[1536,384]{1,0:T(8,128)(2,1)} %copy-done.8, ...), custom_call_target="tpu_custom_call" | custom-call | flops 1000 | bytes 1000 | tf_op jit(solution)/shard_map/project/pallas_call | solution.py:261
  259.8 3.6 merge.2.refs_0_
  263.4 1.5 collective-permute-start.26
  265.8 7.6 %suffix.3 = (f32[640,384]{1,0:T(8,128)}, f32[640,128]{1,0:T(8,128)}) custom-call(s32[640,1]{1,0:T(8,128)} %copy.26.row_start, bf16[640,384]{1,0:T(8,128)(2,1)} %get-tuple-element.183.refs_0_.queries, bf16[640,384]{1,0:T(8,128)(2,1)} %get-tuple-element.171.keys, bf16[640,384]{1,0:T(8,128)(2,1)} %project.5.values), custom_call_target="tpu_custom_call" | custom-call | flops 1000 | bytes 1000 | tf_op jit(solution)/shard_map/suffix/pallas_call | solution.py:461
  273.4 3.7 collective-permute-done.26.refs_2_
  277.1 3.8 merge.3.refs_1_
  280.9 1.5 collective-permute-start.27
  282.4 11.4 %collective-permute-done.27.refs_3_ = bf16[640,384]{1,0:T(8,128)(2,1)S(1)} collective-permute-done((bf16[640,384]{1,0:T(8,128)(2,1)}, bf16[640,384]{1,0:T(8,128)(2,1)S(1)}, u32[]{:S(2)}, u32[]{:S(2)}) %collective-permute-start.27) | collective-permute-done | bytes 491552 | tf_op jit(solution)/shard_map/ppermute | solution.py:612
  294.6 12.0 %output.1 = f32[4,640,768]{2,1,0:T(8,128)} custom-call(s32[2]{0:T(128)} %pad_add_fusion.5.place, bf16[640,384]{1,0:T(8,128)(2,1)} %merge.2.refs_0_, bf16[640,384]{1,0:T(8,128)(2,1)} %merge.3.refs_1_, bf16[640,384]{1,0:T(8,128)(2,1)} %copy-done.15, bf16[640,384]{1,0:T(8,128)(2,1)} %copy-done.16, bf16[768,6144]{1,0:T(8,128)(2,1)} %refs_4_.5, ...), custom_call_target="tpu_custom_call" | custom-call | flops 1000 | bytes 1000 | tf_op jit(solution)/shard_map/output/pallas_call | solution.py:554
  306.6 2.3 fusion.13
  308.9 1.3 collective-permute-start.30
  310.2 1.5 collective-permute-start.31
  311.7 1.3 collective-permute-start.36
  313.7 11.2 %collective-permute-done.30 = bf16[320,768]{1,0:T(8,128)(2,1)S(1)} collective-permute-done((bf16[320,768]{1,0:T(8,128)(2,1)S(1)}, bf16[320,768]{1,0:T(8,128)(2,1)S(1)}, u32[]{:S(2)}, u32[]{:S(2)}) %collective-permute-start.30) | collective-permute-done | bytes 491552 | tf_op jit(solution)/shard_map/ppermute | solution.py:829
  324.9 2.6 fusion.8
  327.5 5.3 %collective-permute-start.32 = (bf16[320,768]{1,0:T(8,128)(2,1)}, bf16[320,768]{1,0:T(8,128)(2,1)S(1)}, u32[]{:S(2)}, u32[]{:S(2)}) collective-permute-start(bf16[320,768]{1,0:T(8,128)(2,1)} %get-tuple-element.203), channel_id=1, source_target_pairs={{0,2},{1,3},{2,4},{3,5},{8,10},{9,11},{10,12},{11,13},{16,18},{17,... | collective-permute-start | bytes 1474568 | tf_op jit(solution)/shard_map/ppermute | solution.py:829
  332.8 1.3 collective-permute-start.33
  334.1 1.3 collective-permute-done.36
  335.4 9.7 %collective-permute-done.32 = bf16[320,768]{1,0:T(8,128)(2,1)S(1)} collective-permute-done((bf16[320,768]{1,0:T(8,128)(2,1)}, bf16[320,768]{1,0:T(8,128)(2,1)S(1)}, u32[]{:S(2)}, u32[]{:S(2)}) %collective-permute-start.32) | collective-permute-done | bytes 491552 | tf_op jit(solution)/shard_map/ppermute | solution.py:829
  346.0 2.7 fusion.7
  348.7 4.5 %collective-permute-start.38 = (bf16[320,768]{1,0:T(8,128)(2,1)S(1)}, bf16[320,768]{1,0:T(8,128)(2,1)S(1)}, u32[]{:S(2)}, u32[]{:S(2)}) collective-permute-start(bf16[320,768]{1,0:T(8,128)(2,1)S(1)} %get-tuple-element.217), channel_id=1, source_target_pairs={{0,2},{1,3},{2,4},{3,5},{8,10},{9,11},{10,12},{11,13},{16,18},{17,... | collective-permute-start | bytes 1474568 | tf_op jit(solution)/shard_map/ppermute | solution.py:829
  353.2 1.3 collective-permute-start.39
  354.5 4.6 %collective-permute-start.34 = (bf16[320,768]{1,0:T(8,128)(2,1)S(1)}, bf16[320,768]{1,0:T(8,128)(2,1)S(1)}, u32[]{:S(2)}, u32[]{:S(2)}) collective-permute-start(bf16[320,768]{1,0:T(8,128)(2,1)S(1)} %get-tuple-element.207), channel_id=1, source_target_pairs={{0,2},{1,3},{2,4},{3,5},{4,6},{5,7},{8,10},{9,11},{10,12},{11,13},... | collective-permute-start | bytes 1474568 | tf_op jit(solution)/shard_map/ppermute | solution.py:829
  359.0 1.9 collective-permute-start.35
  360.9 3.9 collective-permute-done.38
  364.8 4.4 %collective-permute-done.39 = bf16[320,768]{1,0:T(8,128)(2,1)S(1)} collective-permute-done((bf16[320,768]{1,0:T(8,128)(2,1)S(1)}, bf16[320,768]{1,0:T(8,128)(2,1)S(1)}, u32[]{:S(2)}, u32[]{:S(2)}) %collective-permute-start.39) | collective-permute-done | bytes 491552 | tf_op jit(solution)/shard_map/ppermute | solution.py:829
  369.2 1.8 fusion.2
  371.0 1.9 collective-permute-start.40
  372.9 4.7 %collective-permute-start.41 = (bf16[320,768]{1,0:T(8,128)(2,1)S(1)}, bf16[320,768]{1,0:T(8,128)(2,1)}, u32[]{:S(2)}, u32[]{:S(2)}) collective-permute-start(bf16[320,768]{1,0:T(8,128)(2,1)S(1)} %get-tuple-element.224), channel_id=1, source_target_pairs={{2,0},{3,1},{4,2},{5,3},{6,4},{7,5},{10,8},{11,9},{12,10},{13,11},... | collective-permute-start | bytes 1474568 | tf_op jit(solution)/shard_map/ppermute | solution.py:829
  377.8 2.1 collective-permute-done.35
  379.8 4.2 %collective-permute-done.40 = bf16[320,768]{1,0:T(8,128)(2,1)} collective-permute-done((bf16[320,768]{1,0:T(8,128)(2,1)S(1)}, bf16[320,768]{1,0:T(8,128)(2,1)}, u32[]{:S(2)}, u32[]{:S(2)}) %collective-permute-start.40) | collective-permute-done | bytes 491552 | tf_op jit(solution)/shard_map/ppermute | solution.py:829
  384.1 4.2 %collective-permute-done.41 = bf16[320,768]{1,0:T(8,128)(2,1)} collective-permute-done((bf16[320,768]{1,0:T(8,128)(2,1)S(1)}, bf16[320,768]{1,0:T(8,128)(2,1)}, u32[]{:S(2)}, u32[]{:S(2)}) %collective-permute-start.41) | collective-permute-done | bytes 491552 | tf_op jit(solution)/shard_map/ppermute | solution.py:829
  388.3 2.4 fusion.1
  (128 shorter events, 24.4 us)
Async XLA Ops:
  0.0 32.7 %collective-permute-start.2 = (bf16[640,768]{1,0:T(8,128)(2,1)}, bf16[640,768]{1,0:T(8,128)(2,1)S(1)}, u32[]{:S(2)}, u32[]{:S(2)}) collective-permute-start(bf16[640,768]{1,0:T(8,128)(2,1)} %refs_0_), channel_id=1, source_target_pairs={{0,2},{1,3},{2,4},{3,5},{4,6},{5,7},{8,10},{9,11},{10,12},{11,13},... | collective-permute-start | bytes 2949128 | tf_op jit(solution)/shard_map/ppermute | solution.py:645
  3.5 29.2 %collective-permute-start.3 = (bf16[640,768]{1,0:T(8,128)(2,1)}, bf16[640,768]{1,0:T(8,128)(2,1)}, u32[]{:S(2)}, u32[]{:S(2)}) collective-permute-start(bf16[640,768]{1,0:T(8,128)(2,1)} %refs_0_), channel_id=1, source_target_pairs={{2,0},{3,1},{4,2},{5,3},{6,4},{7,5},{10,8},{11,9},{12,10},{13,11},... | collective-permute-start | bytes 2949128 | tf_op jit(solution)/shard_map/ppermute | solution.py:648
  5.9 26.8 %collective-permute-start.4 = (bf16[640,768]{1,0:T(8,128)(2,1)}, bf16[640,768]{1,0:T(8,128)(2,1)}, u32[]{:S(2)}, u32[]{:S(2)}) collective-permute-start(bf16[640,768]{1,0:T(8,128)(2,1)} %refs_0_), channel_id=1, source_target_pairs={{0,1},{1,0},{2,3},{3,2},{4,5},{5,4},{6,7},{7,6},{8,9},{9,8},{10,11... | collective-permute-start | bytes 2949128 | tf_op jit(solution)/shard_map/ppermute | solution.py:612
  7.2 14.0 %collective-permute-start = (s32[2,8]{1,0:T(2,128)S(1)}, s32[2,8]{1,0:T(2,128)S(1)}, u32[]{:S(2)}, u32[]{:S(2)}) collective-permute-start(s32[2,8]{1,0:T(2,128)S(1)} %pad_add_fusion.1), channel_id=1, source_target_pairs={{0,16},{8,24},{16,0},{24,8},{1,17},{9,25},{17,1},{25,9},{2,18},{10... | collective-permute-start | bytes 200 | tf_op jit(solution)/shard_map/ppermute | solution.py:605
  21.2 87.1 %collective-permute-start.1 = (bf16[1536,1152]{1,0:T(8,128)(2,1)}, bf16[1536,1152]{1,0:T(8,128)(2,1)}, u32[]{:S(2)}, u32[]{:S(2)}) collective-permute-start(bf16[1536,1152]{1,0:T(8,128)(2,1)} %parts.2.refs_0_), channel_id=1, source_target_pairs={{0,16},{8,24},{16,0},{24,8},{1,17},{9,25},{17,1},{25,9},{2,18},{10... | collective-permute-start | bytes 10616840 | tf_op jit(solution)/shard_map/ppermute | solution.py:605
  22.7 19.9 %copy-start.17 = (bf16[2304]{0:T(1024)(128)(2,1)S(1)}, bf16[2304]{0:T(1024)(128)(2,1)}, u32[]{:S(2)}) copy-start(bf16[2304]{0:T(1024)(128)(2,1)} %param.16) | copy-start | bytes 13828
  32.7 0.9 copy-start.9
  33.6 23.3 %collective-permute-start.5 = (bf16[640,768]{1,0:T(8,128)(2,1)}, bf16[640,768]{1,0:T(8,128)(2,1)S(1)}, u32[]{:S(2)}, u32[]{:S(2)}) collective-permute-start(bf16[640,768]{1,0:T(8,128)(2,1)} %copy-done.9), channel_id=1, source_target_pairs={{2,4},{3,5},{4,6},{5,7},{10,12},{11,13},{12,14},{13,15},{18,20},{1... | collective-permute-start | bytes 2949128 | tf_op jit(solution)/shard_map/ppermute | solution.py:645
  37.1 24.1 %collective-permute-start.6 = (bf16[640,768]{1,0:T(8,128)(2,1)}, bf16[640,768]{1,0:T(8,128)(2,1)}, u32[]{:S(2)}, u32[]{:S(2)}) collective-permute-start(bf16[640,768]{1,0:T(8,128)(2,1)} %collective-permute-done.3.refs_3_), channel_id=1, source_target_pairs={{2,0},{3,1},{4,2},{5,3},{10,8},{11,9},{12,10},{13,11},{18,16},{19,... | collective-permute-start | bytes 2949128 | tf_op jit(solution)/shard_map/ppermute | solution.py:648
  39.0 26.9 %collective-permute-start.7 = (bf16[640,768]{1,0:T(8,128)(2,1)}, bf16[640,768]{1,0:T(8,128)(2,1)}, u32[]{:S(2)}, u32[]{:S(2)}) collective-permute-start(bf16[640,768]{1,0:T(8,128)(2,1)} %copy-done.9), channel_id=1, source_target_pairs={{2,3},{3,2},{4,5},{5,4},{6,7},{7,6},{10,11},{11,10},{12,13},{13,12... | collective-permute-start | bytes 2949128 | tf_op jit(solution)/shard_map/ppermute | solution.py:625
  42.7 41.4 %collective-permute-start.8 = (bf16[640,768]{1,0:T(8,128)(2,1)}, bf16[640,768]{1,0:T(8,128)(2,1)}, u32[]{:S(2)}, u32[]{:S(2)}) collective-permute-start(bf16[640,768]{1,0:T(8,128)(2,1)} %collective-permute-done.3.refs_3_), channel_id=1, source_target_pairs={{0,1},{1,0},{2,3},{3,2},{4,5},{5,4},{8,9},{9,8},{10,11},{11,10},{1... | collective-permute-start | bytes 2949128 | tf_op jit(solution)/shard_map/ppermute | solution.py:625
  52.0 54.2 %copy-start.19 = (s32[8]{0:T(128)S(1)}, s32[8]{0:T(128)}, u32[]{:S(2)}) copy-start(s32[8]{0:T(128)} %param.23) | copy-start | bytes 100
  56.9 33.4 %copy-start.3 = (bf16[640,768]{1,0:T(8,128)(2,1)}, bf16[640,768]{1,0:T(8,128)(2,1)S(1)}, u32[]{:S(2)}) copy-start(bf16[640,768]{1,0:T(8,128)(2,1)S(1)} %collective-permute-done.5.refs_6_) | copy-start | bytes 2949124
  65.9 23.2 %collective-permute-start.10 = (bf16[640,768]{1,0:T(8,128)(2,1)S(1)}, bf16[640,768]{1,0:T(8,128)(2,1)S(1)}, u32[]{:S(2)}, u32[]{:S(2)}) collective-permute-start(bf16[640,768]{1,0:T(8,128)(2,1)S(1)} %collective-permute-done.5.refs_6_), channel_id=1, source_target_pairs={{4,6},{5,7},{12,14},{13,15},{20,22},{21,23},{28,30},{29,31}} | collective-permute-start | bytes 2949128 | tf_op jit(solution)/shard_map/ppermute | solution.py:645
  66.6 22.5 %collective-permute-start.11 = (bf16[640,768]{1,0:T(8,128)(2,1)}, bf16[640,768]{1,0:T(8,128)(2,1)S(1)}, u32[]{:S(2)}, u32[]{:S(2)}) collective-permute-start(bf16[640,768]{1,0:T(8,128)(2,1)} %collective-permute-done.6.refs_7_), channel_id=1, source_target_pairs={{2,0},{3,1},{10,8},{11,9},{18,16},{19,17},{26,24},{27,25}} | collective-permute-start | bytes 2949128 | tf_op jit(solution)/shard_map/ppermute | solution.py:648
  84.1 21.2 %collective-permute-start.9 = (bf16[640,768]{1,0:T(8,128)(2,1)}, bf16[640,768]{1,0:T(8,128)(2,1)}, u32[]{:S(2)}, u32[]{:S(2)}) collective-permute-start(bf16[640,768]{1,0:T(8,128)(2,1)} %broadcast_select_fusion.1), channel_id=1, source_target_pairs={{0,1},{1,0},{2,3},{3,2},{4,5},{5,4},{6,7},{7,6},{8,9},{9,8},{10,11... | collective-permute-start | bytes 2949128 | tf_op jit(solution)/shard_map/ppermute | solution.py:668
  89.1 34.8 %collective-permute-start.13 = (bf16[1536,1152]{1,0:T(8,128)(2,1)}, bf16[1536,1152]{1,0:T(8,128)(2,1)}, u32[]{:S(2)}, u32[]{:S(2)}) collective-permute-start(bf16[1536,1152]{1,0:T(8,128)(2,1)} %parts.2.refs_0_), channel_id=1, source_target_pairs={{0,8},{8,0},{16,24},{24,16},{1,9},{9,1},{17,25},{25,17},{2,10},{10... | collective-permute-start | bytes 10616840 | tf_op jit(solution)/shard_map/ppermute | solution.py:602
  89.2 20.3 %copy-start.4 = (bf16[640,768]{1,0:T(8,128)(2,1)}, bf16[640,768]{1,0:T(8,128)(2,1)S(1)}, u32[]{:S(2)}) copy-start(bf16[640,768]{1,0:T(8,128)(2,1)S(1)} %collective-permute-done.10.refs_9_) | copy-start | bytes 2949124
  89.2 20.3 %copy-start.5 = (bf16[640,768]{1,0:T(8,128)(2,1)}, bf16[640,768]{1,0:T(8,128)(2,1)S(1)}, u32[]{:S(2)}) copy-start(bf16[640,768]{1,0:T(8,128)(2,1)S(1)} %collective-permute-done.11.refs_10_) | copy-start | bytes 2949124
  105.3 3.0 collective-permute-start.12
  108.3 1.2 copy-start.10
  108.3 15.8 %collective-permute-start.14 = (bf16[1536,1152]{1,0:T(8,128)(2,1)}, bf16[1536,1152]{1,0:T(8,128)(2,1)}, u32[]{:S(2)}, u32[]{:S(2)}) collective-permute-start(bf16[1536,1152]{1,0:T(8,128)(2,1)} %collective-permute-done.1.refs_2_), channel_id=1, source_target_pairs={{0,8},{8,0},{16,24},{24,16},{1,9},{9,1},{17,25},{25,17},{2,10},{10... | collective-permute-start | bytes 10616840 | tf_op jit(solution)/shard_map/ppermute | solution.py:602
  108.4 87.6 %collective-permute-start.19 = (bf16[2,2048,768]{2,1,0:T(8,128)(2,1)}, bf16[2,2048,768]{2,1,0:T(8,128)(2,1)}, u32[]{:S(2)}, u32[]{:S(2)}) collective-permute-start(bf16[2,2048,768]{2,1,0:T(8,128)(2,1)} %refs_2_.3), channel_id=1, source_target_pairs={{0,8},{8,0},{16,24},{24,16},{1,9},{9,1},{17,25},{25,17},{2,10},{10... | collective-permute-start | bytes 18874376 | tf_op jit(solution)/shard_map/ppermute | solution.py:602
  108.9 87.1 %collective-permute-start.20 = (bf16[2,2048,768]{2,1,0:T(8,128)(2,1)}, bf16[2,2048,768]{2,1,0:T(8,128)(2,1)}, u32[]{:S(2)}, u32[]{:S(2)}) collective-permute-start(bf16[2,2048,768]{2,1,0:T(8,128)(2,1)} %refs_4_.4), channel_id=1, source_target_pairs={{0,8},{8,0},{16,24},{24,16},{1,9},{9,1},{17,25},{25,17},{2,10},{10... | collective-permute-start | bytes 18874376 | tf_op jit(solution)/shard_map/ppermute | solution.py:602
  109.0 53.9 %collective-permute-start.17 = (bf16[1536,768]{1,0:T(8,128)(2,1)}, bf16[1536,768]{1,0:T(8,128)(2,1)}, u32[]{:S(2)}, u32[]{:S(2)}) collective-permute-start(bf16[1536,768]{1,0:T(8,128)(2,1)} %get-tuple-element.165), channel_id=1, source_target_pairs={{0,16},{8,24},{16,0},{24,8},{1,17},{9,25},{17,1},{25,9},{2,18},{10... | collective-permute-start | bytes 7077896 | tf_op jit(solution)/shard_map/ppermute | solution.py:605
  109.5 14.4 %copy-start = (bf16[1536,1152]{1,0:T(8,128)(2,1)S(1)}, bf16[1536,1152]{1,0:T(8,128)(2,1)}, u32[]{:S(2)}) copy-start(bf16[1536,1152]{1,0:T(8,128)(2,1)} %get-tuple-element.163.refs_0_) | copy-start | bytes 10616836
  123.9 40.5 %collective-permute-start.16 = (bf16[1536,1152]{1,0:T(8,128)(2,1)S(1)}, bf16[1536,1152]{1,0:T(8,128)(2,1)S(1)}, u32[]{:S(2)}, u32[]{:S(2)}) collective-permute-start(bf16[1536,1152]{1,0:T(8,128)(2,1)S(1)} %copy-done), channel_id=1, source_target_pairs={{0,8},{8,0},{16,24},{24,16},{1,9},{9,1},{17,25},{25,17},{2,10},{10... | collective-permute-start | bytes 10616840 | tf_op jit(solution)/shard_map/ppermute | solution.py:602
  162.9 4.9 %collective-permute-start.18 = (bf16[1536,768]{1,0:T(8,128)(2,1)}, bf16[1536,768]{1,0:T(8,128)(2,1)}, u32[]{:S(2)}, u32[]{:S(2)}) collective-permute-start(bf16[1536,768]{1,0:T(8,128)(2,1)} %collective-permute-done.17.refs_2_), channel_id=1, source_target_pairs={{0,8},{8,0},{16,24},{24,16},{1,9},{9,1},{17,25},{25,17},{2,10},{10... | collective-permute-start | bytes 7077896 | tf_op jit(solution)/shard_map/ppermute | solution.py:602
  162.9 80.3 %collective-permute-start.28 = (bf16[768,1536]{1,0:T(8,128)(2,1)}, bf16[768,1536]{1,0:T(8,128)(2,1)}, u32[]{:S(2)}, u32[]{:S(2)}) collective-permute-start(bf16[768,1536]{1,0:T(8,128)(2,1)} %pad_maximum_fusion), channel_id=1, source_target_pairs={{0,1},{1,0},{2,3},{3,2},{4,5},{5,4},{6,7},{7,6},{8,9},{9,8},{10,11... | collective-permute-start | bytes 7077896 | tf_op jit(solution)/shard_map/ppermute | solution.py:612
  164.4 3.4 copy-start.1
  164.4 26.7 %collective-permute-start.15 = (bf16[640,384]{1,0:T(8,128)(2,1)}, bf16[640,384]{1,0:T(8,128)(2,1)S(1)}, u32[]{:S(2)}, u32[]{:S(2)}) collective-permute-start(bf16[640,384]{1,0:T(8,128)(2,1)} %get-tuple-element.175.queries.refs_0_), channel_id=1, source_target_pairs={{0,16},{8,24},{16,0},{24,8},{1,17},{9,25},{17,1},{25,9},{2,18},{10... | collective-permute-start | bytes 1474568 | tf_op jit(solution)/shard_map/ppermute | solution.py:605
  181.9 13.5 %collective-permute-start.22 = (bf16[640,384]{1,0:T(8,128)(2,1)}, bf16[640,384]{1,0:T(8,128)(2,1)S(1)}, u32[]{:S(2)}, u32[]{:S(2)}) collective-permute-start(bf16[640,384]{1,0:T(8,128)(2,1)} %get-tuple-element.183.refs_0_.queries), channel_id=1, source_target_pairs={{0,16},{8,24},{16,0},{24,8},{1,17},{9,25},{17,1},{25,9},{2,18},{10... | collective-permute-start | bytes 1474568 | tf_op jit(solution)/shard_map/ppermute | solution.py:605
  191.0 4.9 %copy-start.13 = (bf16[640,384]{1,0:T(8,128)(2,1)}, bf16[640,384]{1,0:T(8,128)(2,1)S(1)}, u32[]{:S(2)}) copy-start(bf16[640,384]{1,0:T(8,128)(2,1)S(1)} %collective-permute-done.15.refs_1_) | copy-start | bytes 1474564
  195.5 24.1 %copy-start.14 = (bf16[640,384]{1,0:T(8,128)(2,1)}, bf16[640,384]{1,0:T(8,128)(2,1)S(1)}, u32[]{:S(2)}) copy-start(bf16[640,384]{1,0:T(8,128)(2,1)S(1)} %collective-permute-done.22.refs_1_) | copy-start | bytes 1474564
  195.5 47.8 %collective-permute-start.23 = (bf16[1536,384]{1,0:T(8,128)(2,1)}, bf16[1536,384]{1,0:T(8,128)(2,1)S(1)}, u32[]{:S(2)}, u32[]{:S(2)}) collective-permute-start(bf16[1536,384]{1,0:T(8,128)(2,1)} %get-tuple-element.182), channel_id=1, source_target_pairs={{0,16},{8,24},{16,0},{24,8},{1,17},{9,25},{17,1},{25,9},{2,18},{10... | collective-permute-start | bytes 3538952 | tf_op jit(solution)/shard_map/ppermute | solution.py:605
  219.5 23.7 %collective-permute-start.21 = (bf16[640,512]{1,0:T(8,128)(2,1)}, bf16[640,512]{1,0:T(8,128)(2,1)S(1)}, u32[]{:S(2)}, u32[]{:S(2)}) collective-permute-start(bf16[640,512]{1,0:T(8,128)(2,1)} %get-tuple-element.180), channel_id=1, source_target_pairs={{0,16},{8,24},{16,0},{24,8},{1,17},{9,25},{17,1},{25,9},{2,18},{10... | collective-permute-start | bytes 1966088 | tf_op jit(solution)/shard_map/ppermute | solution.py:605
  243.2 39.2 %collective-permute-start.29 = (bf16[768,1536]{1,0:T(8,128)(2,1)}, bf16[768,1536]{1,0:T(8,128)(2,1)S(1)}, u32[]{:S(2)}, u32[]{:S(2)}) collective-permute-start(bf16[768,1536]{1,0:T(8,128)(2,1)} %collective-permute-done.28.refs_5_), channel_id=1, source_target_pairs={{0,8},{8,0},{16,24},{24,16},{1,9},{9,1},{17,25},{25,17},{2,10},{10... | collective-permute-start | bytes 7077896 | tf_op jit(solution)/shard_map/ppermute | solution.py:602
  243.3 16.5 %copy-start.11 = (bf16[640,512]{1,0:T(8,128)(2,1)}, bf16[640,512]{1,0:T(8,128)(2,1)S(1)}, u32[]{:S(2)}) copy-start(bf16[640,512]{1,0:T(8,128)(2,1)S(1)} %collective-permute-done.21.refs_1_) | copy-start | bytes 1966084
  243.3 5.8 %copy-start.7 = (bf16[1536,384]{1,0:T(8,128)(2,1)}, bf16[1536,384]{1,0:T(8,128)(2,1)S(1)}, u32[]{:S(2)}) copy-start(bf16[1536,384]{1,0:T(8,128)(2,1)S(1)} %collective-permute-done.23.refs_2_) | copy-start | bytes 3538948
  243.3 5.8 %collective-permute-start.24 = (bf16[1536,384]{1,0:T(8,128)(2,1)S(1)}, bf16[1536,384]{1,0:T(8,128)(2,1)S(1)}, u32[]{:S(2)}, u32[]{:S(2)}) collective-permute-start(bf16[1536,384]{1,0:T(8,128)(2,1)S(1)} %collective-permute-done.23.refs_2_), channel_id=1, source_target_pairs={{0,8},{8,0},{16,24},{24,16},{1,9},{9,1},{17,25},{25,17},{2,10},{10... | collective-permute-start | bytes 3538952 | tf_op jit(solution)/shard_map/ppermute | solution.py:602
  243.9 29.6 %collective-permute-start.25 = (bf16[640,512]{1,0:T(8,128)(2,1)}, bf16[640,512]{1,0:T(8,128)(2,1)S(1)}, u32[]{:S(2)}, u32[]{:S(2)}) collective-permute-start(bf16[640,512]{1,0:T(8,128)(2,1)} %get-tuple-element.186), channel_id=1, source_target_pairs={{0,16},{8,24},{16,0},{24,8},{1,17},{9,25},{17,1},{25,9},{2,18},{10... | collective-permute-start | bytes 1966088 | tf_op jit(solution)/shard_map/ppermute | solution.py:605
  249.1 1.1 copy-start.8
  263.4 13.7 %collective-permute-start.26 = (bf16[640,384]{1,0:T(8,128)(2,1)}, bf16[640,384]{1,0:T(8,128)(2,1)S(1)}, u32[]{:S(2)}, u32[]{:S(2)}) collective-permute-start(bf16[640,384]{1,0:T(8,128)(2,1)} %merge.2.refs_0_), channel_id=1, source_target_pairs={{0,1},{1,0},{2,3},{3,2},{4,5},{5,4},{6,7},{7,6},{8,9},{9,8},{10,11... | collective-permute-start | bytes 1474568 | tf_op jit(solution)/shard_map/ppermute | solution.py:612
  273.4 3.7 copy-start.12
  277.1 16.7 %copy-start.15 = (bf16[640,384]{1,0:T(8,128)(2,1)}, bf16[640,384]{1,0:T(8,128)(2,1)S(1)}, u32[]{:S(2)}) copy-start(bf16[640,384]{1,0:T(8,128)(2,1)S(1)} %collective-permute-done.26.refs_2_) | copy-start | bytes 1474564
  280.9 12.9 %collective-permute-start.27 = (bf16[640,384]{1,0:T(8,128)(2,1)}, bf16[640,384]{1,0:T(8,128)(2,1)S(1)}, u32[]{:S(2)}, u32[]{:S(2)}) collective-permute-start(bf16[640,384]{1,0:T(8,128)(2,1)} %merge.3.refs_1_), channel_id=1, source_target_pairs={{0,1},{1,0},{2,3},{3,2},{4,5},{5,4},{6,7},{7,6},{8,9},{9,8},{10,11... | collective-permute-start | bytes 1474568 | tf_op jit(solution)/shard_map/ppermute | solution.py:612
  282.4 11.4 %copy-start.6 = (bf16[768,1536]{1,0:T(8,128)(2,1)}, bf16[768,1536]{1,0:T(8,128)(2,1)S(1)}, u32[]{:S(2)}) copy-start(bf16[768,1536]{1,0:T(8,128)(2,1)S(1)} %collective-permute-done.29.refs_6_) | copy-start | bytes 7077892
  293.8 0.8 copy-start.16
  308.9 16.0 %collective-permute-start.30 = (bf16[320,768]{1,0:T(8,128)(2,1)S(1)}, bf16[320,768]{1,0:T(8,128)(2,1)S(1)}, u32[]{:S(2)}, u32[]{:S(2)}) collective-permute-start(bf16[320,768]{1,0:T(8,128)(2,1)S(1)} %get-tuple-element.199), channel_id=1, source_target_pairs={{0,2},{1,3},{8,10},{9,11},{16,18},{17,19},{24,26},{25,27}} | collective-permute-start | bytes 1474568 | tf_op jit(solution)/shard_map/ppermute | solution.py:829
  310.2 14.7 %collective-permute-start.31 = (bf16[320,768]{1,0:T(8,128)(2,1)S(1)}, bf16[320,768]{1,0:T(8,128)(2,1)}, u32[]{:S(2)}, u32[]{:S(2)}) collective-permute-start(bf16[320,768]{1,0:T(8,128)(2,1)S(1)} %get-tuple-element.200), channel_id=1, source_target_pairs={{6,4},{7,5},{14,12},{15,13},{22,20},{23,21},{30,28},{31,29}} | collective-permute-start | bytes 1474568 | tf_op jit(solution)/shard_map/ppermute | solution.py:829
  311.7 23.7 %collective-permute-start.36 = (bf16[320,768]{1,0:T(8,128)(2,1)S(1)}, bf16[320,768]{1,0:T(8,128)(2,1)S(1)}, u32[]{:S(2)}, u32[]{:S(2)}) collective-permute-start(bf16[320,768]{1,0:T(8,128)(2,1)S(1)} %get-tuple-element.211), channel_id=1, source_target_pairs={{0,2},{1,3},{8,10},{9,11},{16,18},{17,19},{24,26},{25,27}} | collective-permute-start | bytes 1474568 | tf_op jit(solution)/shard_map/ppermute | solution.py:829
  313.0 22.4 %collective-permute-start.37 = (bf16[320,768]{1,0:T(8,128)(2,1)S(1)}, bf16[320,768]{1,0:T(8,128)(2,1)S(1)}, u32[]{:S(2)}, u32[]{:S(2)}) collective-permute-start(bf16[320,768]{1,0:T(8,128)(2,1)S(1)} %get-tuple-element.212), channel_id=1, source_target_pairs={{6,4},{7,5},{14,12},{15,13},{22,20},{23,21},{30,28},{31,29}} | collective-permute-start | bytes 1474568 | tf_op jit(solution)/shard_map/ppermute | solution.py:829
  327.5 17.6 %collective-permute-start.32 = (bf16[320,768]{1,0:T(8,128)(2,1)}, bf16[320,768]{1,0:T(8,128)(2,1)S(1)}, u32[]{:S(2)}, u32[]{:S(2)}) collective-permute-start(bf16[320,768]{1,0:T(8,128)(2,1)} %get-tuple-element.203), channel_id=1, source_target_pairs={{0,2},{1,3},{2,4},{3,5},{8,10},{9,11},{10,12},{11,13},{16,18},{17,... | collective-permute-start | bytes 1474568 | tf_op jit(solution)/shard_map/ppermute | solution.py:829
  332.8 13.2 %collective-permute-start.33 = (bf16[320,768]{1,0:T(8,128)(2,1)S(1)}, bf16[320,768]{1,0:T(8,128)(2,1)}, u32[]{:S(2)}, u32[]{:S(2)}) collective-permute-start(bf16[320,768]{1,0:T(8,128)(2,1)S(1)} %get-tuple-element.204), channel_id=1, source_target_pairs={{4,2},{5,3},{6,4},{7,5},{12,10},{13,11},{14,12},{15,13},{20,18},{2... | collective-permute-start | bytes 1474568 | tf_op jit(solution)/shard_map/ppermute | solution.py:829
  348.6 29.0 %copy-start.18 = (bf16[768]{0:T(1024)(128)(2,1)S(1)}, bf16[768]{0:T(1024)(128)(2,1)}, u32[]{:S(2)}) copy-start(bf16[768]{0:T(1024)(128)(2,1)} %param.18) | copy-start | bytes 4612
  348.6 29.0 %copy-start.2 = (bf16[640,768]{1,0:T(8,128)(2,1)S(1)}, bf16[640,768]{1,0:T(8,128)(2,1)}, u32[]{:S(2)}) copy-start(bf16[640,768]{1,0:T(8,128)(2,1)} %refs_0_) | copy-start | bytes 2949124
  348.7 16.2 %collective-permute-start.38 = (bf16[320,768]{1,0:T(8,128)(2,1)S(1)}, bf16[320,768]{1,0:T(8,128)(2,1)S(1)}, u32[]{:S(2)}, u32[]{:S(2)}) collective-permute-start(bf16[320,768]{1,0:T(8,128)(2,1)S(1)} %get-tuple-element.217), channel_id=1, source_target_pairs={{0,2},{1,3},{2,4},{3,5},{8,10},{9,11},{10,12},{11,13},{16,18},{17,... | collective-permute-start | bytes 1474568 | tf_op jit(solution)/shard_map/ppermute | solution.py:829
  353.2 16.1 %collective-permute-start.39 = (bf16[320,768]{1,0:T(8,128)(2,1)S(1)}, bf16[320,768]{1,0:T(8,128)(2,1)S(1)}, u32[]{:S(2)}, u32[]{:S(2)}) collective-permute-start(bf16[320,768]{1,0:T(8,128)(2,1)S(1)} %get-tuple-element.218), channel_id=1, source_target_pairs={{4,2},{5,3},{6,4},{7,5},{12,10},{13,11},{14,12},{15,13},{20,18},{2... | collective-permute-start | bytes 1474568 | tf_op jit(solution)/shard_map/ppermute | solution.py:829
  354.5 23.3 %collective-permute-start.34 = (bf16[320,768]{1,0:T(8,128)(2,1)S(1)}, bf16[320,768]{1,0:T(8,128)(2,1)S(1)}, u32[]{:S(2)}, u32[]{:S(2)}) collective-permute-start(bf16[320,768]{1,0:T(8,128)(2,1)S(1)} %get-tuple-element.207), channel_id=1, source_target_pairs={{0,2},{1,3},{2,4},{3,5},{4,6},{5,7},{8,10},{9,11},{10,12},{11,13},... | collective-permute-start | bytes 1474568 | tf_op jit(solution)/shard_map/ppermute | solution.py:829
  359.0 20.8 %collective-permute-start.35 = (bf16[320,768]{1,0:T(8,128)(2,1)S(1)}, bf16[320,768]{1,0:T(8,128)(2,1)}, u32[]{:S(2)}, u32[]{:S(2)}) collective-permute-start(bf16[320,768]{1,0:T(8,128)(2,1)S(1)} %get-tuple-element.208), channel_id=1, source_target_pairs={{2,0},{3,1},{4,2},{5,3},{6,4},{7,5},{10,8},{11,9},{12,10},{13,11},... | collective-permute-start | bytes 1474568 | tf_op jit(solution)/shard_map/ppermute | solution.py:829
  371.0 13.1 %collective-permute-start.40 = (bf16[320,768]{1,0:T(8,128)(2,1)S(1)}, bf16[320,768]{1,0:T(8,128)(2,1)}, u32[]{:S(2)}, u32[]{:S(2)}) collective-permute-start(bf16[320,768]{1,0:T(8,128)(2,1)S(1)} %get-tuple-element.223), channel_id=1, source_target_pairs={{0,2},{1,3},{2,4},{3,5},{4,6},{5,7},{8,10},{9,11},{10,12},{11,13},... | collective-permute-start | bytes 1474568 | tf_op jit(solution)/shard_map/ppermute | solution.py:829
  372.9 15.4 %collective-permute-start.41 = (bf16[320,768]{1,0:T(8,128)(2,1)S(1)}, bf16[320,768]{1,0:T(8,128)(2,1)}, u32[]{:S(2)}, u32[]{:S(2)}) collective-permute-start(bf16[320,768]{1,0:T(8,128)(2,1)S(1)} %get-tuple-element.224), channel_id=1, source_target_pairs={{2,0},{3,1},{4,2},{5,3},{6,4},{7,5},{10,8},{11,9},{12,10},{13,11},... | collective-permute-start | bytes 1474568 | tf_op jit(solution)/shard_map/ppermute | solution.py:829
